TPU v7x, 128 devices: a whole 4x4x4 slice. The times are simulated.
128 devices in a mesh: dp: 2 (over y_hi), row: 16 (over x, z), col: 4 (over y_lo, core).
Axes of the slice: x: 4, y: 4 (y_hi: 2, y_lo: 2; y = y_hi * 2 + y_lo), z: 4, core: 2. Of those that a mesh axis runs over, the one named last changes fastest.
Arguments:
- params: float32 [2048, 36864], P('row', ('col', 'dp')), may hold values from -16 to 16
- grad_parts: bfloat16 [2, 2048, 36864], P('dp', 'row', 'col'), may hold values from -16 to 16
- row_moment: float32 [2048], P('row'), may hold values from 0.01 to 1
- col_moment: float32 [36864], P('col'), may hold values from 0.02 to 2
Outputs:
- new_params: float32 [2048, 36864], P('row', ('col', 'dp'))
- new_weights: bfloat16 [2048, 36864], P('row', 'col')
- new_row_moment: float32 [2048], P('row')
- new_col_moment: float32 [36864], P(('col', 'dp'))
- update: float32 [2048, 36864], P('row', ('col', 'dp'))
- clip_factor: float32 [], replicated
- param_scale: float32 [], replicated
All inputs are finite; a program needn't handle non-finite values.
Results may differ from a plain program's by a relative error of at most 0.013.
Values may be sent and summed in bfloat16 or wider, within the bound.
No kernel may reach another device: no remote copies, remote signals or barrier semaphores. Data moves between devices by JAX's collectives and lax.ppermute only.
A program may use at most 64 MiB of HBM per device.

v0:
```python
import jax
import jax.numpy as jnp
from jax import lax
from jax.sharding import PartitionSpec as P

R = 2048
C = 36864
STEP = 10


def shards(params, grad_parts, row_moment, col_moment):
    decay_rate = 1.0 - STEP ** (-0.8)
    relative = min(0.01, STEP ** (-0.5))
    partial_value = grad_parts[0].astype(jnp.float32)
    position = lax.axis_index("dp")
    width = params.shape[1]
    gradient = lax.psum(partial_value.astype(jnp.bfloat16), "dp").astype(jnp.float32)
    weights_here = lax.all_gather(params.astype(jnp.bfloat16), "dp", axis=1, tiled=True).astype(
        params.dtype
    )
    squares = gradient * gradient + 1e-30
    row_totals = lax.psum(jnp.sum(squares, axis=1), "col")
    col_totals = lax.psum(jnp.sum(squares, axis=0).astype(jnp.bfloat16), "row").astype(jnp.float32)
    new_rows = decay_rate * row_moment + (1.0 - decay_rate) * (row_totals / C)
    new_cols = decay_rate * col_moment + (1.0 - decay_rate) * (col_totals / R)
    weight_local = jnp.sum(params * params)
    row_mean = lax.psum(jnp.sum(new_rows), "row") / R
    update = gradient * lax.rsqrt(new_rows[:, None] * new_cols[None, :] / row_mean)
    update_part = lax.dynamic_slice_in_dim(update, position * width, width, 1)
    update_sum, weight_sum = lax.psum(
        (jnp.sum(update_part * update_part), weight_local), ("dp", "row", "col")
    )
    clip_factor = jnp.maximum(1.0, jnp.sqrt(update_sum / (R * C)))
    param_scale = jnp.maximum(0.001, jnp.sqrt(weight_sum / (R * C)))
    step_size = relative * param_scale
    updated = weights_here - step_size / clip_factor * update
    new_params = lax.dynamic_slice_in_dim(updated, position * width, width, 1)
    new_weights = updated.astype(jnp.bfloat16)
    new_col_part = lax.dynamic_slice_in_dim(new_cols, position * width, width, 0)
    return (new_params, new_weights, new_rows, new_col_part, update_part, clip_factor, param_scale)


def solution(mesh):
    in_specs = (P("row", ("col", "dp")), P("dp", "row", "col"), P("row"), P("col"))
    out_specs = (
        P("row", ("col", "dp")),
        P("row", "col"),
        P("row"),
        P(("col", "dp")),
        P("row", ("col", "dp")),
        P(),
        P(),
    )
    return jax.shard_map(shards, mesh=mesh, in_specs=in_specs, out_specs=out_specs, check_vma=False)
```

profile of v0, /device:TPU:1, one launch (start us, length us, event | category | flops | bytes accessed | tf_op | source)
XLA Modules:
  0.0 295.9 jit_solution(15531764468389127342)
XLA Ops:
  7.2 0.0 all-reduce.3.cloned.1.call-start
  7.2 0.0 copy-start.3
  7.2 0.0 copy-start.1
  7.2 0.7 all-reduce.3.cloned.1.call-update
  7.9 0.0 all-gather.2.cloned.1.call-start
  7.9 4.5 %fusion.5 = (bf16[128,4608]{1,0:T(8,128)(2,1)}, f32[]{:T(128)}) fusion(f32[128,4608]{1,0:T(8,128)} %param.4), kind=kLoop, calls=%fused_computation.14 | loop fusion | flops 1769471 | bytes 3538948 | tf_op jit(solution)/shard_map/convert_element_type | solution.py:18
  12.5 0.0 all-gather.2.cloned.1.call-update
  12.5 77.9 %all-reduce.3.cloned.1.call-done = bf16[128,9216]{1,0:T(8,128)(2,1)} async-done(((bf16[128,9216]{1,0:T(8,128)(2,1)}), bf16[128,9216]{1,0:T(8,128)(2,1)}) %all-reduce.3.cloned.1.call-update) | async-done | bytes 2359312 | tf_op jit(solution)/shard_map/psum | solution.py:17
  90.4 2.5 fusion.1
  92.9 5.7 %psum.44 = f32[128]{0:T(128)S(1)} all-reduce(f32[128]{0:T(128)S(1)} %get-tuple-element.8), channel_id=1, replica_groups=mesh['dp'=2,'row'=16,'col'=4] {'col'}, use_global_device_ids=true, to_apply=%region_4.0 | all-reduce | flops 128 | bytes 1024 | tf_op jit(solution)/shard_map/psum | solution.py:22
  98.6 60.4 %psum.45 = bf16[9216]{0:T(1024)(128)(2,1)S(1)} all-reduce(bf16[9216]{0:T(1024)(128)(2,1)S(1)} %get-tuple-element.7), channel_id=1, replica_groups=mesh['dp'=2,'row'=16,'col'=4] {'row'}, use_global_device_ids=true, to_apply=%region_6.0 | all-reduce | flops 9216 | bytes 36864 | tf_op jit(solution)/shard_map/psum | solution.py:23
  159.1 0.0 copy-done.3
  159.1 0.6 fusion.4
  159.7 0.0 copy-start.2
  159.7 29.1 %psum.46 = f32[]{:T(128)} all-reduce(f32[]{:T(128)} %get-tuple-element.15), channel_id=1, replica_groups=mesh['dp'=2,'row'=16,'col'=4] {'row'}, use_global_device_ids=true, to_apply=%region_8.0 | all-reduce | flops 1 | bytes 8 | tf_op jit(solution)/shard_map/psum | solution.py:27
  188.8 0.0 copy-done.1
  189.5 0.0 copy-start
  189.5 2.7 convert_multiply_fusion
  192.1 2.6 multiply_reduce_fusion
  194.7 84.0 %all-reduce = (f32[]{:T(128)}, f32[]{:T(128)}) all-reduce(f32[]{:T(128)} %get-tuple-element.18, f32[]{:T(128)} %get-tuple-element.13), channel_id=1, replica_groups=mesh['dp'=2,'row'=16,'col'=4] {'dp','row','col'}, use_global_device_ids=true, to_apply=%region_1.0 | all-reduce | flops 2 | bytes 16 | tf_op jit(solution)/shard_map/psum | solution.py:30
  278.6 0.7 dynamic_slice.11
  280.8 0.0 all-gather.2.cloned.1.call-done
  280.8 0.0 copy-done.2
  280.8 0.0 copy-done
  280.8 4.5 %fusion.3 = (bf16[128,9216]{1,0:T(8,128)(2,1)}, f32[128,9216]{1,0:T(8,128)S(1)}) fusion(f32[]{:T(128)S(6)} %div.23, f32[9216]{0:T(1024)S(1)} %multiply_add_fusion, f32[128]{0:T(128)S(1)} %get-tuple-element.16, bf16[128,9216]{1,0:T(8,128)(2,1)S(1)} %copy-done, f32[]{:T(128)S(6)} %div.27, bf16[128,9216]{1,0:T(8,128)(2,1)} %all-gather.2.cloned.1.call-done), kind=kLoop, calls=%fused_computation.12 | loop fusion | flops 9437184 | bytes 11833864 | tf_op jit(solution)/shard_map/convert_element_type | solution.py:38
  285.3 1.6 constant_dynamic-slice_fusion
  (1 shorter events, 0.0 us)
Async XLA Ops:
  7.2 83.2 %all-reduce.3.cloned.1.call-start = ((), (), s32[]{:S(2)}) async-start(), calls=%async_computation.1 | async-start | bytes 4718592 | tf_op jit(solution)/shard_map/psum | solution.py:17
  7.2 151.9 %copy-start.3 = (f32[128]{0:T(128)S(1)}, f32[128]{0:T(128)}, u32[]{:S(2)}) copy-start(f32[128]{0:T(128)} %param.6) | copy-start | bytes 1540
  7.2 181.6 %copy-start.1 = (f32[9216]{0:T(1024)S(1)}, f32[9216]{0:T(1024)}, u32[]{:S(2)}) copy-start(f32[9216]{0:T(1024)} %param.7) | copy-start | bytes 110596
  7.9 272.9 %all-gather.2.cloned.1.call-start = ((), (), s32[]{:S(2)}) async-start(), calls=%async_computation | async-start | bytes 3538944 | tf_op jit(solution)/shard_map/all_gather | solution.py:18
  159.7 121.1 %copy-start.2 = (f32[128]{0:T(128)}, f32[128]{0:T(128)S(1)}, u32[]{:S(2)}) copy-start(f32[128]{0:T(128)S(1)} %get-tuple-element.16) | copy-start | bytes 1540
  189.5 91.3 %copy-start = (bf16[128,9216]{1,0:T(8,128)(2,1)S(1)}, bf16[128,9216]{1,0:T(8,128)(2,1)}, u32[]{:S(2)}) copy-start(bf16[128,9216]{1,0:T(8,128)(2,1)} %all-reduce.3.cloned.1.call-done) | copy-start | bytes 7077892
Sparse Core Ops, SparseCore 0:
  10.4 79.9 all-reduce.2
  92.7 39.5 all-gather.1
where the time goes:
time: 296 us
  blocking collectives  179 us (60%)
  waiting for transfers between devices  78.6 us (27%)
  between operations  18.4 us (6%)
  other arithmetic  17.3 us (6%)
    psum x1, blocking collectives, shards(): lax.psum((jnp.sum(update_part * update_part), weight_local), ('dp', 'row'...  84 us
    psum x1, waiting for transfers between devices, shards(): lax.psum(partial_value.astype(jnp.bfloat16), 'dp').astype(jnp.float32)  77.9 us
    psum x1, blocking collectives, shards(): lax.psum(jnp.sum(squares, axis=0).astype(jnp.bfloat16), 'row')  60.4 us
    psum x1, blocking collectives, shards(): row_mean = lax.psum(jnp.sum(new_rows), 'row') / R  29.1 us
  transfers between devices with their start and end apart: 2, of which 1 were waited for; matrix products, arithmetic and copies ran while one was open for 5% of the time, Pallas kernels for 0%

commit v1 on v0

v1 whole, which is shorter than its diff:
```python
import jax
import jax.numpy as jnp
from jax import lax
from jax.sharding import PartitionSpec as P

R = 2048
C = 36864
STEP = 10
CHUNKS = 4
SWAP = [(0, 1), (1, 0)]


def shards(params, grad_parts, row_moment, col_moment):
    decay_rate = 1.0 - STEP ** (-0.8)
    relative = min(0.01, STEP ** (-0.5))
    rows, width = params.shape
    step = width // CHUNKS
    position = lax.axis_index("dp")
    partial = grad_parts[0]

    def half(array, index, offset, size, axis):
        return lax.dynamic_slice_in_dim(array, index * width + offset, size, axis)

    pieces = []
    row_part = jnp.zeros((rows,), jnp.float32)
    col_parts = []
    received = [
        lax.ppermute(half(partial, 1 - position, k * step, step, 1), "dp", SWAP) for k in range(CHUNKS)
    ]
    for k in range(CHUNKS):
        piece = half(partial, position, k * step, step, 1).astype(jnp.float32) + received[k].astype(jnp.float32)
        squares = piece * piece + 1e-30
        row_part = row_part + jnp.sum(squares, axis=1)
        col_parts.append(jnp.sum(squares, axis=0))
        pieces.append(piece)
    gradient = jnp.concatenate(pieces, axis=1)
    col_part = jnp.concatenate(col_parts)
    weight_part = jnp.sum(params * params)

    sent = jnp.broadcast_to(row_part[None, None, :], (8, 1, rows))
    row_totals = jnp.sum(lax.all_to_all(sent, ("dp", "col"), 0, 0), axis=(0, 1))
    new_rows = decay_rate * row_moment + (1.0 - decay_rate) * (row_totals / C)

    sent = jnp.broadcast_to(col_part.astype(jnp.bfloat16).reshape(1, width // 128, 128), (16, width // 128, 128))
    got = lax.all_to_all(sent, "row", 0, 0)
    col_totals = jnp.sum(got.astype(jnp.float32), axis=0).reshape(width)
    old_cols = half(col_moment, position, 0, width, 0)
    new_cols = decay_rate * old_cols + (1.0 - decay_rate) * (col_totals / R)

    scaled = gradient * gradient * (1.0 / new_rows)[:, None] * (1.0 / new_cols)[None, :]
    sums = jnp.stack([jnp.sum(scaled), weight_part, jnp.sum(new_rows)])
    sums = jnp.pad(sums, (0, 125))
    sent = jnp.broadcast_to(sums[None, None, :], (128, 1, 128))
    totals = jnp.sum(lax.all_to_all(sent, ("dp", "row", "col"), 0, 0), axis=(0, 1))
    row_mean = totals[2] / (8 * R)
    clip_factor = jnp.maximum(1.0, jnp.sqrt(totals[0] * row_mean / (R * C)))
    param_scale = jnp.maximum(0.001, jnp.sqrt(totals[1] / (R * C)))
    step_size = relative * param_scale / clip_factor

    update = gradient * lax.rsqrt(new_rows / row_mean)[:, None] * lax.rsqrt(new_cols)[None, :]
    new_params = params - step_size * update
    own = new_params.astype(jnp.bfloat16)
    new_weights = jnp.zeros((rows, 2 * width), jnp.bfloat16)
    others = [lax.ppermute(own[:, k * step : (k + 1) * step], "dp", SWAP) for k in range(CHUNKS)]
    new_weights = lax.dynamic_update_slice_in_dim(new_weights, own, position * width, 1)
    for k in range(CHUNKS):
        new_weights = lax.dynamic_update_slice_in_dim(
            new_weights, others[k], (1 - position) * width + k * step, 1
        )
    return (new_params, new_weights, new_rows, new_cols, update, clip_factor, param_scale)


def solution(mesh):
    in_specs = (P("row", ("col", "dp")), P("dp", "row", "col"), P("row"), P("col"))
    out_specs = (
        P("row", ("col", "dp")),
        P("row", "col"),
        P("row"),
        P(("col", "dp")),
        P("row", ("col", "dp")),
        P(),
        P(),
    )
    return jax.shard_map(shards, mesh=mesh, in_specs=in_specs, out_specs=out_specs, check_vma=False)
```

time: 296 us -> 126 us (0.43)
  blocking collectives: 179 us -> 0 us
  starting transfers between devices: 0.08 us -> 33 us
  waiting for transfers between devices: 78.6 us -> 60.8 us
  between operations: 18.4 us -> 5.14 us
  local copies, waits for them, and re-layouts: 2.27 us -> 8.22 us
    psum x4 -> x0, blocking collectives: 179 us -> none  [the longest x1 84 us: shards(): lax.psum((jnp.sum(update_part * update_part), weight_local), ('dp', 'row'...]
    psum x1 -> x0, waiting for transfers between devices: 77.9 us -> none  [shards(): lax.psum(partial_value.astype(jnp.bfloat16), 'dp').astype(jnp.float32)]
    ppermute x0 -> x8, waiting for transfers between devices: none -> 43.1 us  [the longest x4 21.9 us: shards(): lax.ppermute(own[:, k * step:(k + 1) * step], 'dp', SWAP)]
    all_to_all x0 -> x3, starting transfers between devices: none -> 20.1 us  [the longest x1 7.64 us: shards(): got = lax.all_to_all(sent, 'row', 0, 0)]
    all_to_all x0 -> x3, waiting for transfers between devices: none -> 17.7 us  [the longest x1 8.11 us: shards(): lax.all_to_all(sent, ('dp', 'row', 'col'), 0, 0)]
    ppermute x0 -> x8, starting transfers between devices: none -> 12.9 us  [the longest x4 6.89 us: shards(): lax.ppermute(half(partial, 1 - position, k * step, step, 1), 'dp', SWAP)]
    convert_element_type x2 -> x0, other arithmetic: 8.97 us -> none  [the longest x1 4.52 us: shards(): params.astype(jnp.bfloat16)]
    reduce_sum x3 -> x7, other arithmetic: 5.68 us -> 9.57 us  [the longest x1 3.39 us: shards(): row_part = row_part + jnp.sum(squares, axis=1)]
  transfers between devices with their start and end apart: 2 -> 11, of which waited for: 1 -> 10; matrix products, arithmetic and copies ran while one was open for 5% -> 4% of each run, Pallas kernels for 0% -> 0%
where the time goes in v1:
time: 126 us; the launch traced here: 125 us
  waiting for transfers between devices  60.8 us (48%)
  starting transfers between devices  33 us (26%)
  other arithmetic  17.4 us (14%)
  local copies, waits for them, and re-layouts  8.22 us (7%)
  between operations  5.14 us (4%)
    ppermute x4, waiting for transfers between devices, shards(): lax.ppermute(own[:, k * step:(k + 1) * step], 'dp', SWAP)  21.9 us
    ppermute x4, waiting for transfers between devices, shards(): lax.ppermute(half(partial, 1 - position, k * step, step, 1), 'dp', SWAP)  21.2 us
    all_to_all x1, waiting for transfers between devices, shards(): lax.all_to_all(sent, ('dp', 'row', 'col'), 0, 0)  8.11 us
    all_to_all x1, starting transfers between devices, shards(): got = lax.all_to_all(sent, 'row', 0, 0)  7.64 us
    ppermute x4, starting transfers between devices, shards(): lax.ppermute(half(partial, 1 - position, k * step, step, 1), 'dp', SWAP)  6.89 us
    all_to_all x1, starting transfers between devices, shards(): lax.all_to_all(sent, ('dp', 'row', 'col'), 0, 0)  6.41 us
    ppermute x4, starting transfers between devices, shards(): lax.ppermute(own[:, k * step:(k + 1) * step], 'dp', SWAP)  6.02 us
    all_to_all x1, starting transfers between devices, shards(): row_totals = jnp.sum(lax.all_to_all(sent, ('dp', 'col'), 0, 0), axis=(0, 1))  6.01 us
  transfers between devices with their start and end apart: 11, of which 10 were waited for; matrix products, arithmetic and copies ran while one was open for 4% of the time, Pallas kernels for 0%

profile of v1, /device:TPU:1, one launch (start us, length us, event | category | flops | bytes accessed | tf_op | source)
XLA Modules:
  0.0 124.6 jit_solution(12839560894569900418)
XLA Ops:
  0.6 0.0 copy-start
  0.6 1.5 %dynamic-slice_bitcast_fusion.2 = (bf16[128,1152]{1,0:T(8,128)(2,1)S(1)}, bf16[128,1152]{1,0:T(8,128)(2,1)S(1)}, bf16[128,1152]{1,0:T(8,128)(2,1)S(1)}, bf16[128,1152]{1,0:T(8,128)(2,1)S(1)}) fusion(bf16[1,128,9216]{2,1,0:T(8,128)(2,1)} %param.5, s32[]{:T(128)S(6)} %select_n.33, s32[]{:T(128)S(6)} %select_n.35, s32[]{:T(128)S(6)} %select_n.31, s32[]{:T(128)S(6)} %select_n.37), kind=kLoop, calls=%fused_computation.24 | loop fusion | bytes 2359312 | tf_op jit(solution)/shard_map/dynamic_slice | solution.py:22
  2.1 3.8 %collective-permute-start.1 = (bf16[128,1152]{1,0:T(8,128)(2,1)S(1)}, bf16[128,1152]{1,0:T(8,128)(2,1)}, u32[]{:S(2)}, u32[]{:S(2)}) collective-permute-start(bf16[128,1152]{1,0:T(8,128)(2,1)S(1)} %get-tuple-element.36), channel_id=1, source_target_pairs={{0,64},{64,0},{1,65},{65,1},{2,66},{66,2},{3,67},{67,3},{4,68},{68... | collective-permute-start | bytes 884744 | tf_op jit(solution)/shard_map/ppermute | solution.py:28
  6.0 0.1 collective-permute-start.2
  6.1 2.9 %collective-permute-start = (bf16[128,1152]{1,0:T(8,128)(2,1)S(1)}, bf16[128,1152]{1,0:T(8,128)(2,1)}, u32[]{:S(2)}, u32[]{:S(2)}) collective-permute-start(bf16[128,1152]{1,0:T(8,128)(2,1)S(1)} %get-tuple-element.38), channel_id=1, source_target_pairs={{0,64},{64,0},{1,65},{65,1},{2,66},{66,2},{3,67},{67,3},{4,68},{68... | collective-permute-start | bytes 884744 | tf_op jit(solution)/shard_map/ppermute | solution.py:28
  8.9 0.1 collective-permute-start.3
  9.0 0.0 copy-done
  9.0 0.0 copy-start.4
  9.0 1.2 multiply_reduce_fusion
  10.2 2.3 %collective-permute-done.1 = bf16[128,1152]{1,0:T(8,128)(2,1)} collective-permute-done((bf16[128,1152]{1,0:T(8,128)(2,1)S(1)}, bf16[128,1152]{1,0:T(8,128)(2,1)}, u32[]{:S(2)}, u32[]{:S(2)}) %collective-permute-start.1) | collective-permute-done | bytes 294944 | tf_op jit(solution)/shard_map/ppermute | solution.py:28
  12.5 6.3 %collective-permute-done.2 = bf16[128,1152]{1,0:T(8,128)(2,1)} collective-permute-done((bf16[128,1152]{1,0:T(8,128)(2,1)S(1)}, bf16[128,1152]{1,0:T(8,128)(2,1)}, u32[]{:S(2)}, u32[]{:S(2)}) %collective-permute-start.2) | collective-permute-done | bytes 294944 | tf_op jit(solution)/shard_map/ppermute | solution.py:28
  18.8 6.3 %collective-permute-done = bf16[128,1152]{1,0:T(8,128)(2,1)} collective-permute-done((bf16[128,1152]{1,0:T(8,128)(2,1)S(1)}, bf16[128,1152]{1,0:T(8,128)(2,1)}, u32[]{:S(2)}, u32[]{:S(2)}) %collective-permute-start) | collective-permute-done | bytes 294944 | tf_op jit(solution)/shard_map/ppermute | solution.py:28
  25.2 6.3 %collective-permute-done.3 = bf16[128,1152]{1,0:T(8,128)(2,1)} collective-permute-done((bf16[128,1152]{1,0:T(8,128)(2,1)S(1)}, bf16[128,1152]{1,0:T(8,128)(2,1)}, u32[]{:S(2)}, u32[]{:S(2)}) %collective-permute-start.3) | collective-permute-done | bytes 294944 | tf_op jit(solution)/shard_map/ppermute | solution.py:28
  31.5 0.0 copy-done.4
  31.5 3.4 %fusion.3 = (f32[128]{0:T(128)S(1)}, bf16[1152]{0:T(1024)(128)(2,1)}, f32[128,1152]{1,0:T(8,128)S(1)}, bf16[1152]{0:T(1024)(128)(2,1)}, f32[128]{0:T(128)S(1)}, ...) fusion(bf16[128,1152]{1,0:T(8,128)(2,1)} %collective-permute-do, ...), kind=kLoop, calls=%fused_computation.16 | loop fusion | flops 4123648 | bytes 4729872 | tf_op jit(solution)/shard_map/reduce_sum | solution.py:33
  34.9 0.6 broadcast_in_dim.8
  35.5 6.0 %all-to-all-start = ((f32[8,1,128]{2,1,0:T(1,128)}), f32[8,1,128]{2,1,0:T(1,128)S(1)}, u32[]{:S(2)}, u32[]{:S(2)}) async-start(f32[8,1,128]{2,1,0:T(1,128)} %broadcast_in_dim.8), calls=%async_computation | async-start | bytes 8192 | tf_op jit(solution)/shard_map/all_to_all | solution.py:41
  41.5 0.7 pad_maximum_fusion.1
  42.2 3.9 %all-to-all-done = f32[8,1,128]{2,1,0:T(1,128)S(1)} async-done(((f32[8,1,128]{2,1,0:T(1,128)}), f32[8,1,128]{2,1,0:T(1,128)S(1)}, u32[]{:S(2)}, u32[]{:S(2)}) %all-to-all-start) | async-done | bytes 4128 | tf_op jit(solution)/shard_map/all_to_all | solution.py:41
  46.1 0.7 broadcast_in_dim.9
  46.8 7.6 %all-to-all-start.1 = ((bf16[16,36,128]{2,1,0:T(8,128)(2,1)}), bf16[16,36,128]{2,1,0:T(8,128)(2,1)}, u32[]{:S(2)}, u32[]{:S(2)}) async-start(bf16[16,36,128]{2,1,0:T(8,128)(2,1)} %broadcast_in_dim.9), calls=%async_computation.1 | async-start | bytes 327680 | tf_op jit(solution)/shard_map/all_to_all | solution.py:45
  54.4 0.7 broadcast_divide_fusion.1
  55.1 0.0 copy-start.6
  55.1 0.6 reduce_sum.138
  55.7 5.7 %all-to-all-done.1 = bf16[16,36,128]{2,1,0:T(8,128)(2,1)} async-done(((bf16[16,36,128]{2,1,0:T(8,128)(2,1)}), bf16[16,36,128]{2,1,0:T(8,128)(2,1)}, u32[]{:S(2)}, u32[]{:S(2)}) %all-to-all-start.1) | async-done | bytes 147488 | tf_op jit(solution)/shard_map/all_to_all | solution.py:45
  61.4 1.0 convert_reduce_fusion
  62.4 1.4 %broadcast_divide_fusion = (f32[4608]{0:T(1024)S(1)}, f32[4608]{0:T(1024)}) fusion(f32[36,128]{1,0:T(8,128)S(1)} %convert_reduce_fusion, f32[9216]{0:T(1024)} %param.7, s32[]{:T(128)S(6)} %select_n.30), kind=kLoop, calls=%fused_computation.28 | loop fusion | flops 18432 | bytes 73732 | tf_op jit(solution)/shard_map/div | solution.py:50
  63.8 2.5 %multiply_reduce_fusion.1 = f32[]{:T(128)} fusion(f32[128,1152]{1,0:T(8,128)} %get-tuple-element.35, f32[128,1152]{1,0:T(8,128)S(1)} %get-tuple-element.29, f32[128,1152]{1,0:T(8,128)S(1)} %get-tuple-element.24, f32[128,1152]{1,0:T(8,128)} %get-tuple-element.32, f32[4608]{0:T(1024)S(1)} %get-tuple-element.21, f32[128]{0:T(128)S(1)} %get-tuple-element.19), kind=kLoop, calls=%fused_computation.4 | loop fusion | flops 4128767 | bytes 2378244 | tf_op jit(solution)/shard_map/reduce_sum | solution.py:51
  66.4 2.0 %select_maximum_fusion = f32[128]{0:T(128)S(1)} fusion(f32[1]{0:T(128)} %bitcast.16, f32[1]{0:T(128)} %bitcast.15, f32[1]{0:T(128)} %bitcast.14), kind=kLoop, calls=%fused_computation.38 | loop fusion | flops 768 | bytes 524 | tf_op jit(solution)/shard_map/stack | solution.py:51
  68.4 0.7 broadcast_in_dim.10
  69.0 6.4 %all-to-all-start.2 = ((f32[128,1,128]{2,1,0:T(1,128)}), f32[128,1,128]{2,1,0:T(1,128)}, u32[]{:S(2)}, u32[]{:S(2)}) async-start(f32[128,1,128]{2,1,0:T(1,128)} %broadcast_in_dim.10), calls=%async_computation.2 | async-start | bytes 131072 | tf_op jit(solution)/shard_map/all_to_all | solution.py:54
  75.5 1.3 %rsqrt.7 = f32[4608]{0:T(1024)} rsqrt(f32[4608]{0:T(1024)} %get-tuple-element.22) | non-fusion elementwise | bytes 36864 | tf_op jit(solution)/shard_map/rsqrt | solution.py:60
  76.8 8.1 %all-to-all-done.2 = f32[128,1,128]{2,1,0:T(1,128)} async-done(((f32[128,1,128]{2,1,0:T(1,128)}), f32[128,1,128]{2,1,0:T(1,128)}, u32[]{:S(2)}, u32[]{:S(2)}) %all-to-all-start.2) | async-done | bytes 65568 | tf_op jit(solution)/shard_map/all_to_all | solution.py:54
  84.9 0.9 reduce_sum.139
  85.8 0.6 fusion.9
  88.5 0.0 copy-start.1
  88.5 0.0 copy-start.2
  88.5 0.0 copy-start.5
  88.5 0.2 broadcast_in_dim.11
  88.7 0.0 copy-done.6
  88.7 0.8 copy-done.1
  89.5 0.2 copy-done.2
  89.7 0.0 copy-done.5
  89.7 3.0 %constant_dynamic-update-slice_fusion.4 = (bf16[128,9216]{1,0:T(8,128)(2,1)S(1)}, bf16[128,4608]{1,0:T(8,128)(2,1)S(1)}, f32[128,4608]{1,0:T(8,128)}, f32[128,4608]{1,0:T(8,128)}) fusion(bf16[128,9216]{1,0:T(8,128)(2,1)S(1)} %broadcast_in_dim.11, s32[]{:T(128)S(6)} %select_n.30, f32[128,4608]{1,0:T(8,128)S(1)} %copy-done, f32[]{:T(128)S(6)} %div.44, ...), kind=kLoop, calls=%fused_computation.37 | loop fusion | flops 4718592 | bytes 11817480 | tf_op jit(solution)/shard_map/dynamic_update_slice | solution.py:65
  92.7 0.1 fusion.8
  92.8 1.3 %collective-permute-start.4 = (bf16[128,1152]{1,0:T(8,128)(2,1)S(1)}, bf16[128,1152]{1,0:T(8,128)(2,1)S(1)}, u32[]{:S(2)}, u32[]{:S(2)}) collective-permute-start(bf16[128,1152]{1,0:T(8,128)(2,1)S(1)} %get-tuple-element.43), channel_id=1, source_target_pairs={{0,64},{64,0},{1,65},{65,1},{2,66},{66,2},{3,67},{67,3},{4,68},{68... | collective-permute-start | bytes 884744 | tf_op jit(solution)/shard_map/ppermute | solution.py:64
  94.1 1.7 %collective-permute-start.5 = (bf16[128,1152]{1,0:T(8,128)(2,1)S(1)}, bf16[128,1152]{1,0:T(8,128)(2,1)S(1)}, u32[]{:S(2)}, u32[]{:S(2)}) collective-permute-start(bf16[128,1152]{1,0:T(8,128)(2,1)S(1)} %get-tuple-element.42), channel_id=1, source_target_pairs={{0,64},{64,0},{1,65},{65,1},{2,66},{66,2},{3,67},{67,3},{4,68},{68... | collective-permute-start | bytes 884744 | tf_op jit(solution)/shard_map/ppermute | solution.py:64
  95.8 1.2 collective-permute-start.7
  97.1 1.7 %collective-permute-start.6 = (bf16[128,1152]{1,0:T(8,128)(2,1)S(1)}, bf16[128,1152]{1,0:T(8,128)(2,1)S(1)}, u32[]{:S(2)}, u32[]{:S(2)}) collective-permute-start(bf16[128,1152]{1,0:T(8,128)(2,1)S(1)} %get-tuple-element.41), channel_id=1, source_target_pairs={{0,64},{64,0},{1,65},{65,1},{2,66},{66,2},{3,67},{67,3},{4,68},{68... | collective-permute-start | bytes 884744 | tf_op jit(solution)/shard_map/ppermute | solution.py:64
  98.8 3.0 %collective-permute-done.4 = bf16[128,1152]{1,0:T(8,128)(2,1)S(1)} collective-permute-done((bf16[128,1152]{1,0:T(8,128)(2,1)S(1)}, bf16[128,1152]{1,0:T(8,128)(2,1)S(1)}, u32[]{:S(2)}, u32[]{:S(2)}) %collective-permute-start.4) | collective-permute-done | bytes 294944 | tf_op jit(solution)/shard_map/ppermute | solution.py:64
  101.9 6.3 %collective-permute-done.5 = bf16[128,1152]{1,0:T(8,128)(2,1)S(1)} collective-permute-done((bf16[128,1152]{1,0:T(8,128)(2,1)S(1)}, bf16[128,1152]{1,0:T(8,128)(2,1)S(1)}, u32[]{:S(2)}, u32[]{:S(2)}) %collective-permute-start.5) | collective-permute-done | bytes 294944 | tf_op jit(solution)/shard_map/ppermute | solution.py:64
  108.2 12.6 %collective-permute-done.6 = bf16[128,1152]{1,0:T(8,128)(2,1)S(1)} collective-permute-done((bf16[128,1152]{1,0:T(8,128)(2,1)S(1)}, bf16[128,1152]{1,0:T(8,128)(2,1)S(1)}, u32[]{:S(2)}, u32[]{:S(2)}) %collective-permute-start.6) | collective-permute-done | bytes 294944 | tf_op jit(solution)/shard_map/ppermute | solution.py:64
  120.8 0.0 collective-permute-done.7
  120.9 0.0 copy-start.3
  120.9 1.4 %copy-done.3 = bf16[128,9216]{1,0:T(8,128)(2,1)} copy-done((bf16[128,9216]{1,0:T(8,128)(2,1)}, bf16[128,9216]{1,0:T(8,128)(2,1)S(1)}, u32[]{:S(2)}) %copy-start.3) | copy-done | bytes 2359320
  (7 shorter events, 0.2 us)
Async XLA Ops:
  0.6 8.4 %copy-start = (f32[128,4608]{1,0:T(8,128)S(1)}, f32[128,4608]{1,0:T(8,128)}, u32[]{:S(2)}) copy-start(f32[128,4608]{1,0:T(8,128)} %param.4) | copy-start | bytes 7077892
  2.1 10.4 %collective-permute-start.1 = (bf16[128,1152]{1,0:T(8,128)(2,1)S(1)}, bf16[128,1152]{1,0:T(8,128)(2,1)}, u32[]{:S(2)}, u32[]{:S(2)}) collective-permute-start(bf16[128,1152]{1,0:T(8,128)(2,1)S(1)} %get-tuple-element.36), channel_id=1, source_target_pairs={{0,64},{64,0},{1,65},{65,1},{2,66},{66,2},{3,67},{67,3},{4,68},{68... | collective-permute-start | bytes 884744 | tf_op jit(solution)/shard_map/ppermute | solution.py:28
  6.0 12.9 %collective-permute-start.2 = (bf16[128,1152]{1,0:T(8,128)(2,1)S(1)}, bf16[128,1152]{1,0:T(8,128)(2,1)}, u32[]{:S(2)}, u32[]{:S(2)}) collective-permute-start(bf16[128,1152]{1,0:T(8,128)(2,1)S(1)} %get-tuple-element.37), channel_id=1, source_target_pairs={{0,64},{64,0},{1,65},{65,1},{2,66},{66,2},{3,67},{67,3},{4,68},{68... | collective-permute-start | bytes 884744 | tf_op jit(solution)/shard_map/ppermute | solution.py:28
  6.1 19.1 %collective-permute-start = (bf16[128,1152]{1,0:T(8,128)(2,1)S(1)}, bf16[128,1152]{1,0:T(8,128)(2,1)}, u32[]{:S(2)}, u32[]{:S(2)}) collective-permute-start(bf16[128,1152]{1,0:T(8,128)(2,1)S(1)} %get-tuple-element.38), channel_id=1, source_target_pairs={{0,64},{64,0},{1,65},{65,1},{2,66},{66,2},{3,67},{67,3},{4,68},{68... | collective-permute-start | bytes 884744 | tf_op jit(solution)/shard_map/ppermute | solution.py:28
  8.9 22.5 %collective-permute-start.3 = (bf16[128,1152]{1,0:T(8,128)(2,1)S(1)}, bf16[128,1152]{1,0:T(8,128)(2,1)}, u32[]{:S(2)}, u32[]{:S(2)}) collective-permute-start(bf16[128,1152]{1,0:T(8,128)(2,1)S(1)} %get-tuple-element.39), channel_id=1, source_target_pairs={{0,64},{64,0},{1,65},{65,1},{2,66},{66,2},{3,67},{67,3},{4,68},{68... | collective-permute-start | bytes 884744 | tf_op jit(solution)/shard_map/ppermute | solution.py:28
  9.0 22.5 %copy-start.4 = (bf16[1,128,9216]{2,1,0:T(8,128)(2,1)S(1)}, bf16[1,128,9216]{2,1,0:T(8,128)(2,1)}, u32[]{:S(2)}) copy-start(bf16[1,128,9216]{2,1,0:T(8,128)(2,1)} %param.5) | copy-start | bytes 7077892
  35.5 10.6 %all-to-all-start = ((f32[8,1,128]{2,1,0:T(1,128)}), f32[8,1,128]{2,1,0:T(1,128)S(1)}, u32[]{:S(2)}, u32[]{:S(2)}) async-start(f32[8,1,128]{2,1,0:T(1,128)} %broadcast_in_dim.8), calls=%async_computation | async-start | bytes 8192 | tf_op jit(solution)/shard_map/all_to_all | solution.py:41
  46.8 14.7 %all-to-all-start.1 = ((bf16[16,36,128]{2,1,0:T(8,128)(2,1)}), bf16[16,36,128]{2,1,0:T(8,128)(2,1)}, u32[]{:S(2)}, u32[]{:S(2)}) async-start(bf16[16,36,128]{2,1,0:T(8,128)(2,1)} %broadcast_in_dim.9), calls=%async_computation.1 | async-start | bytes 327680 | tf_op jit(solution)/shard_map/all_to_all | solution.py:45
  55.1 33.6 %copy-start.6 = (f32[128]{0:T(128)}, f32[128]{0:T(128)S(1)}, u32[]{:S(2)}) copy-start(f32[128]{0:T(128)S(1)} %get-tuple-element.20) | copy-start | bytes 1540
  69.0 15.9 %all-to-all-start.2 = ((f32[128,1,128]{2,1,0:T(1,128)}), f32[128,1,128]{2,1,0:T(1,128)}, u32[]{:S(2)}, u32[]{:S(2)}) async-start(f32[128,1,128]{2,1,0:T(1,128)} %broadcast_in_dim.10), calls=%async_computation.2 | async-start | bytes 131072 | tf_op jit(solution)/shard_map/all_to_all | solution.py:54
  88.5 1.1 copy-start.1
  88.5 1.2 copy-start.2
  88.5 1.2 copy-start.5
  92.8 9.0 %collective-permute-start.4 = (bf16[128,1152]{1,0:T(8,128)(2,1)S(1)}, bf16[128,1152]{1,0:T(8,128)(2,1)S(1)}, u32[]{:S(2)}, u32[]{:S(2)}) collective-permute-start(bf16[128,1152]{1,0:T(8,128)(2,1)S(1)} %get-tuple-element.43), channel_id=1, source_target_pairs={{0,64},{64,0},{1,65},{65,1},{2,66},{66,2},{3,67},{67,3},{4,68},{68... | collective-permute-start | bytes 884744 | tf_op jit(solution)/shard_map/ppermute | solution.py:64
  94.1 14.0 %collective-permute-start.5 = (bf16[128,1152]{1,0:T(8,128)(2,1)S(1)}, bf16[128,1152]{1,0:T(8,128)(2,1)S(1)}, u32[]{:S(2)}, u32[]{:S(2)}) collective-permute-start(bf16[128,1152]{1,0:T(8,128)(2,1)S(1)} %get-tuple-element.42), channel_id=1, source_target_pairs={{0,64},{64,0},{1,65},{65,1},{2,66},{66,2},{3,67},{67,3},{4,68},{68... | collective-permute-start | bytes 884744 | tf_op jit(solution)/shard_map/ppermute | solution.py:64
  95.8 25.0 %collective-permute-start.7 = (bf16[128,1152]{1,0:T(8,128)(2,1)S(1)}, bf16[128,1152]{1,0:T(8,128)(2,1)S(1)}, u32[]{:S(2)}, u32[]{:S(2)}) collective-permute-start(bf16[128,1152]{1,0:T(8,128)(2,1)S(1)} %get-tuple-element.40), channel_id=1, source_target_pairs={{0,64},{64,0},{1,65},{65,1},{2,66},{66,2},{3,67},{67,3},{4,68},{68... | collective-permute-start | bytes 884744 | tf_op jit(solution)/shard_map/ppermute | solution.py:64
  97.1 23.7 %collective-permute-start.6 = (bf16[128,1152]{1,0:T(8,128)(2,1)S(1)}, bf16[128,1152]{1,0:T(8,128)(2,1)S(1)}, u32[]{:S(2)}, u32[]{:S(2)}) collective-permute-start(bf16[128,1152]{1,0:T(8,128)(2,1)S(1)} %get-tuple-element.41), channel_id=1, source_target_pairs={{0,64},{64,0},{1,65},{65,1},{2,66},{66,2},{3,67},{67,3},{4,68},{68... | collective-permute-start | bytes 884744 | tf_op jit(solution)/shard_map/ppermute | solution.py:64
  120.9 1.4 %copy-start.3 = (bf16[128,9216]{1,0:T(8,128)(2,1)}, bf16[128,9216]{1,0:T(8,128)(2,1)S(1)}, u32[]{:S(2)}) copy-start(bf16[128,9216]{1,0:T(8,128)(2,1)S(1)} %constant_dynamic-update-slice_fusion) | copy-start | bytes 7077892

commit v2 on v0

v2 whole, which is shorter than its diff:
```python
import functools

import jax
import jax.numpy as jnp
from jax import lax
from jax.experimental import pallas as pl
from jax.experimental.pallas import tpu as pltpu
from jax.sharding import PartitionSpec as P

R = 2048
C = 36864
STEP = 10
DECAY = 1.0 - STEP ** (-0.8)
RELATIVE = min(0.01, STEP ** (-0.5))
LANES = 128
SWAP = [(0, 1), (1, 0)]
PIECES = 4
BLOCK = 512
EARLY = 3
LATE = (4, 2)
VMEM_LIMIT = 24 << 20
f32, bf16 = jnp.float32, jnp.bfloat16
shape = jax.ShapeDtypeStruct


def down(row):
    return jnp.broadcast_to(row, (LANES, LANES)).T


def flat(acc):
    return jnp.sum(acc.T, axis=0, keepdims=True)


def tile(at):
    return slice(at * LANES, (at + 1) * LANES)


def sums_kernel(mine_ref, got_ref, grad_ref, row_ref, sent_ref, acc_ref, cols_ref):
    k = pl.program_id(0)
    tiles = got_ref.shape[1] // LANES

    @pl.when(k == 0)
    def _():
        acc_ref[...] = jnp.zeros_like(acc_ref)
        cols_ref[...] = jnp.zeros_like(cols_ref)

    acc = acc_ref[...]
    for t in range(tiles):
        g = mine_ref[:, tile(t)].astype(f32) + got_ref[:, tile(t)].astype(f32)
        grad_ref[:, tile(t)] = g
        squares = g * g + 1e-30
        acc = acc + squares
        cols_ref[pl.ds(k * tiles + t, 1), :] = jnp.sum(squares, axis=0, keepdims=True)
    acc_ref[...] = acc

    @pl.when(k == pl.num_programs(0) - 1)
    def _():
        row_ref[...] = flat(acc_ref[...])
        sent = cols_ref[...].astype(bf16)
        for peer in range(sent_ref.shape[0]):
            sent_ref[peer] = sent


def moments_kernel(
    grad_ref, got_ref, row_ref, old_rows_ref, old_cols_ref, weight_ref,
    new_cols_ref, copy_ref, sent_ref, inv_cols, acc_ref,
):
    k = pl.program_id(0)
    height = new_cols_ref.shape[0]
    tiles = grad_ref.shape[1] // LANES

    @pl.when(k == 0)
    def _():
        totals = got_ref[0].astype(f32)
        for peer in range(1, got_ref.shape[0]):
            totals = totals + got_ref[peer].astype(f32)
        new_cols = DECAY * old_cols_ref[...] + (1.0 - DECAY) * (totals[:height] / R)
        new_cols_ref[...] = new_cols
        copy_ref[...] = new_cols
        inv_cols[...] = 1.0 / new_cols
        acc_ref[...] = jnp.zeros_like(acc_ref)

    acc = acc_ref[...]
    for t in range(tiles):
        g = grad_ref[:, tile(t)]
        acc = acc + g * g * inv_cols[pl.ds(k * tiles + t, 1), :]
    acc_ref[...] = acc

    @pl.when(k == pl.num_programs(0) - 1)
    def _():
        at = lax.broadcasted_iota(jnp.int32, (4, LANES), 0)
        rows = [row_ref[...], flat(acc_ref[...]), old_rows_ref[...], jnp.full((1, LANES), weight_ref[0, 0])]
        sent = jnp.zeros((4, LANES), f32)
        for i, row in enumerate(rows):
            sent = jnp.where(at == i, jnp.broadcast_to(row, (4, LANES)), sent)
        sent_ref[...] = jnp.broadcast_to(sent[None], sent_ref.shape)


def weights_block(grad_ref, params_ref, out_ref, row_scale, col_scale, step_size, first, to=0):
    for t in range(grad_ref.shape[1] // LANES):
        update = grad_ref[:, tile(t)] * row_scale * col_scale[pl.ds(first + t, 1), :]
        new = (params_ref[:, tile(t)] - step_size * update).astype(bf16)
        out_ref[:, pl.ds(pl.multiple_of(to + t * LANES, LANES), LANES)] = new


def first_weights_kernel(
    at_ref, got_ref, cols_ref, grad_ref, params_ref,
    out_ref, rows_ref, clip_ref, scale_ref, step_ref, row_scale, col_scale, all_rows,
):
    k = pl.program_id(0)

    @pl.when(k == 0)
    def _():
        update_sum = jnp.zeros((1, LANES), f32)
        row_sum = jnp.zeros((1, LANES), f32)
        weight_sum = jnp.zeros((1, LANES), f32)
        for block in range(16):
            got = None
            for d in range(2):
                for c in range(4):
                    term = got_ref[d * 64 + block * 4 + c]
                    got = term if got is None else got + term
            rows = DECAY * got_ref[block * 4][2:3] + (1.0 - DECAY) * (got[0:1] / C)
            all_rows[block : block + 1, :] = rows
            update_sum = update_sum + got[1:2] / rows
            row_sum = row_sum + rows
            weight_sum = weight_sum + got[3:4]
        row_mean = jnp.sum(row_sum, axis=1, keepdims=True) / R
        rows = all_rows[pl.ds(at_ref[1], 1), :]
        rows_ref[...] = rows
        row_scale[...] = down(lax.rsqrt(rows / row_mean))
        col_scale[...] = lax.rsqrt(cols_ref[...])
        update_mean = jnp.sum(update_sum, axis=1, keepdims=True) * row_mean / (R * C)
        weight_mean = weight_sum[:, :1] / (R * C)
        clip_factor = jnp.maximum(1.0, jnp.sqrt(update_mean))
        param_scale = jnp.maximum(0.001, jnp.sqrt(weight_mean))
        clip_ref[...] = clip_factor
        scale_ref[...] = param_scale
        step_ref[...] = RELATIVE * param_scale / clip_factor
        if EARLY:
            scale = jnp.zeros((LANES, LANES), f32)
            for t in range(EARLY * BLOCK // LANES):
                scale_cols = jnp.broadcast_to(col_scale[t : t + 1, :], (LANES, LANES))
                scale = jnp.where(lax.broadcasted_iota(jnp.int32, scale.shape, 0) == t, scale_cols, scale)
            out_ref[:, pl.ds(LATE[0] * BLOCK, LANES)] = scale.astype(bf16)

    first = (EARLY + k) * (BLOCK // LANES)
    weights_block(grad_ref, params_ref, out_ref, row_scale[...], col_scale, step_ref[...], first, k * BLOCK)


def weights_kernel(start, grad_ref, params_ref, row_scale, col_scale, step_ref, out_ref):
    first = (start + pl.program_id(0)) * (BLOCK // LANES)
    weights_block(grad_ref, params_ref, out_ref, row_scale[...], col_scale, step_ref[...], first)


def params_kernel(at_ref, grad_ref, params_ref, row_scale, col_scale, step_ref, new_ref, update_ref, weights_ref):
    first = pl.program_id(0) * (BLOCK // LANES)
    across, step_size = row_scale[...], step_ref[...]
    for t in range(BLOCK // LANES):
        update = grad_ref[:, tile(t)] * across * col_scale[pl.ds(first + t, 1), :]
        new = params_ref[:, tile(t)] - step_size * update
        update_ref[:, tile(t)] = update
        new_ref[:, tile(t)] = new
        weights_ref[:, tile(t)] = new.astype(bf16)


def early_kernel(at_ref, mine_ref, grad_ref, params_ref, row_scale, cols_ref, step_ref, _, out_ref, scale_ref):
    k = pl.program_id(0)

    @pl.when(k == 0)
    def _():
        scale_ref[...] = cols_ref[...].astype(f32)

    first = k * (BLOCK // LANES)
    across, step_size = row_scale[...], step_ref[...]
    for t in range(BLOCK // LANES):
        g = mine_ref[0, :, tile(t)].astype(f32) + grad_ref[:, tile(t)].astype(f32)
        update = g * across * scale_ref[pl.ds(first + t, 1), :]
        out_ref[:, tile(t)] = (params_ref[:, tile(t)].astype(f32) - step_size * update).astype(bf16)


def place_kernel(at_ref, got_ref, _, out_ref):
    out_ref[...] = got_ref[...]


def whole(*dims):
    return pl.BlockSpec(dims, lambda *_: (0,) * len(dims))


def call(kernel, grid, ins, outs, args, nbytes, scratch=(), at=None, aliases=None):
    prefetch = () if at is None else (at,)
    return pl.pallas_call(
        kernel,
        grid_spec=pltpu.PrefetchScalarGridSpec(
            num_scalar_prefetch=len(prefetch), grid=(grid,), in_specs=ins,
            out_specs=[spec for spec, _ in outs], scratch_shapes=list(scratch),
        ),
        out_shape=[out for _, out in outs],
        input_output_aliases=aliases or {},
        cost_estimate=pl.CostEstimate(flops=nbytes, bytes_accessed=nbytes, transcendentals=0),
        compiler_params=pltpu.CompilerParams(vmem_limit_bytes=VMEM_LIMIT),
    )(*prefetch, *args)


def shards(params, grad_parts, row_moment, col_moment):
    rows, width = params.shape
    height = width // LANES
    padded = -(-height // 16) * 16
    piece = width // PIECES
    blocks = width // BLOCK
    position = lax.axis_index("dp")
    other = 1 - position
    at = jnp.stack([position, lax.axis_index("row")]).astype(jnp.int32)
    any_spec = pl.BlockSpec(memory_space=pl.ANY)
    row_spec, col_spec, one_spec = whole(1, rows), whole(height, LANES), whole(1, 1)
    square = whole(rows, LANES)
    block_at = lambda first: pl.BlockSpec((rows, BLOCK), lambda k, *_: (0, first + k))

    outgoing = lax.dynamic_slice_in_dim(grad_parts[0], other * width, width, 1)
    got = lax.ppermute(outgoing, "dp", SWAP)
    later, later_params, later_cols, _ = lax.optimization_barrier((grad_parts[0], params, col_moment, outgoing))
    mine = lax.dynamic_slice_in_dim(later, position * width, width, 1)
    parts = lax.dynamic_slice_in_dim(later, position * width, EARLY * BLOCK, 1)
    ahead = jnp.concatenate([parts, later_params[:, : EARLY * BLOCK].astype(bf16)], axis=1)
    ahead = lax.ppermute(ahead, "dp", SWAP)
    weight_part = jnp.sum(later_params * later_params).reshape(1, 1)
    old_cols = lax.dynamic_slice_in_dim(later_cols, position * width, width, 0).reshape(height, LANES)
    got, mine, weight_part, old_cols, at = lax.optimization_barrier((got, mine, weight_part, old_cols, at))

    part = pl.BlockSpec((rows, piece), lambda k: (0, k))
    gradient, row_part, sent = call(
        sums_kernel, PIECES, [part, part],
        [(part, shape((rows, width), f32)), (row_spec, shape((1, rows), f32)),
         (whole(16, padded, LANES), shape((16, padded, LANES), bf16))],
        (mine, got), 8 * rows * width,
        [pltpu.VMEM((rows, LANES), f32), pltpu.VMEM((padded, LANES), f32)],
    )

    col_parts = lax.all_to_all(sent, "row", 0, 0)
    wide = pl.BlockSpec((rows, 3 * BLOCK), lambda k: (0, k))
    new_cols, cols_copy, sent = call(
        moments_kernel, blocks // 3,
        [wide, whole(16, padded, LANES), row_spec, row_spec, col_spec, pl.BlockSpec(memory_space=pltpu.SMEM)],
        [(col_spec, shape((height, LANES), f32))] * 2 + [(whole(128, 4, LANES), shape((128, 4, LANES), f32))],
        (gradient, col_parts, row_part, row_moment.reshape(1, rows), old_cols, weight_part), 4 * rows * width,
        [pltpu.VMEM((height, LANES), f32), pltpu.VMEM((rows, LANES), f32)],
    )
    sent, ahead = lax.optimization_barrier((sent, ahead))
    parts = lax.all_to_all(sent, ("dp", "row", "col"), 0, 0)
    sent_width = LATE[0] * BLOCK + (LANES if EARLY else 0)
    out, new_rows, clip_factor, param_scale, step_size, row_scale, col_scale = call(
        first_weights_kernel, LATE[0],
        [whole(128, 4, LANES), col_spec, block_at(EARLY), block_at(EARLY)],
        [(whole(rows, sent_width), shape((rows, sent_width), bf16)), (row_spec, shape((1, rows), f32)),
         (one_spec, shape((1, 1), f32)), (one_spec, shape((1, 1), f32)), (one_spec, shape((1, 1), f32)),
         (square, shape((rows, LANES), f32)), (col_spec, shape((height, LANES), f32))],
        (parts, cols_copy, gradient, params), 4 * rows * LATE[0] * BLOCK,
        [pltpu.VMEM((16, LANES), f32)], at,
    )
    late = [lax.ppermute(out, "dp", SWAP)]
    start = EARLY + LATE[0]
    for count in LATE[1:]:
        (out,) = call(
            functools.partial(weights_kernel, start), count,
            [block_at(start), block_at(start), square, col_spec, one_spec],
            [(block_at(0), shape((rows, count * BLOCK), bf16))],
            (gradient, params, row_scale, col_scale, step_size), 4 * rows * count * BLOCK,
        )
        late.append(lax.ppermute(out, "dp", SWAP))
        start += count

    new_params, update, new_weights = call(
        params_kernel, blocks,
        [block_at(0), block_at(0), square, col_spec, one_spec],
        [(block_at(0), shape((rows, width), f32)), (block_at(0), shape((rows, width), f32)),
         (pl.BlockSpec((rows, BLOCK), lambda k, at: (0, at[0] * blocks + k)), shape((rows, 2 * width), bf16))],
        (gradient, params, row_scale, col_scale, step_size), 18 * rows * width, (), at,
    )
    out_shape = shape((rows, 2 * width), bf16)
    (new_weights,) = call(
        early_kernel, EARLY,
        [pl.BlockSpec((1, rows, BLOCK), lambda k, at: (0, 0, (1 - at[0]) * blocks + k)),
         block_at(0), block_at(EARLY), square,
         pl.BlockSpec((rows, LANES), lambda *_: (0, LATE[0] * BLOCK // LANES)), one_spec, any_spec],
        [(pl.BlockSpec((rows, BLOCK), lambda k, at: (0, (1 - at[0]) * blocks + k)), out_shape)],
        (grad_parts, ahead, ahead, row_scale, late[0], step_size, new_weights),
        8 * rows * EARLY * BLOCK, [pltpu.VMEM((rows, LANES), f32)], at, {7: 0},
    )
    start = EARLY
    for count, values in zip(LATE, late):
        (new_weights,) = call(
            place_kernel, count, [block_at(0), any_spec],
            [(pl.BlockSpec((rows, BLOCK), lambda k, at, s=start: (0, (1 - at[0]) * blocks + s + k)), out_shape)],
            (values, new_weights), 4 * rows * count * BLOCK, (), at, {2: 0},
        )
        start += count
    return (
        new_params, new_weights, new_rows.reshape(rows), new_cols.reshape(width), update,
        clip_factor.reshape(()), param_scale.reshape(()),
    )


def solution(mesh):
    in_specs = (P("row", ("col", "dp")), P("dp", "row", "col"), P("row"), P("col"))
    out_specs = (
        P("row", ("col", "dp")),
        P("row", "col"),
        P("row"),
        P(("col", "dp")),
        P("row", ("col", "dp")),
        P(),
        P(),
    )
    return jax.shard_map(shards, mesh=mesh, in_specs=in_specs, out_specs=out_specs, check_vma=False)
```

time: 296 us -> 97.1 us (0.33)
  blocking collectives: 179 us -> 35.1 us
  waiting for transfers between devices: 78.6 us -> 27.9 us
  Pallas kernels: 0 us -> 19.5 us
  between operations: 18.4 us -> 0.69 us
  other arithmetic: 17.3 us -> 2.24 us
  starting transfers between devices: 0.08 us -> 6.8 us
    psum x4 -> x0, blocking collectives: 179 us -> none  [the longest x1 84 us: shards(): lax.psum((jnp.sum(update_part * update_part), weight_local), ('dp', 'row'...]
    psum x1 -> x0, waiting for transfers between devices: 77.9 us -> none  [shards(): lax.psum(partial_value.astype(jnp.bfloat16), 'dp').astype(jnp.float32)]
    all_to_all x0 -> x2, blocking collectives: none -> 35.1 us  [the longest x1 20.7 us: shards(): parts = lax.all_to_all(sent, ('dp', 'row', 'col'), 0, 0)]
    ppermute x0 -> x4, waiting for transfers between devices: none -> 27.9 us  [the longest x1 21.9 us: shards(): got = lax.ppermute(outgoing, 'dp', SWAP)]
    pallas_call x0 -> x8, Pallas kernels: none -> 19.5 us  [call(): pl.pallas_call(kernel, grid_spec=pltpu.PrefetchScalarGridSpec(num_scalar_...]
    convert_element_type x2 -> x0, other arithmetic: 8.97 us -> none  [the longest x1 4.52 us: shards(): params.astype(jnp.bfloat16)]
    ppermute x0 -> x4, starting transfers between devices: none -> 6.8 us  [the longest x1 3.74 us: shards(): got = lax.ppermute(outgoing, 'dp', SWAP)]
    reduce_sum x3 -> x1, other arithmetic: 5.68 us -> 1.21 us  [shards(): weight_part = jnp.sum(later_params * later_params).reshape(1, 1)]
  transfers between devices with their start and end apart: 2 -> 4, of which waited for: 1 -> 3; matrix products, arithmetic and copies ran while one was open for 5% -> 4% of each run, Pallas kernels for 0% -> 17%
where the time goes in v2:
time: 97.1 us; the launch traced here: 96.2 us
  blocking collectives  35.1 us (36%)
  waiting for transfers between devices  27.9 us (29%)
  Pallas kernels  19.5 us (20%)
  starting transfers between devices  6.8 us (7%)
  local copies, waits for them, and re-layouts  4.06 us (4%)
  other arithmetic  2.24 us (2%)
    ppermute x1, waiting for transfers between devices, shards(): got = lax.ppermute(outgoing, 'dp', SWAP)  21.9 us
    all_to_all x1, blocking collectives, shards(): parts = lax.all_to_all(sent, ('dp', 'row', 'col'), 0, 0)  20.7 us
    pallas_call x8, Pallas kernels, call(): pl.pallas_call(kernel, grid_spec=pltpu.PrefetchScalarGridSpec(num_scalar_...  19.5 us
    all_to_all x1, blocking collectives, shards(): col_parts = lax.all_to_all(sent, 'row', 0, 0)  14.3 us
    ppermute x1, waiting for transfers between devices, shards(): late = [lax.ppermute(out, 'dp', SWAP)]  5.23 us
    ppermute x1, starting transfers between devices, shards(): got = lax.ppermute(outgoing, 'dp', SWAP)  3.74 us
    dynamic_slice x1, local copies, waits for them, and re-layouts, shards(): outgoing = lax.dynamic_slice_in_dim(grad_parts[0], other * width, width, 1)  2.51 us
  transfers between devices with their start and end apart: 4, of which 3 were waited for; matrix products, arithmetic and copies ran while one was open for 4% of the time, Pallas kernels for 17%

profile of v2, /device:TPU:1, one launch (start us, length us, event | category | flops | bytes accessed | tf_op | source)
XLA Modules:
  0.0 96.2 jit_solution(1047223299940786996)
XLA Ops:
  0.6 0.0 copy-start
  0.6 0.0 copy-start.1
  0.7 2.5 %dynamic-slice_bitcast_fusion = bf16[128,4608]{1,0:T(8,128)(2,1)} fusion(bf16[1,128,9216]{2,1,0:T(8,128)(2,1)} %mine_ref.1, s32[]{:T(128)S(6)} %select_n.8), kind=kLoop, calls=%fused_computation.1 | loop fusion | bytes 2359300 | tf_op jit(solution)/shard_map/dynamic_slice | solution.py:219
  3.2 3.7 %collective-permute-start = (bf16[128,4608]{1,0:T(8,128)(2,1)}, bf16[128,4608]{1,0:T(8,128)(2,1)}, u32[]{:S(2)}, u32[]{:S(2)}) collective-permute-start(bf16[128,4608]{1,0:T(8,128)(2,1)} %dynamic-slice_bitcast_fusion), channel_id=1, source_target_pairs={{0,64},{64,0},{1,65},{65,1},{2,66},{66,2},{3,67},{67,3},{4,68},{68... | collective-permute-start | bytes 3538952 | tf_op jit(solution)/shard_map/ppermute | solution.py:220
  6.9 0.0 copy-done.1
  7.0 1.0 %constant_dynamic-slice_fusion = bf16[128,1536]{1,0:T(8,128)(2,1)S(1)} fusion(bf16[128,9216]{1,0:T(8,128)(2,1)} %bitcast.13, s32[]{:T(128)S(6)} %select_n.9), kind=kLoop, calls=%fused_computation.5 | loop fusion | bytes 786436 | tf_op jit(solution)/shard_map/dynamic_slice | solution.py:223
  8.0 1.0 %pad_maximum_fusion = bf16[128,3072]{1,0:T(8,128)(2,1)} fusion(bf16[128,1536]{1,0:T(8,128)(2,1)S(1)} %slice.7, bf16[128,1536]{1,0:T(8,128)(2,1)S(1)} %constant_dynamic-slice_fusion), kind=kLoop, calls=%fused_computation.3 | loop fusion | flops 1572864 | bytes 1572864 | tf_op jit(solution)/shard_map/concatenate | solution.py:224
  9.0 0.0 collective-permute-start.1
  9.0 0.0 copy-done
  9.0 0.0 copy-start.2
  9.0 0.1 dynamic-slice_bitcast_fusion.1.old_cols_ref
  9.1 1.2 %multiply_reduce_fusion = f32[]{:T(128)} fusion(f32[128,4608]{1,0:T(8,128)S(1)} %copy-done.1), kind=kLoop, calls=%fused_computation | loop fusion | flops 1179647 | bytes 2359300 | tf_op jit(solution)/shard_map/reduce_sum | solution.py:226
  10.3 0.1 pad_add_fusion.at_ref
  10.3 0.3 copy-done.2
  10.6 0.0 copy-start.3
  10.6 0.1 constant_dynamic-slice_fusion.1.mine_ref
  10.7 21.9 %collective-permute-done.got_ref = bf16[128,4608]{1,0:T(8,128)(2,1)} collective-permute-done((bf16[128,4608]{1,0:T(8,128)(2,1)}, bf16[128,4608]{1,0:T(8,128)(2,1)}, u32[]{:S(2)}, u32[]{:S(2)}) %collective-permute-start) | collective-permute-done | bytes 1179680 | tf_op jit(solution)/shard_map/ppermute | solution.py:220
  32.6 2.8 %shard_map.99 = (f32[128,4608]{1,0:T(8,128)S(1)}, f32[1,128]{1,0:T(1,128)S(1)}, bf16[16,48,128]{2,1,0:T(8,128)(2,1)S(1)}) custom-call(bf16[128,4608]{1,0:T(8,128)(2,1)S(1)} %constant_dynamic-slice_fusion.1.mine_ref, bf16[128,4608]{1,0:T(8,128)(2,1)} %collective-permute-done.got_ref), custom_call_target="tpu_custom_call" | custom-call | flops 4718592 | bytes 4718592 | tf_op jit(solution)/shard_map/pallas_call | solution.py:192
  35.4 14.3 %all_to_all.10.got_ref = bf16[16,48,128]{2,1,0:T(8,128)(2,1)S(1)} all-to-all(bf16[16,48,128]{2,1,0:T(8,128)(2,1)S(1)} %get-tuple-element.40), channel_id=1, replica_groups=mesh['dp'=2,'row'=16,'col'=4] {'row'}, dimensions={0} | all-to-all | bytes 393216 | tf_op jit(solution)/shard_map/all_to_all | solution.py:239
  49.8 0.0 copy-done.3
  49.8 1.9 %shard_map.100 = (f32[36,128]{1,0:T(8,128)}, f32[36,128]{1,0:T(8,128)S(1)}, f32[128,4,128]{2,1,0:T(4,128)S(1)}) custom-call(f32[128,4608]{1,0:T(8,128)S(1)} %get-tuple-element.39.grad_ref, bf16[16,48,128]{2,1,0:T(8,128)(2,1)S(1)} %all_to_all.10.got_ref, f32[1,128]{1,0:T(1,128)S(1)} %get-tuple-element.41.row_ref, f32[1,128]{1,0:T(1,128)S(1)} %bitcast.15, ...), custom_call_target="tpu_custom_call" | custom-call | flops 2359296 | bytes 2359296 | tf_op jit(solution)/shard_map/pallas_call | solution.py:192
  51.7 0.0 collective-permute-done.1.grad_ref.params_ref
  51.7 20.7 %all_to_all.11.got_ref = f32[128,4,128]{2,1,0:T(4,128)S(1)} all-to-all(f32[128,4,128]{2,1,0:T(4,128)S(1)} %get-tuple-element.45), channel_id=1, replica_groups=mesh['dp'=2,'row'=16,'col'=4] {'dp','row','col'}, dimensions={0} | all-to-all | bytes 524288 | tf_op jit(solution)/shard_map/all_to_all | solution.py:249
  72.4 1.9 %shard_map.101 = (bf16[128,2176]{1,0:T(8,128)(2,1)S(1)}, f32[1,128]{1,0:T(1,128)}, f32[1,1]{1,0:T(1,128)}, f32[1,1]{1,0:T(1,128)}, f32[1,1]{1,0:T(1,128)}, /*ind...) custom-call(s32[2]{0:T(128)S(1)} %pad_add_fusion.at_ref, f32[128,4,128]{2,1,0:T(4,128)S(1)} %all_to_all.11.got_ref, ...), custom_call_target="tpu_custom_call" | custom-call | flops 1048576 | bytes 1048576 | tf_op jit(solution)/shard_map/pallas_call | solution.py:192
  74.3 1.1 %collective-permute-start.3 = (bf16[128,2176]{1,0:T(8,128)(2,1)S(1)}, bf16[128,2176]{1,0:T(8,128)(2,1)S(1)}, u32[]{:S(2)}, u32[]{:S(2)}) collective-permute-start(bf16[128,2176]{1,0:T(8,128)(2,1)S(1)} %get-tuple-element.51), channel_id=1, source_target_pairs={{0,64},{64,0},{1,65},{65,1},{2,66},{66,2},{3,67},{67,3},{4,68},{68... | collective-permute-start | bytes 1671176 | tf_op jit(solution)/shard_map/ppermute | solution.py:260
  75.4 1.0 %shard_map.103 = bf16[128,1024]{1,0:T(8,128)(2,1)S(1)} custom-call(f32[128,4608]{1,0:T(8,128)S(1)} %get-tuple-element.39.grad_ref, f32[128,4608]{1,0:T(8,128)S(1)} %copy-done.1, f32[128,128]{1,0:T(8,128)S(1)} %get-tuple-element.47.row_scale, f32[36,128]{1,0:T(8,128)S(1)} %get-tuple-element.48.col_scale, f32[1,1]{1,0:T(1,128)} %get-tuple-element.49.step_ref), custom_call_target="tpu_custom_call" | custom-call | flops 524288 | bytes 524288 | tf_op jit(solution)/shard_map/pallas_call | solution.py:192
  76.4 1.9 %collective-permute-start.2 = (bf16[128,1024]{1,0:T(8,128)(2,1)S(1)}, bf16[128,1024]{1,0:T(8,128)(2,1)S(1)}, u32[]{:S(2)}, u32[]{:S(2)}) collective-permute-start(bf16[128,1024]{1,0:T(8,128)(2,1)S(1)} %shard_map.103), channel_id=1, source_target_pairs={{0,64},{64,0},{1,65},{65,1},{2,66},{66,2},{3,67},{67,3},{4,68},{68... | collective-permute-start | bytes 786440 | tf_op jit(solution)/shard_map/ppermute | solution.py:269
  78.3 5.7 %shard_map.102 = (f32[128,4608]{1,0:T(8,128)}, f32[128,4608]{1,0:T(8,128)}, bf16[128,9216]{1,0:T(8,128)(2,1)}) custom-call(s32[2]{0:T(128)S(1)} %pad_add_fusion.at_ref, f32[128,4608]{1,0:T(8,128)S(1)} %get-tuple-element.39.grad_ref, f32[128,4608]{1,0:T(8,128)S(1)} %copy-done.1, f32[128,128]{1,0:T(8,128)S(1)} %get-tuple-element.47.row_scale, ...), custom_call_target="tpu_custom_call" | custom-call | flops 10616832 | bytes 10616832 | tf_op jit(solution)/shard_map/pallas_call | solution.py:192
  84.1 5.2 %collective-permute-done.3.cols_ref.got_ref = bf16[128,2176]{1,0:T(8,128)(2,1)S(1)} collective-permute-done((bf16[128,2176]{1,0:T(8,128)(2,1)S(1)}, bf16[128,2176]{1,0:T(8,128)(2,1)S(1)}, u32[]{:S(2)}, u32[]{:S(2)}) %collective-permute-start.3) | collective-permute-done | bytes 557088 | tf_op jit(solution)/shard_map/ppermute | solution.py:260
  89.3 2.8 %shard_map.104._ = bf16[128,9216]{1,0:T(8,128)(2,1)} custom-call(s32[2]{0:T(128)S(1)} %pad_add_fusion.at_ref, bf16[1,128,9216]{2,1,0:T(8,128)(2,1)S(1)} %copy-done.2, bf16[128,3072]{1,0:T(8,128)(2,1)S(1)} %collective-permute-done.1.grad_ref.params_ref, ...), custom_call_target="tpu_custom_call", output_to_operand_aliasing={{}: (7, {})} | custom-call | flops 1572864 | bytes 1572864 | tf_op jit(solution)/shard_map/pallas_call | solution.py:192
  92.1 2.0 %shard_map.105._ = bf16[128,9216]{1,0:T(8,128)(2,1)} custom-call(s32[2]{0:T(128)S(1)} %pad_add_fusion.at_ref, bf16[128,2176]{1,0:T(8,128)(2,1)S(1)} %collective-permute-done.3.cols_ref.got_ref, bf16[128,9216]{1,0:T(8,128)(2,1)} %shard_map.104._), custom_call_target="tpu_custom_call", output_to_operand_aliasing={{}: (2, {})} | custom-call | flops 1048576 | bytes 1048576 | tf_op jit(solution)/shard_map/pallas_call | solution.py:192
  94.2 0.7 collective-permute-done.2.got_ref
  94.9 1.3 %shard_map.106 = bf16[128,9216]{1,0:T(8,128)(2,1)} custom-call(s32[2]{0:T(128)S(1)} %pad_add_fusion.at_ref, bf16[128,1024]{1,0:T(8,128)(2,1)S(1)} %collective-permute-done.2.got_ref, bf16[128,9216]{1,0:T(8,128)(2,1)} %shard_map.105._), custom_call_target="tpu_custom_call", output_to_operand_aliasing={{}: (2, {})} | custom-call | flops 524288 | bytes 524288 | tf_op jit(solution)/shard_map/pallas_call | solution.py:192
  (1 shorter events, 0.0 us)
Async XLA Ops:
  0.6 8.3 %copy-start = (f32[9216]{0:T(1024)S(1)}, f32[9216]{0:T(1024)}, u32[]{:S(2)}) copy-start(f32[9216]{0:T(1024)} %param.7) | copy-start | bytes 110596
  0.6 6.3 %copy-start.1 = (f32[128,4608]{1,0:T(8,128)S(1)}, f32[128,4608]{1,0:T(8,128)}, u32[]{:S(2)}) copy-start(f32[128,4608]{1,0:T(8,128)} %params_ref.5) | copy-start | bytes 7077892
  3.2 29.5 %collective-permute-start = (bf16[128,4608]{1,0:T(8,128)(2,1)}, bf16[128,4608]{1,0:T(8,128)(2,1)}, u32[]{:S(2)}, u32[]{:S(2)}) collective-permute-start(bf16[128,4608]{1,0:T(8,128)(2,1)} %dynamic-slice_bitcast_fusion), channel_id=1, source_target_pairs={{0,64},{64,0},{1,65},{65,1},{2,66},{66,2},{3,67},{67,3},{4,68},{68... | collective-permute-start | bytes 3538952 | tf_op jit(solution)/shard_map/ppermute | solution.py:220
  9.0 42.7 %collective-permute-start.1 = (bf16[128,3072]{1,0:T(8,128)(2,1)}, bf16[128,3072]{1,0:T(8,128)(2,1)S(1)}, u32[]{:S(2)}, u32[]{:S(2)}) collective-permute-start(bf16[128,3072]{1,0:T(8,128)(2,1)} %pad_maximum_fusion), channel_id=1, source_target_pairs={{0,64},{64,0},{1,65},{65,1},{2,66},{66,2},{3,67},{67,3},{4,68},{68... | collective-permute-start | bytes 2359304 | tf_op jit(solution)/shard_map/ppermute | solution.py:225
  9.0 1.7 %copy-start.2 = (bf16[1,128,9216]{2,1,0:T(8,128)(2,1)S(1)}, bf16[1,128,9216]{2,1,0:T(8,128)(2,1)}, u32[]{:S(2)}) copy-start(bf16[1,128,9216]{2,1,0:T(8,128)(2,1)} %mine_ref.1) | copy-start | bytes 7077892
  10.6 39.2 %copy-start.3 = (f32[128]{0:T(128)S(1)}, f32[128]{0:T(128)}, u32[]{:S(2)}) copy-start(f32[128]{0:T(128)} %param.6) | copy-start | bytes 1540
  74.3 15.0 %collective-permute-start.3 = (bf16[128,2176]{1,0:T(8,128)(2,1)S(1)}, bf16[128,2176]{1,0:T(8,128)(2,1)S(1)}, u32[]{:S(2)}, u32[]{:S(2)}) collective-permute-start(bf16[128,2176]{1,0:T(8,128)(2,1)S(1)} %get-tuple-element.51), channel_id=1, source_target_pairs={{0,64},{64,0},{1,65},{65,1},{2,66},{66,2},{3,67},{67,3},{4,68},{68... | collective-permute-start | bytes 1671176 | tf_op jit(solution)/shard_map/ppermute | solution.py:260
  76.4 18.5 %collective-permute-start.2 = (bf16[128,1024]{1,0:T(8,128)(2,1)S(1)}, bf16[128,1024]{1,0:T(8,128)(2,1)S(1)}, u32[]{:S(2)}, u32[]{:S(2)}) collective-permute-start(bf16[128,1024]{1,0:T(8,128)(2,1)S(1)} %shard_map.103), channel_id=1, source_target_pairs={{0,64},{64,0},{1,65},{65,1},{2,66},{66,2},{3,67},{67,3},{4,68},{68... | collective-permute-start | bytes 786440 | tf_op jit(solution)/shard_map/ppermute | solution.py:269

commit v3 on v0

v3 whole, which is shorter than its diff:
```python
import functools

import jax
import jax.numpy as jnp
from jax import lax
from jax.experimental import pallas as pl
from jax.experimental.pallas import tpu as pltpu
from jax.sharding import PartitionSpec as P

R = 2048
C = 36864
STEP = 10
DECAY = 1.0 - STEP ** (-0.8)
RELATIVE = min(0.01, STEP ** (-0.5))
LANES = 128
SWAP = [(0, 1), (1, 0)]
BLOCK = 512
WIDE = 1536
AHEAD = (3, 2)
EARLY = sum(AHEAD)
LATE = (2, 2)
VMEM_LIMIT = 24 << 20
f32, bf16 = jnp.float32, jnp.bfloat16
shape = jax.ShapeDtypeStruct


def down(row):
    return jnp.broadcast_to(row, (LANES, LANES)).T


def flat(acc):
    return jnp.sum(acc.T, axis=0, keepdims=True)


def tile(at):
    return slice(at * LANES, (at + 1) * LANES)


def span(start, count):
    return pl.ds(pl.multiple_of(start, LANES), count)


def begin(*copies):
    copies = [pltpu.make_async_copy(*copy) for copy in copies]
    for copy in copies:
        copy.start()
    return copies


def steps(width):
    return [(start, WIDE) for start in range(0, width, WIDE)]


def half_kernel(grad_ref, out_ref, buf, in_sems, out_sems):
    width = buf.shape[1]
    other = (1 - lax.axis_index("dp")) * width
    pieces = steps(width)
    ins = [
        begin((grad_ref.at[0, :, span(other + s, n)], buf.at[:, s : s + n], in_sems.at[i]))[0]
        for i, (s, n) in enumerate(pieces)
    ]
    outs = []
    for i, (s, n) in enumerate(pieces):
        ins[i].wait()
        outs += begin((buf.at[:, s : s + n], out_ref.at[:, s : s + n], out_sems.at[i]))
    for copy in outs:
        copy.wait()


def prepare_kernel(grad_ref, params_ref, _, *refs):
    ahead_refs, (weight_ref, params, parts, values, sems, out_sems) = refs[: len(AHEAD)], refs[len(AHEAD) :]
    width = params.shape[1]
    mine = lax.axis_index("dp") * width
    pieces = steps(width)
    ins = [
        begin((params_ref.at[:, s : s + n], params.at[:, s : s + n], sems.at[i]))[0] for i, (s, n) in enumerate(pieces)
    ]
    grad = begin((grad_ref.at[0, :, span(mine, EARLY * BLOCK)], parts, sems.at[len(pieces)]))[0]
    acc = jnp.zeros((LANES, LANES), f32)
    for i, (s, n) in enumerate(pieces):
        ins[i].wait()
        for t in range(s // LANES, (s + n) // LANES):
            value = params[:, tile(t)]
            acc = acc + value * value
            if t < EARLY * BLOCK // LANES:
                values[:, tile(t)] = value.astype(bf16)
    grad.wait()
    outs, start = [], 0
    for i, (count, ahead_ref) in enumerate(zip(AHEAD, ahead_refs)):
        n = count * BLOCK
        outs += begin(
            (parts.at[:, start : start + n], ahead_ref.at[:, 0:n], out_sems.at[2 * i]),
            (values.at[:, start : start + n], ahead_ref.at[:, n : 2 * n], out_sems.at[2 * i + 1]),
        )
        start += n
    weight_ref[...] = jnp.sum(jnp.sum(acc, axis=0, keepdims=True), axis=1, keepdims=True)
    for copy in outs:
        copy.wait()


def sums_kernel(grad_parts_ref, got_ref, _, grad_ref, row_ref, sent_ref, mine, got, grad, cols, sems, out_sems):
    width = grad.shape[1]
    first = lax.axis_index("dp") * width
    pieces = steps(width)
    ins = [
        begin(
            (grad_parts_ref.at[0, :, span(first + s, n)], mine.at[:, s : s + n], sems.at[2 * i]),
            (got_ref.at[:, s : s + n], got.at[:, s : s + n], sems.at[2 * i + 1]),
        )
        for i, (s, n) in enumerate(pieces)
    ]
    cols[...] = jnp.zeros_like(cols)
    acc = jnp.zeros((LANES, LANES), f32)
    outs = []
    for i, (s, n) in enumerate(pieces):
        for copy in ins[i]:
            copy.wait()
        for t in range(s // LANES, (s + n) // LANES):
            g = mine[:, tile(t)].astype(f32) + got[:, tile(t)].astype(f32)
            grad[:, tile(t)] = g
            squares = g * g + 1e-30
            acc = acc + squares
            cols[t : t + 1, :] = jnp.sum(squares, axis=0, keepdims=True)
        outs += begin((grad.at[:, s : s + n], grad_ref.at[:, s : s + n], out_sems.at[i]))
    row_ref[...] = flat(acc)
    sent = cols[...].astype(bf16)
    for peer in range(sent_ref.shape[0]):
        sent_ref[peer] = sent
    for copy in outs:
        copy.wait()


def moments_kernel(
    grad_ref, got_ref, row_ref, old_rows_ref, old_cols_ref, weight_ref,
    new_cols_ref, copy_ref, sent_ref, grad, inv_cols, sent, sems, out_sem,
):
    width = grad.shape[1]
    height = width // LANES
    pieces = steps(width)
    ins = [begin((grad_ref.at[:, s : s + n], grad.at[:, s : s + n], sems.at[i]))[0] for i, (s, n) in enumerate(pieces)]
    totals = got_ref[0].astype(f32)
    for peer in range(1, got_ref.shape[0]):
        totals = totals + got_ref[peer].astype(f32)
    old_cols = jnp.where(lax.axis_index("dp") == 0, old_cols_ref[:height], old_cols_ref[height:])
    new_cols = DECAY * old_cols + (1.0 - DECAY) * (totals[:height] / R)
    new_cols_ref[...] = new_cols
    copy_ref[...] = new_cols
    inv_cols[...] = 1.0 / new_cols
    acc = jnp.zeros((LANES, LANES), f32)
    for i, (s, n) in enumerate(pieces):
        ins[i].wait()
        for t in range(s // LANES, (s + n) // LANES):
            g = grad[:, tile(t)]
            acc = acc + g * g * inv_cols[t : t + 1, :]
    at = lax.broadcasted_iota(jnp.int32, (4, LANES), 0)
    value = jnp.zeros((4, LANES), f32)
    for i, row in enumerate([row_ref[...], flat(acc), old_rows_ref[...], weight_ref[...]]):
        value = jnp.where(at == i, jnp.broadcast_to(row, (4, LANES)), value)
    sent[...] = jnp.broadcast_to(value[None], sent.shape)
    (copy,) = begin((sent, sent_ref, out_sem))
    copy.wait()


def weights_piece(grad, params, out_ref, row_scale, col_scale, step_size, first):
    for t in range(grad.shape[1] // LANES):
        update = grad[:, tile(t)] * row_scale * col_scale[first + t : first + t + 1, :]
        out_ref[:, tile(t)] = (params[:, tile(t)] - step_size * update).astype(bf16)


def first_weights_kernel(
    got_ref, cols_ref, grad_ref, params_ref,
    out_ref, rows_ref, clip_ref, scale_ref, step_ref, row_scale, col_scale, grad, params, all_rows, sems,
):
    start, count = EARLY * BLOCK, grad.shape[1]
    ins = begin(
        (grad_ref.at[:, start : start + count], grad, sems.at[0]),
        (params_ref.at[:, start : start + count], params, sems.at[1]),
    )
    update_sum = jnp.zeros((1, LANES), f32)
    row_sum = jnp.zeros((1, LANES), f32)
    weight_sum = jnp.zeros((1, LANES), f32)
    for block in range(16):
        got = None
        for d in range(2):
            for c in range(4):
                term = got_ref[d * 64 + block * 4 + c]
                got = term if got is None else got + term
        rows = DECAY * got_ref[block * 4][2:3] + (1.0 - DECAY) * (got[0:1] / C)
        all_rows[block : block + 1, :] = rows
        update_sum = update_sum + got[1:2] / rows
        row_sum = row_sum + rows
        weight_sum = weight_sum + got[3:4]
    row_mean = jnp.sum(row_sum, axis=1, keepdims=True) / R
    rows = all_rows[pl.ds(lax.axis_index("row"), 1), :]
    rows_ref[...] = rows
    row_scale[...] = down(lax.rsqrt(rows / row_mean))
    col_scale[...] = lax.rsqrt(cols_ref[...])
    update_mean = jnp.sum(update_sum, axis=1, keepdims=True) * row_mean / (R * C)
    weight_mean = weight_sum[:, :1] / (R * C)
    clip_factor = jnp.maximum(1.0, jnp.sqrt(update_mean))
    param_scale = jnp.maximum(0.001, jnp.sqrt(weight_mean))
    clip_ref[...] = clip_factor
    scale_ref[...] = param_scale
    step_size = RELATIVE * param_scale / clip_factor
    step_ref[...] = step_size
    scale = jnp.zeros((LANES, LANES), f32)
    at = lax.broadcasted_iota(jnp.int32, scale.shape, 0)
    for t in range(EARLY * BLOCK // LANES):
        scale = jnp.where(at == t, jnp.broadcast_to(col_scale[t : t + 1, :], scale.shape), scale)
    out_ref[:, count : count + LANES] = scale.astype(bf16)
    for copy in ins:
        copy.wait()
    weights_piece(grad, params, out_ref, row_scale[...], col_scale, step_size, start // LANES)


def weights_kernel(start, grad_ref, params_ref, row_scale, col_scale, step_ref, out_ref, grad, params, sems):
    count = grad.shape[1]
    ins = begin(
        (grad_ref.at[:, start : start + count], grad, sems.at[0]),
        (params_ref.at[:, start : start + count], params, sems.at[1]),
    )
    for copy in ins:
        copy.wait()
    weights_piece(grad, params, out_ref, row_scale[...], col_scale, step_ref[...], start // LANES)


def params_kernel(
    grad_ref, params_ref, row_scale, col_scale, step_ref,
    new_ref, update_ref, weights_ref, grad, params, update, new, weights, sems, out_sems,
):
    width = grad.shape[1]
    mine = lax.axis_index("dp") * width
    pieces = steps(width)
    ins = [
        begin(
            (grad_ref.at[:, s : s + n], grad.at[:, s : s + n], sems.at[2 * i]),
            (params_ref.at[:, s : s + n], params.at[:, s : s + n], sems.at[2 * i + 1]),
        )
        for i, (s, n) in enumerate(pieces)
    ]
    across, step_size = row_scale[...], step_ref[...]
    outs = []
    for i, (s, n) in enumerate(pieces):
        for copy in ins[i]:
            copy.wait()
        for t in range(s // LANES, (s + n) // LANES):
            value = grad[:, tile(t)] * across * col_scale[t : t + 1, :]
            moved = params[:, tile(t)] - step_size * value
            update[:, tile(t)] = value
            new[:, tile(t)] = moved
            weights[:, tile(t)] = moved.astype(bf16)
        outs += begin(
            (update.at[:, s : s + n], update_ref.at[:, s : s + n], out_sems.at[3 * i]),
            (new.at[:, s : s + n], new_ref.at[:, s : s + n], out_sems.at[3 * i + 1]),
            (weights.at[:, s : s + n], weights_ref.at[:, span(mine + s, n)], out_sems.at[3 * i + 2]),
        )
    for copy in outs:
        copy.wait()


def early_kernel(start, width, grad_ref, ahead_ref, row_scale, late_ref, step_ref, _, out_ref,
                 mine, got, scale, out, scales, sems, out_sem):
    count = mine.shape[1]
    first = (1 - lax.axis_index("dp")) * width + start
    ins = begin(
        (late_ref.at[:, LATE[0] * BLOCK : LATE[0] * BLOCK + LANES], scale, sems.at[0]),
        (grad_ref.at[0, :, span(first, count)], mine, sems.at[1]),
        (ahead_ref, got, sems.at[2]),
    )
    across, step_size = row_scale[...], step_ref[...]
    for copy in ins:
        copy.wait()
    scales[...] = scale[...].astype(f32)
    for t in range(count // LANES):
        g = mine[:, tile(t)].astype(f32) + got[:, tile(t)].astype(f32)
        at = start // LANES + t
        update = g * across * scales[at : at + 1, :]
        out[:, tile(t)] = (got[:, tile(count // LANES + t)].astype(f32) - step_size * update).astype(bf16)
    (copy,) = begin((out, out_ref.at[:, span(first, count)], out_sem))
    copy.wait()


def place_kernel(start, width, got_ref, _, out_ref, got, sems):
    first = (1 - lax.axis_index("dp")) * width + start
    count = got.shape[1]
    (copy,) = begin((got_ref.at[:, 0:count], got, sems.at[0]))
    copy.wait()
    (copy,) = begin((got, out_ref.at[:, span(first, count)], sems.at[1]))
    copy.wait()


HBM, VMEM = pltpu.HBM, pltpu.VMEM
dma = pltpu.SemaphoreType.DMA


def call(kernel, ins, outs, scratch, args, nbytes, aliases=None):
    return pl.pallas_call(
        kernel,
        in_specs=[pl.BlockSpec(memory_space=space) for space in ins],
        out_specs=[pl.BlockSpec(memory_space=space) for space, _ in outs],
        out_shape=[out for _, out in outs],
        scratch_shapes=list(scratch),
        input_output_aliases=aliases or {},
        cost_estimate=pl.CostEstimate(flops=nbytes, bytes_accessed=nbytes, transcendentals=0),
        compiler_params=pltpu.CompilerParams(vmem_limit_bytes=VMEM_LIMIT),
    )(*args)


def shards(params, grad_parts, row_moment, col_moment):
    rows, width = params.shape
    height = width // LANES
    padded = -(-height // 16) * 16
    early = EARLY * BLOCK
    count = len(steps(width))

    (outgoing,) = call(
        half_kernel, [HBM], [(HBM, shape((rows, width), bf16))],
        [VMEM((rows, width), bf16), dma((count,)), dma((count,))], (grad_parts,), 4 * rows * width,
    )
    got = lax.ppermute(outgoing, "dp", SWAP)
    *ahead, weight_part = call(
        prepare_kernel, [HBM, HBM, HBM],
        [(HBM, shape((rows, 2 * n * BLOCK), bf16)) for n in AHEAD] + [(VMEM, shape((1, 1), f32))],
        [VMEM((rows, width), f32), VMEM((rows, early), bf16), VMEM((rows, early), bf16), dma((count + 1,)),
         dma((2 * len(AHEAD),))],
        (grad_parts, params, outgoing), 4 * rows * (width + early),
    )
    arrived = [lax.ppermute(ahead[0], "dp", SWAP)]

    gradient, row_part, sent = call(
        sums_kernel, [HBM, HBM, VMEM],
        [(HBM, shape((rows, width), f32)), (VMEM, shape((1, rows), f32)),
         (VMEM, shape((16, padded, LANES), bf16))],
        [VMEM((rows, width), bf16), VMEM((rows, width), bf16), VMEM((rows, width), f32), VMEM((padded, LANES), f32),
         dma((2 * count,)), dma((count,))],
        (grad_parts, got, weight_part), 8 * rows * width,
    )
    col_parts = lax.all_to_all(sent, "row", 0, 0)
    new_cols, cols_copy, sent = call(
        moments_kernel, [HBM] + [VMEM] * 5,
        [(VMEM, shape((height, LANES), f32)), (VMEM, shape((height, LANES), f32)),
         (HBM, shape((128, 4, LANES), f32))],
        [VMEM((rows, width), f32), VMEM((height, LANES), f32), VMEM((128, 4, LANES), f32), dma((count,)), dma],
        (gradient, col_parts, row_part, row_moment.reshape(1, rows), col_moment.reshape(2 * height, LANES), weight_part),
        4 * rows * width,
    )
    sent, arrived[0], *ahead = lax.optimization_barrier((sent, arrived[0], *ahead))
    parts = lax.all_to_all(sent, ("dp", "row", "col"), 0, 0)
    arrived += [lax.ppermute(values, "dp", SWAP) for values in ahead[1:]]

    n = LATE[0] * BLOCK
    out, new_rows, clip_factor, param_scale, step_size, row_scale, col_scale = call(
        first_weights_kernel, [VMEM, VMEM, HBM, HBM],
        [(VMEM, shape((rows, n + LANES), bf16)), (VMEM, shape((1, rows), f32)),
         (VMEM, shape((1, 1), f32)), (VMEM, shape((1, 1), f32)), (VMEM, shape((1, 1), f32)),
         (VMEM, shape((rows, LANES), f32)), (VMEM, shape((height, LANES), f32))],
        [VMEM((rows, n), f32), VMEM((rows, n), f32), VMEM((16, LANES), f32), dma((2,))],
        (parts, cols_copy, gradient, params), 8 * rows * n,
    )
    late = [lax.ppermute(out, "dp", SWAP)]
    start = early + n
    for blocks in LATE[1:]:
        n = blocks * BLOCK
        (out,) = call(
            functools.partial(weights_kernel, start), [HBM, HBM, VMEM, VMEM, VMEM],
            [(VMEM, shape((rows, n), bf16))], [VMEM((rows, n), f32), VMEM((rows, n), f32), dma((2,))],
            (gradient, params, row_scale, col_scale, step_size), 8 * rows * n,
        )
        late.append(lax.ppermute(out, "dp", SWAP))
        start += n

    out_shape = shape((rows, 2 * width), bf16)
    new_params, update, new_weights = call(
        params_kernel, [HBM, HBM, VMEM, VMEM, VMEM],
        [(HBM, shape((rows, width), f32)), (HBM, shape((rows, width), f32)), (HBM, out_shape)],
        [VMEM((rows, width), f32)] * 4 + [VMEM((rows, width), bf16), dma((2 * count,)), dma((3 * count,))],
        (gradient, params, row_scale, col_scale, step_size), 18 * rows * width,
    )
    start = 0
    for blocks, values in zip(AHEAD, arrived):
        n = blocks * BLOCK
        (new_weights,) = call(
            functools.partial(early_kernel, start, width), [HBM, HBM, VMEM, HBM, VMEM, HBM], [(HBM, out_shape)],
            [VMEM((rows, n), bf16), VMEM((rows, 2 * n), bf16), VMEM((rows, LANES), bf16), VMEM((rows, n), bf16),
             VMEM((rows, LANES), f32), dma((3,)), dma],
            (grad_parts, values, row_scale, late[0], step_size, new_weights), 8 * rows * n, {5: 0},
        )
        start += n
    for blocks, values in zip(LATE, late):
        n = blocks * BLOCK
        (new_weights,) = call(
            functools.partial(place_kernel, start, width), [HBM, HBM], [(HBM, out_shape)],
            [VMEM((rows, n), bf16), dma((2,))], (values, new_weights), 4 * rows * n, {1: 0},
        )
        start += n
    return (
        new_params, new_weights, new_rows.reshape(rows), new_cols.reshape(width), update,
        clip_factor.reshape(()), param_scale.reshape(()),
    )


def solution(mesh):
    in_specs = (P("row", ("col", "dp")), P("dp", "row", "col"), P("row"), P("col"))
    out_specs = (
        P("row", ("col", "dp")),
        P("row", "col"),
        P("row"),
        P(("col", "dp")),
        P("row", ("col", "dp")),
        P(),
        P(),
    )
    return jax.shard_map(shards, mesh=mesh, in_specs=in_specs, out_specs=out_specs, check_vma=False)
```

time: 296 us -> 91.1 us (0.31)
  blocking collectives: 179 us -> 14.3 us
  waiting for transfers between devices: 78.6 us -> 32.4 us
  starting transfers between devices: 0.08 us -> 21.2 us
  between operations: 18.4 us -> 0.77 us
  other arithmetic: 17.3 us -> 0 us
  Pallas kernels: 0 us -> 16.7 us
    psum x4 -> x0, blocking collectives: 179 us -> none  [the longest x1 84 us: shards(): lax.psum((jnp.sum(update_part * update_part), weight_local), ('dp', 'row'...]
    psum x1 -> x0, waiting for transfers between devices: 77.9 us -> none  [shards(): lax.psum(partial_value.astype(jnp.bfloat16), 'dp').astype(jnp.float32)]
    ppermute x0 -> x5, waiting for transfers between devices: none -> 24.4 us  [the longest x1 22.1 us: shards(): got = lax.ppermute(outgoing, 'dp', SWAP)]
    pallas_call x0 -> x11, Pallas kernels: none -> 16.7 us  [call(): pl.pallas_call(kernel, in_specs=[pl.BlockSpec(memory_space=space) for spa...]
    all_to_all x0 -> x1, blocking collectives: none -> 14.3 us  [shards(): col_parts = lax.all_to_all(sent, 'row', 0, 0)]
    ppermute x0 -> x5, starting transfers between devices: none -> 11.2 us  [the longest x1 3.82 us: shards(): got = lax.ppermute(outgoing, 'dp', SWAP)]
    all_to_all x0 -> x1, starting transfers between devices: none -> 9.95 us  [shards(): parts = lax.all_to_all(sent, ('dp', 'row', 'col'), 0, 0)]
    convert_element_type x2 -> x0, other arithmetic: 8.97 us -> none  [the longest x1 4.52 us: shards(): params.astype(jnp.bfloat16)]
  transfers between devices with their start and end apart: 2 -> 6, of which waited for: 1 -> 4; matrix products, arithmetic and copies ran while one was open for 5% -> 0% of each run, Pallas kernels for 0% -> 17%
where the time goes in v3:
time: 91.1 us; the launch traced here: 90.2 us
  waiting for transfers between devices  32.4 us (36%)
  starting transfers between devices  21.2 us (23%)
  Pallas kernels  16.7 us (18%)
  blocking collectives  14.3 us (16%)
  local copies, waits for them, and re-layouts  4.83 us (5%)
    ppermute x1, waiting for transfers between devices, shards(): got = lax.ppermute(outgoing, 'dp', SWAP)  22.1 us
    pallas_call x11, Pallas kernels, call(): pl.pallas_call(kernel, in_specs=[pl.BlockSpec(memory_space=space) for spa...  16.7 us
    all_to_all x1, blocking collectives, shards(): col_parts = lax.all_to_all(sent, 'row', 0, 0)  14.3 us
    all_to_all x1, starting transfers between devices, shards(): parts = lax.all_to_all(sent, ('dp', 'row', 'col'), 0, 0)  9.95 us
    all_to_all x1, waiting for transfers between devices, shards(): parts = lax.all_to_all(sent, ('dp', 'row', 'col'), 0, 0)  8.03 us
    unnamed x16, local copies, waits for them, and re-layouts  4.83 us
    ppermute x1, starting transfers between devices, shards(): got = lax.ppermute(outgoing, 'dp', SWAP)  3.82 us
    ppermute x1, starting transfers between devices, shards(): arrived += [lax.ppermute(values, 'dp', SWAP) for values in ahead[1:]]  2.98 us
  transfers between devices with their start and end apart: 6, of which 4 were waited for; matrix products, arithmetic and copies ran while one was open for 0% of the time, Pallas kernels for 17%

profile of v3, /device:TPU:1, one launch (start us, length us, event | category | flops | bytes accessed | tf_op | source)
XLA Modules:
  0.0 90.2 jit_solution(16229768007699656603)
XLA Ops:
  0.6 0.0 copy-start
  0.6 1.7 %copy-done = bf16[1,128,9216]{2,1,0:T(8,128)(2,1)S(1)} copy-done((bf16[1,128,9216]{2,1,0:T(8,128)(2,1)S(1)}, bf16[1,128,9216]{2,1,0:T(8,128)(2,1)}, u32[]{:S(2)}) %copy-start) | copy-done | bytes 2359320
  2.3 0.0 copy-start.2
  2.3 0.3 shard_map.99._
  2.6 3.8 %collective-permute-start = (bf16[128,4608]{1,0:T(8,128)(2,1)S(1)}, bf16[128,4608]{1,0:T(8,128)(2,1)S(1)}, u32[]{:S(2)}, u32[]{:S(2)}) collective-permute-start(bf16[128,4608]{1,0:T(8,128)(2,1)S(1)} %shard_map.99._), channel_id=1, source_target_pairs={{0,64},{64,0},{1,65},{65,1},{2,66},{66,2},{3,67},{67,3},{4,68},{68... | collective-permute-start | bytes 3538952 | tf_op jit(solution)/shard_map/ppermute | solution.py:320
  6.4 0.0 copy-done.2
  6.4 1.2 %shard_map.100 = (bf16[128,3072]{1,0:T(8,128)(2,1)S(1)}, bf16[128,2048]{1,0:T(8,128)(2,1)S(1)}, f32[1,1]{1,0:T(1,128)}) custom-call(bf16[1,128,9216]{2,1,0:T(8,128)(2,1)S(1)} %copy-done, f32[128,4608]{1,0:T(8,128)S(1)} %copy-done.2, bf16[128,4608]{1,0:T(8,128)(2,1)S(1)} %shard_map.99._), custom_call_target="tpu_custom_call" | custom-call | flops 3670016 | bytes 3670016 | tf_op jit(solution)/shard_map/pallas_call | solution.py:297
  7.6 0.0 copy-start.7
  7.6 0.8 copy-done.7
  8.4 0.0 copy-start.5
  8.4 0.0 copy-start.6
  8.4 1.3 %collective-permute-start.1 = (bf16[128,3072]{1,0:T(8,128)(2,1)S(1)}, bf16[128,3072]{1,0:T(8,128)(2,1)S(1)}, u32[]{:S(2)}, u32[]{:S(2)}) collective-permute-start(bf16[128,3072]{1,0:T(8,128)(2,1)S(1)} %get-tuple-element.34), channel_id=1, source_target_pairs={{0,64},{64,0},{1,65},{65,1},{2,66},{66,2},{3,67},{67,3},{4,68},{68... | collective-permute-start | bytes 2359304 | tf_op jit(solution)/shard_map/ppermute | solution.py:328
  9.7 22.1 %collective-permute-done.got_ref = bf16[128,4608]{1,0:T(8,128)(2,1)S(1)} collective-permute-done((bf16[128,4608]{1,0:T(8,128)(2,1)S(1)}, bf16[128,4608]{1,0:T(8,128)(2,1)S(1)}, u32[]{:S(2)}, u32[]{:S(2)}) %collective-permute-start) | collective-permute-done | bytes 1179680 | tf_op jit(solution)/shard_map/ppermute | solution.py:320
  31.8 1.8 %shard_map.101 = (f32[128,4608]{1,0:T(8,128)S(1)}, f32[1,128]{1,0:T(1,128)S(1)}, bf16[16,48,128]{2,1,0:T(8,128)(2,1)S(1)}) custom-call(bf16[1,128,9216]{2,1,0:T(8,128)(2,1)S(1)} %copy-done, bf16[128,4608]{1,0:T(8,128)(2,1)S(1)} %collective-permute-done.got_ref, f32[1,1]{1,0:T(1,128)} %get-tuple-element.29._.weight_ref), custom_call_target="tpu_custom_call" | custom-call | flops 4718592 | bytes 4718592 | tf_op jit(solution)/shard_map/pallas_call | solution.py:297
  33.6 14.3 %all_to_all.10.got_ref = bf16[16,48,128]{2,1,0:T(8,128)(2,1)S(1)} all-to-all(bf16[16,48,128]{2,1,0:T(8,128)(2,1)S(1)} %get-tuple-element.31), channel_id=1, replica_groups=mesh['dp'=2,'row'=16,'col'=4] {'row'}, dimensions={0} | all-to-all | bytes 393216 | tf_op jit(solution)/shard_map/all_to_all | solution.py:338
  48.0 0.0 copy-done.5
  48.0 0.0 copy-done.6
  48.0 1.9 %shard_map.102 = (f32[36,128]{1,0:T(8,128)}, f32[36,128]{1,0:T(8,128)S(1)}, f32[128,4,128]{2,1,0:T(4,128)S(1)}) custom-call(f32[128,4608]{1,0:T(8,128)S(1)} %get-tuple-element.30.grad_ref, bf16[16,48,128]{2,1,0:T(8,128)(2,1)S(1)} %all_to_all.10.got_ref, f32[1,128]{1,0:T(1,128)S(1)} %get-tuple-element.32.row_ref, f32[1,128]{1,0:T(1,128)S(1)} %bitcast.7, ...), custom_call_target="tpu_custom_call" | custom-call | flops 2359296 | bytes 2359296 | tf_op jit(solution)/shard_map/pallas_call | solution.py:297
  49.8 0.0 copy-start.4
  49.8 0.7 copy-done.4
  50.5 0.0 collective-permute-done.1.ahead_ref
  50.5 9.9 %all-to-all-start.1 = ((f32[128,4,128]{2,1,0:T(4,128)}), f32[128,4,128]{2,1,0:T(4,128)S(1)}, u32[]{:S(2)}, u32[]{:S(2)}) async-start(f32[128,4,128]{2,1,0:T(4,128)} %copy-done.4), calls=%async_computation.1 | async-start | bytes 524288 | tf_op jit(solution)/shard_map/all_to_all | solution.py:348
  60.5 3.0 %collective-permute-start.4 = (bf16[128,2048]{1,0:T(8,128)(2,1)}, bf16[128,2048]{1,0:T(8,128)(2,1)}, u32[]{:S(2)}, u32[]{:S(2)}) collective-permute-start(bf16[128,2048]{1,0:T(8,128)(2,1)} %copy-done.7), channel_id=1, source_target_pairs={{0,64},{64,0},{1,65},{65,1},{2,66},{66,2},{3,67},{67,3},{4,68},{68... | collective-permute-start | bytes 1572872 | tf_op jit(solution)/shard_map/ppermute | solution.py:349
  63.5 8.0 %all-to-all-done.1.got_ref = f32[128,4,128]{2,1,0:T(4,128)S(1)} async-done(((f32[128,4,128]{2,1,0:T(4,128)}), f32[128,4,128]{2,1,0:T(4,128)S(1)}, u32[]{:S(2)}, u32[]{:S(2)}) %all-to-all-start.1) | async-done | bytes 262176 | tf_op jit(solution)/shard_map/all_to_all | solution.py:348
  71.5 0.0 copy-start.3
  71.5 1.7 %copy-done.3 = f32[128,4608]{1,0:T(8,128)S(1)} copy-done((f32[128,4608]{1,0:T(8,128)S(1)}, f32[128,4608]{1,0:T(8,128)}, u32[]{:S(2)}) %copy-start.3) | copy-done | bytes 2359320
  73.2 0.9 shard_map.103
  74.1 1.1 %collective-permute-start.3 = (bf16[128,1152]{1,0:T(8,128)(2,1)S(1)}, bf16[128,1152]{1,0:T(8,128)(2,1)S(1)}, u32[]{:S(2)}, u32[]{:S(2)}) collective-permute-start(bf16[128,1152]{1,0:T(8,128)(2,1)S(1)} %get-tuple-element.42), channel_id=1, source_target_pairs={{0,64},{64,0},{1,65},{65,1},{2,66},{66,2},{3,67},{67,3},{4,68},{68... | collective-permute-start | bytes 884744 | tf_op jit(solution)/shard_map/ppermute | solution.py:360
  75.2 0.9 shard_map.105
  76.0 0.0 copy-start.1
  76.1 2.0 %collective-permute-start.2 = (bf16[128,1024]{1,0:T(8,128)(2,1)S(1)}, bf16[128,1024]{1,0:T(8,128)(2,1)S(1)}, u32[]{:S(2)}, u32[]{:S(2)}) collective-permute-start(bf16[128,1024]{1,0:T(8,128)(2,1)S(1)} %shard_map.105), channel_id=1, source_target_pairs={{0,64},{64,0},{1,65},{65,1},{2,66},{66,2},{3,67},{67,3},{4,68},{68... | collective-permute-start | bytes 786440 | tf_op jit(solution)/shard_map/ppermute | solution.py:369
  78.1 3.9 %shard_map.104 = (f32[128,4608]{1,0:T(8,128)}, f32[128,4608]{1,0:T(8,128)}, bf16[128,9216]{1,0:T(8,128)(2,1)}) custom-call(f32[128,4608]{1,0:T(8,128)S(1)} %get-tuple-element.30.grad_ref, f32[128,4608]{1,0:T(8,128)S(1)} %copy-done.3, f32[128,128]{1,0:T(8,128)S(1)} %get-tuple-element.38.row_scale, f32[36,128]{1,0:T(8,128)S(1)} %get-tuple-element.39.col_scale, ...), custom_call_target="tpu_custom_call" | custom-call | flops 10616832 | bytes 10616832 | tf_op jit(solution)/shard_map/pallas_call | solution.py:297
  81.9 1.9 %collective-permute-done.3.late_ref.got_ref = bf16[128,1152]{1,0:T(8,128)(2,1)S(1)} collective-permute-done((bf16[128,1152]{1,0:T(8,128)(2,1)S(1)}, bf16[128,1152]{1,0:T(8,128)(2,1)S(1)}, u32[]{:S(2)}, u32[]{:S(2)}) %collective-permute-start.3) | collective-permute-done | bytes 294944 | tf_op jit(solution)/shard_map/ppermute | solution.py:360
  83.9 0.0 copy-done.1
  83.9 1.8 %shard_map.106._ = bf16[128,9216]{1,0:T(8,128)(2,1)} custom-call(bf16[1,128,9216]{2,1,0:T(8,128)(2,1)S(1)} %copy-done.1, bf16[128,3072]{1,0:T(8,128)(2,1)S(1)} %collective-permute-done.1.ahead_ref, f32[128,128]{1,0:T(8,128)S(1)} %get-tuple-element.38.row_scale, ...), custom_call_target="tpu_custom_call", output_to_operand_aliasing={{}: (5, {})} | custom-call | flops 1572864 | bytes 1572864 | tf_op jit(solution)/shard_map/pallas_call | solution.py:297
  85.7 0.0 collective-permute-done.4.ahead_ref
  85.7 2.7 %shard_map.107._ = bf16[128,9216]{1,0:T(8,128)(2,1)} custom-call(bf16[1,128,9216]{2,1,0:T(8,128)(2,1)S(1)} %copy-done.1, bf16[128,2048]{1,0:T(8,128)(2,1)} %collective-permute-done.4.ahead_ref, f32[128,128]{1,0:T(8,128)S(1)} %get-tuple-element.38.row_scale, ...), custom_call_target="tpu_custom_call", output_to_operand_aliasing={{}: (5, {})} | custom-call | flops 1048576 | bytes 1048576 | tf_op jit(solution)/shard_map/pallas_call | solution.py:297
  88.4 0.8 shard_map.108._
  89.1 0.4 collective-permute-done.2.got_ref
  89.5 0.7 shard_map.109
Async XLA Ops:
  0.6 1.7 %copy-start = (bf16[1,128,9216]{2,1,0:T(8,128)(2,1)S(1)}, bf16[1,128,9216]{2,1,0:T(8,128)(2,1)}, u32[]{:S(2)}) copy-start(bf16[1,128,9216]{2,1,0:T(8,128)(2,1)} %grad_ref.7) | copy-start | bytes 7077892
  2.3 4.1 %copy-start.2 = (f32[128,4608]{1,0:T(8,128)S(1)}, f32[128,4608]{1,0:T(8,128)}, u32[]{:S(2)}) copy-start(f32[128,4608]{1,0:T(8,128)} %params_ref.7) | copy-start | bytes 7077892
  2.6 29.2 %collective-permute-start = (bf16[128,4608]{1,0:T(8,128)(2,1)S(1)}, bf16[128,4608]{1,0:T(8,128)(2,1)S(1)}, u32[]{:S(2)}, u32[]{:S(2)}) collective-permute-start(bf16[128,4608]{1,0:T(8,128)(2,1)S(1)} %shard_map.99._), channel_id=1, source_target_pairs={{0,64},{64,0},{1,65},{65,1},{2,66},{66,2},{3,67},{67,3},{4,68},{68... | collective-permute-start | bytes 3538952 | tf_op jit(solution)/shard_map/ppermute | solution.py:320
  7.6 0.8 copy-start.7
  8.4 39.5 %copy-start.5 = (f32[9216]{0:T(1024)S(1)}, f32[9216]{0:T(1024)}, u32[]{:S(2)}) copy-start(f32[9216]{0:T(1024)} %param.7) | copy-start | bytes 110596
  8.4 39.5 %copy-start.6 = (f32[128]{0:T(128)S(1)}, f32[128]{0:T(128)}, u32[]{:S(2)}) copy-start(f32[128]{0:T(128)} %param.6) | copy-start | bytes 1540
  8.4 42.1 %collective-permute-start.1 = (bf16[128,3072]{1,0:T(8,128)(2,1)S(1)}, bf16[128,3072]{1,0:T(8,128)(2,1)S(1)}, u32[]{:S(2)}, u32[]{:S(2)}) collective-permute-start(bf16[128,3072]{1,0:T(8,128)(2,1)S(1)} %get-tuple-element.34), channel_id=1, source_target_pairs={{0,64},{64,0},{1,65},{65,1},{2,66},{66,2},{3,67},{67,3},{4,68},{68... | collective-permute-start | bytes 2359304 | tf_op jit(solution)/shard_map/ppermute | solution.py:328
  49.8 0.7 copy-start.4
  50.5 21.0 %all-to-all-start.1 = ((f32[128,4,128]{2,1,0:T(4,128)}), f32[128,4,128]{2,1,0:T(4,128)S(1)}, u32[]{:S(2)}, u32[]{:S(2)}) async-start(f32[128,4,128]{2,1,0:T(4,128)} %copy-done.4), calls=%async_computation.1 | async-start | bytes 524288 | tf_op jit(solution)/shard_map/all_to_all | solution.py:348
  60.5 25.2 %collective-permute-start.4 = (bf16[128,2048]{1,0:T(8,128)(2,1)}, bf16[128,2048]{1,0:T(8,128)(2,1)}, u32[]{:S(2)}, u32[]{:S(2)}) collective-permute-start(bf16[128,2048]{1,0:T(8,128)(2,1)} %copy-done.7), channel_id=1, source_target_pairs={{0,64},{64,0},{1,65},{65,1},{2,66},{66,2},{3,67},{67,3},{4,68},{68... | collective-permute-start | bytes 1572872 | tf_op jit(solution)/shard_map/ppermute | solution.py:349
  71.5 1.7 %copy-start.3 = (f32[128,4608]{1,0:T(8,128)S(1)}, f32[128,4608]{1,0:T(8,128)}, u32[]{:S(2)}) copy-start(f32[128,4608]{1,0:T(8,128)} %params_ref.7) | copy-start | bytes 7077892
  74.1 9.8 %collective-permute-start.3 = (bf16[128,1152]{1,0:T(8,128)(2,1)S(1)}, bf16[128,1152]{1,0:T(8,128)(2,1)S(1)}, u32[]{:S(2)}, u32[]{:S(2)}) collective-permute-start(bf16[128,1152]{1,0:T(8,128)(2,1)S(1)} %get-tuple-element.42), channel_id=1, source_target_pairs={{0,64},{64,0},{1,65},{65,1},{2,66},{66,2},{3,67},{67,3},{4,68},{68... | collective-permute-start | bytes 884744 | tf_op jit(solution)/shard_map/ppermute | solution.py:360
  76.0 7.8 %copy-start.1 = (bf16[1,128,9216]{2,1,0:T(8,128)(2,1)S(1)}, bf16[1,128,9216]{2,1,0:T(8,128)(2,1)}, u32[]{:S(2)}) copy-start(bf16[1,128,9216]{2,1,0:T(8,128)(2,1)} %grad_ref.7) | copy-start | bytes 7077892
  76.1 13.4 %collective-permute-start.2 = (bf16[128,1024]{1,0:T(8,128)(2,1)S(1)}, bf16[128,1024]{1,0:T(8,128)(2,1)S(1)}, u32[]{:S(2)}, u32[]{:S(2)}) collective-permute-start(bf16[128,1024]{1,0:T(8,128)(2,1)S(1)} %shard_map.105), channel_id=1, source_target_pairs={{0,64},{64,0},{1,65},{65,1},{2,66},{66,2},{3,67},{67,3},{4,68},{68... | collective-permute-start | bytes 786440 | tf_op jit(solution)/shard_map/ppermute | solution.py:369

commit v4 on v3

--- a/solution.py
+++ b/solution.py
@@ -18,8 +18,12 @@
 WIDE = 1536
 AHEAD = (3, 2)
 EARLY = sum(AHEAD)
+SCALES = 2 * AHEAD[1] * BLOCK
 LATE = (2, 2)
 VMEM_LIMIT = 24 << 20
+HALF_LIMIT = 24 << 20
+MOMENTS_LIMIT = 24 << 20
+WEIGHTS_LIMIT = 24 << 20
 f32, bf16 = jnp.float32, jnp.bfloat16
 shape = jax.ShapeDtypeStruct
 
@@ -131,8 +135,8 @@
 
 
 def moments_kernel(
-    grad_ref, got_ref, row_ref, old_rows_ref, old_cols_ref, weight_ref,
-    new_cols_ref, copy_ref, sent_ref, grad, inv_cols, sent, sems, out_sem,
+    grad_ref, got_ref, row_ref, old_rows_ref, old_cols_ref, weight_ref, _,
+    new_cols_ref, copy_ref, sent_ref, ahead_ref, grad, inv_cols, sent, scale, rounded, sems, out_sems,
 ):
     width = grad.shape[1]
     height = width // LANES
@@ -146,6 +150,10 @@
     new_cols_ref[...] = new_cols
     copy_ref[...] = new_cols
     inv_cols[...] = 1.0 / new_cols
+    scale[...] = jnp.zeros_like(scale)
+    scale[: EARLY * BLOCK // LANES] = lax.rsqrt(new_cols[: EARLY * BLOCK // LANES])
+    rounded[...] = scale[...].astype(bf16)
+    (scale_copy,) = begin((rounded, ahead_ref.at[:, SCALES : SCALES + LANES], out_sems.at[0]))
     acc = jnp.zeros((LANES, LANES), f32)
     for i, (s, n) in enumerate(pieces):
         ins[i].wait()
@@ -157,7 +165,8 @@
     for i, row in enumerate([row_ref[...], flat(acc), old_rows_ref[...], weight_ref[...]]):
         value = jnp.where(at == i, jnp.broadcast_to(row, (4, LANES)), value)
     sent[...] = jnp.broadcast_to(value[None], sent.shape)
-    (copy,) = begin((sent, sent_ref, out_sem))
+    (copy,) = begin((sent, sent_ref, out_sems.at[1]))
+    scale_copy.wait()
     copy.wait()
 
 
@@ -203,11 +212,6 @@
     scale_ref[...] = param_scale
     step_size = RELATIVE * param_scale / clip_factor
     step_ref[...] = step_size
-    scale = jnp.zeros((LANES, LANES), f32)
-    at = lax.broadcasted_iota(jnp.int32, scale.shape, 0)
-    for t in range(EARLY * BLOCK // LANES):
-        scale = jnp.where(at == t, jnp.broadcast_to(col_scale[t : t + 1, :], scale.shape), scale)
-    out_ref[:, count : count + LANES] = scale.astype(bf16)
     for copy in ins:
         copy.wait()
     weights_piece(grad, params, out_ref, row_scale[...], col_scale, step_size, start // LANES)
@@ -258,14 +262,14 @@
         copy.wait()
 
 
-def early_kernel(start, width, grad_ref, ahead_ref, row_scale, late_ref, step_ref, _, out_ref,
+def early_kernel(start, width, grad_ref, ahead_ref, row_scale, scale_ref, step_ref, _, out_ref,
                  mine, got, scale, out, scales, sems, out_sem):
     count = mine.shape[1]
     first = (1 - lax.axis_index("dp")) * width + start
     ins = begin(
-        (late_ref.at[:, LATE[0] * BLOCK : LATE[0] * BLOCK + LANES], scale, sems.at[0]),
+        (scale_ref.at[:, SCALES : SCALES + LANES], scale, sems.at[0]),
         (grad_ref.at[0, :, span(first, count)], mine, sems.at[1]),
-        (ahead_ref, got, sems.at[2]),
+        (ahead_ref.at[:, 0 : 2 * count], got, sems.at[2]),
     )
     across, step_size = row_scale[...], step_ref[...]
     for copy in ins:
@@ -293,7 +297,7 @@
 dma = pltpu.SemaphoreType.DMA
 
 
-def call(kernel, ins, outs, scratch, args, nbytes, aliases=None):
+def call(kernel, ins, outs, scratch, args, nbytes, aliases=None, limit=VMEM_LIMIT):
     return pl.pallas_call(
         kernel,
         in_specs=[pl.BlockSpec(memory_space=space) for space in ins],
@@ -302,7 +306,7 @@
         scratch_shapes=list(scratch),
         input_output_aliases=aliases or {},
         cost_estimate=pl.CostEstimate(flops=nbytes, bytes_accessed=nbytes, transcendentals=0),
-        compiler_params=pltpu.CompilerParams(vmem_limit_bytes=VMEM_LIMIT),
+        compiler_params=pltpu.CompilerParams(vmem_limit_bytes=limit),
     )(*args)
 
 
@@ -315,12 +319,12 @@
 
     (outgoing,) = call(
         half_kernel, [HBM], [(HBM, shape((rows, width), bf16))],
-        [VMEM((rows, width), bf16), dma((count,)), dma((count,))], (grad_parts,), 4 * rows * width,
+        [VMEM((rows, width), bf16), dma((count,)), dma((count,))], (grad_parts,), 4 * rows * width, None, HALF_LIMIT,
     )
     got = lax.ppermute(outgoing, "dp", SWAP)
     *ahead, weight_part = call(
         prepare_kernel, [HBM, HBM, HBM],
-        [(HBM, shape((rows, 2 * n * BLOCK), bf16)) for n in AHEAD] + [(VMEM, shape((1, 1), f32))],
+        [(HBM, shape((rows, 2 * n * BLOCK + extra), bf16)) for n, extra in zip(AHEAD, (0, LANES))] + [(VMEM, shape((1, 1), f32))],
         [VMEM((rows, width), f32), VMEM((rows, early), bf16), VMEM((rows, early), bf16), dma((count + 1,)),
          dma((2 * len(AHEAD),))],
         (grad_parts, params, outgoing), 4 * rows * (width + early),
@@ -336,26 +340,28 @@
         (grad_parts, got, weight_part), 8 * rows * width,
     )
     col_parts = lax.all_to_all(sent, "row", 0, 0)
-    new_cols, cols_copy, sent = call(
-        moments_kernel, [HBM] + [VMEM] * 5,
+    new_cols, cols_copy, sent, second = call(
+        moments_kernel, [HBM] + [VMEM] * 5 + [HBM],
         [(VMEM, shape((height, LANES), f32)), (VMEM, shape((height, LANES), f32)),
-         (HBM, shape((128, 4, LANES), f32))],
-        [VMEM((rows, width), f32), VMEM((height, LANES), f32), VMEM((128, 4, LANES), f32), dma((count,)), dma],
-        (gradient, col_parts, row_part, row_moment.reshape(1, rows), col_moment.reshape(2 * height, LANES), weight_part),
-        4 * rows * width,
-    )
-    sent, arrived[0], *ahead = lax.optimization_barrier((sent, arrived[0], *ahead))
+         (HBM, shape((128, 4, LANES), f32)), (HBM, ahead[1])],
+        [VMEM((rows, width), f32), VMEM((height, LANES), f32), VMEM((128, 4, LANES), f32), VMEM((rows, LANES), f32),
+         VMEM((rows, LANES), bf16), dma((count,)), dma((2,))],
+        (gradient, col_parts, row_part, row_moment.reshape(1, rows), col_moment.reshape(2 * height, LANES), weight_part,
+         ahead[1]),
+        4 * rows * width, {6: 3}, MOMENTS_LIMIT,
+    )
+    sent, arrived[0], second = lax.optimization_barrier((sent, arrived[0], second))
     parts = lax.all_to_all(sent, ("dp", "row", "col"), 0, 0)
-    arrived += [lax.ppermute(values, "dp", SWAP) for values in ahead[1:]]
+    arrived.append(lax.ppermute(second, "dp", SWAP))
 
     n = LATE[0] * BLOCK
     out, new_rows, clip_factor, param_scale, step_size, row_scale, col_scale = call(
         first_weights_kernel, [VMEM, VMEM, HBM, HBM],
-        [(VMEM, shape((rows, n + LANES), bf16)), (VMEM, shape((1, rows), f32)),
+        [(VMEM, shape((rows, n), bf16)), (VMEM, shape((1, rows), f32)),
          (VMEM, shape((1, 1), f32)), (VMEM, shape((1, 1), f32)), (VMEM, shape((1, 1), f32)),
          (VMEM, shape((rows, LANES), f32)), (VMEM, shape((height, LANES), f32))],
         [VMEM((rows, n), f32), VMEM((rows, n), f32), VMEM((16, LANES), f32), dma((2,))],
-        (parts, cols_copy, gradient, params), 8 * rows * n,
+        (parts, cols_copy, gradient, params), 8 * rows * n, None, WEIGHTS_LIMIT,
     )
     late = [lax.ppermute(out, "dp", SWAP)]
     start = early + n
@@ -383,7 +389,7 @@
             functools.partial(early_kernel, start, width), [HBM, HBM, VMEM, HBM, VMEM, HBM], [(HBM, out_shape)],
             [VMEM((rows, n), bf16), VMEM((rows, 2 * n), bf16), VMEM((rows, LANES), bf16), VMEM((rows, n), bf16),
              VMEM((rows, LANES), f32), dma((3,)), dma],
-            (grad_parts, values, row_scale, late[0], step_size, new_weights), 8 * rows * n, {5: 0},
+            (grad_parts, values, row_scale, arrived[1], step_size, new_weights), 8 * rows * n, {5: 0},
         )
         start += n
     for blocks, values in zip(LATE, late):

time: 91.1 us -> 88.4 us (0.970)
  blocking collectives: 14.3 us -> 33.5 us
  starting transfers between devices: 21.2 us -> 11.3 us
  waiting for transfers between devices: 32.4 us -> 25 us
  local copies, waits for them, and re-layouts: 4.83 us -> 1.68 us
  Pallas kernels: 16.7 us -> 15.7 us
    all_to_all x0 -> x1, blocking collectives: none -> 19.2 us  [shards(): parts = lax.all_to_all(sent, ('dp', 'row', 'col'), 0, 0)]
    all_to_all x1 -> x0, starting transfers between devices: 9.95 us -> none  [shards(): parts = lax.all_to_all(sent, ('dp', 'row', 'col'), 0, 0)]
    all_to_all x1 -> x0, waiting for transfers between devices: 8.03 us -> none  [shards(): parts = lax.all_to_all(sent, ('dp', 'row', 'col'), 0, 0)]
    unnamed x16 -> x10, local copies, waits for them, and re-layouts: 4.83 us -> 1.68 us
    ppermute x1, waiting for transfers between devices: 1.93 us -> 0.01 us  [shards(): late = [lax.ppermute(out, 'dp', SWAP)]]
    ppermute x1, waiting for transfers between devices: 0.36 us -> 2.22 us  [shards(): late.append(lax.ppermute(out, 'dp', SWAP))]
    pallas_call x11, Pallas kernels: 16.7 us -> 15.7 us  [call(): pl.pallas_call(kernel, in_specs=[pl.BlockSpec(memory_space=space) for spa...]
  transfers between devices with their start and end apart: 6 -> 5, of which waited for: 4 -> 2; matrix products, arithmetic and copies ran while one was open for 0% -> 0% of each run, Pallas kernels for 17% -> 17%
where the time goes in v4:
time: 88.4 us; the launch traced here: 88 us
  blocking collectives  33.5 us (38%)
  waiting for transfers between devices  25 us (28%)
  Pallas kernels  15.7 us (18%)
  starting transfers between devices  11.3 us (13%)
  local copies, waits for them, and re-layouts  1.68 us (2%)
    ppermute x1, waiting for transfers between devices, shards(): got = lax.ppermute(outgoing, 'dp', SWAP)  22.8 us
    all_to_all x1, blocking collectives, shards(): parts = lax.all_to_all(sent, ('dp', 'row', 'col'), 0, 0)  19.2 us
    pallas_call x11, Pallas kernels, call(): pl.pallas_call(kernel, in_specs=[pl.BlockSpec(memory_space=space) for spa...  15.7 us
    all_to_all x1, blocking collectives, shards(): col_parts = lax.all_to_all(sent, 'row', 0, 0)  14.3 us
    ppermute x1, starting transfers between devices, shards(): got = lax.ppermute(outgoing, 'dp', SWAP)  3.82 us
    ppermute x1, starting transfers between devices, shards(): arrived.append(lax.ppermute(second, 'dp', SWAP))  2.99 us
    ppermute x1, waiting for transfers between devices, shards(): late.append(lax.ppermute(out, 'dp', SWAP))  2.22 us
    ppermute x1, starting transfers between devices, shards(): late = [lax.ppermute(out, 'dp', SWAP)]  2 us
  transfers between devices with their start and end apart: 5, of which 2 were waited for; matrix products, arithmetic and copies ran while one was open for 0% of the time, Pallas kernels for 17%

profile of v4, /device:TPU:1, one launch (start us, length us, event | category | flops | bytes accessed | tf_op | source)
XLA Modules:
  0.0 88.0 jit_solution(8986016838583029156)
XLA Ops:
  0.6 0.0 copy-start
  0.6 1.7 %copy-done = bf16[1,128,9216]{2,1,0:T(8,128)(2,1)S(1)} copy-done((bf16[1,128,9216]{2,1,0:T(8,128)(2,1)S(1)}, bf16[1,128,9216]{2,1,0:T(8,128)(2,1)}, u32[]{:S(2)}) %copy-start) | copy-done | bytes 2359320
  2.3 0.0 copy-start.2
  2.3 0.3 shard_map.99._
  2.6 3.8 %collective-permute-start = (bf16[128,4608]{1,0:T(8,128)(2,1)S(1)}, bf16[128,4608]{1,0:T(8,128)(2,1)S(1)}, u32[]{:S(2)}, u32[]{:S(2)}) collective-permute-start(bf16[128,4608]{1,0:T(8,128)(2,1)S(1)} %shard_map.99._), channel_id=1, source_target_pairs={{0,64},{64,0},{1,65},{65,1},{2,66},{66,2},{3,67},{67,3},{4,68},{68... | collective-permute-start | bytes 3538952 | tf_op jit(solution)/shard_map/ppermute | solution.py:324
  6.4 0.0 copy-done.2
  6.4 1.2 %shard_map.100 = (bf16[128,3072]{1,0:T(8,128)(2,1)S(1)}, bf16[128,2176]{1,0:T(8,128)(2,1)S(1)}, f32[1,1]{1,0:T(1,128)}) custom-call(bf16[1,128,9216]{2,1,0:T(8,128)(2,1)S(1)} %copy-done, f32[128,4608]{1,0:T(8,128)S(1)} %copy-done.2, bf16[128,4608]{1,0:T(8,128)(2,1)S(1)} %shard_map.99._), custom_call_target="tpu_custom_call" | custom-call | flops 3670016 | bytes 3670016 | tf_op jit(solution)/shard_map/pallas_call | solution.py:301
  7.6 0.0 copy-start.3
  7.6 0.0 copy-start.4
  7.6 1.4 %collective-permute-start.1 = (bf16[128,3072]{1,0:T(8,128)(2,1)S(1)}, bf16[128,3072]{1,0:T(8,128)(2,1)S(1)}, u32[]{:S(2)}, u32[]{:S(2)}) collective-permute-start(bf16[128,3072]{1,0:T(8,128)(2,1)S(1)} %get-tuple-element.36), channel_id=1, source_target_pairs={{0,64},{64,0},{1,65},{65,1},{2,66},{66,2},{3,67},{67,3},{4,68},{68... | collective-permute-start | bytes 2359304 | tf_op jit(solution)/shard_map/ppermute | solution.py:332
  9.0 22.8 %collective-permute-done.got_ref = bf16[128,4608]{1,0:T(8,128)(2,1)S(1)} collective-permute-done((bf16[128,4608]{1,0:T(8,128)(2,1)S(1)}, bf16[128,4608]{1,0:T(8,128)(2,1)S(1)}, u32[]{:S(2)}, u32[]{:S(2)}) %collective-permute-start) | collective-permute-done | bytes 1179680 | tf_op jit(solution)/shard_map/ppermute | solution.py:324
  31.8 1.8 %shard_map.101 = (f32[128,4608]{1,0:T(8,128)S(1)}, f32[1,128]{1,0:T(1,128)S(1)}, bf16[16,48,128]{2,1,0:T(8,128)(2,1)S(1)}) custom-call(bf16[1,128,9216]{2,1,0:T(8,128)(2,1)S(1)} %copy-done, bf16[128,4608]{1,0:T(8,128)(2,1)S(1)} %collective-permute-done.got_ref, f32[1,1]{1,0:T(1,128)} %get-tuple-element.30._.weight_ref), custom_call_target="tpu_custom_call" | custom-call | flops 4718592 | bytes 4718592 | tf_op jit(solution)/shard_map/pallas_call | solution.py:301
  33.6 14.3 %all_to_all.10.got_ref = bf16[16,48,128]{2,1,0:T(8,128)(2,1)S(1)} all-to-all(bf16[16,48,128]{2,1,0:T(8,128)(2,1)S(1)} %get-tuple-element.32), channel_id=1, replica_groups=mesh['dp'=2,'row'=16,'col'=4] {'row'}, dimensions={0} | all-to-all | bytes 393216 | tf_op jit(solution)/shard_map/all_to_all | solution.py:342
  48.0 0.0 copy-done.3
  48.0 0.0 copy-done.4
  48.0 1.9 %shard_map.102 = (f32[36,128]{1,0:T(8,128)}, f32[36,128]{1,0:T(8,128)S(1)}, f32[128,4,128]{2,1,0:T(4,128)S(1)}, bf16[128,2176]{1,0:T(8,128)(2,1)S(1)}) custom-call(f32[128,4608]{1,0:T(8,128)S(1)} %get-tuple-element.31.grad_ref, bf16[16,48,128]{2,1,0:T(8,128)(2,1)S(1)} %all_to_all.10.got_ref, ...), custom_call_target="tpu_custom_call", output_to_operand_aliasing={{3}: (6, {})} | custom-call | flops 2359296 | bytes 2359296 | tf_op jit(solution)/shard_map/pallas_call | solution.py:301
  49.9 0.0 collective-permute-done.1.ahead_ref
  49.9 3.0 %collective-permute-start.4 = (bf16[128,2176]{1,0:T(8,128)(2,1)S(1)}, bf16[128,2176]{1,0:T(8,128)(2,1)S(1)}, u32[]{:S(2)}, u32[]{:S(2)}) collective-permute-start(bf16[128,2176]{1,0:T(8,128)(2,1)S(1)} %get-tuple-element.45), channel_id=1, source_target_pairs={{0,64},{64,0},{1,65},{65,1},{2,66},{66,2},{3,67},{67,3},{4,68},{68... | collective-permute-start | bytes 1671176 | tf_op jit(solution)/shard_map/ppermute | solution.py:355
  52.9 19.2 %all_to_all.11.got_ref = f32[128,4,128]{2,1,0:T(4,128)S(1)} all-to-all(f32[128,4,128]{2,1,0:T(4,128)S(1)} %get-tuple-element.38), channel_id=1, replica_groups=mesh['dp'=2,'row'=16,'col'=4] {'dp','row','col'}, dimensions={0} | all-to-all | bytes 524288 | tf_op jit(solution)/shard_map/all_to_all | solution.py:354
  72.0 0.9 %shard_map.103 = (bf16[128,1024]{1,0:T(8,128)(2,1)S(1)}, f32[1,128]{1,0:T(1,128)}, f32[1,1]{1,0:T(1,128)}, f32[1,1]{1,0:T(1,128)}, f32[1,1]{1,0:T(1,128)}, /*ind...) custom-call(f32[128,4,128]{2,1,0:T(4,128)S(1)} %all_to_all.11.got_ref, f32[36,128]{1,0:T(8,128)S(1)} %get-tuple-element.39.cols_ref, ...), custom_call_target="tpu_custom_call" | custom-call | flops 1048576 | bytes 1048576 | tf_op jit(solution)/shard_map/pallas_call | solution.py:301
  72.9 2.0 %collective-permute-start.3 = (bf16[128,1024]{1,0:T(8,128)(2,1)S(1)}, bf16[128,1024]{1,0:T(8,128)(2,1)S(1)}, u32[]{:S(2)}, u32[]{:S(2)}) collective-permute-start(bf16[128,1024]{1,0:T(8,128)(2,1)S(1)} %get-tuple-element.44), channel_id=1, source_target_pairs={{0,64},{64,0},{1,65},{65,1},{2,66},{66,2},{3,67},{67,3},{4,68},{68... | collective-permute-start | bytes 786440 | tf_op jit(solution)/shard_map/ppermute | solution.py:366
  74.9 0.9 shard_map.105
  75.8 0.0 copy-start.1
  75.8 1.1 %collective-permute-start.2 = (bf16[128,1024]{1,0:T(8,128)(2,1)S(1)}, bf16[128,1024]{1,0:T(8,128)(2,1)S(1)}, u32[]{:S(2)}, u32[]{:S(2)}) collective-permute-start(bf16[128,1024]{1,0:T(8,128)(2,1)S(1)} %shard_map.105), channel_id=1, source_target_pairs={{0,64},{64,0},{1,65},{65,1},{2,66},{66,2},{3,67},{67,3},{4,68},{68... | collective-permute-start | bytes 786440 | tf_op jit(solution)/shard_map/ppermute | solution.py:375
  77.0 3.9 %shard_map.104 = (f32[128,4608]{1,0:T(8,128)}, f32[128,4608]{1,0:T(8,128)}, bf16[128,9216]{1,0:T(8,128)(2,1)}) custom-call(f32[128,4608]{1,0:T(8,128)S(1)} %get-tuple-element.31.grad_ref, f32[128,4608]{1,0:T(8,128)S(1)} %copy-done.2, f32[128,128]{1,0:T(8,128)S(1)} %get-tuple-element.40.row_scale, f32[36,128]{1,0:T(8,128)S(1)} %get-tuple-element.41.col_scale, ...), custom_call_target="tpu_custom_call" | custom-call | flops 10616832 | bytes 10616832 | tf_op jit(solution)/shard_map/pallas_call | solution.py:301
  80.8 0.0 collective-permute-done.4.scale_ref.ahead_ref
  80.8 0.0 copy-done.1
  80.8 1.8 %shard_map.106._ = bf16[128,9216]{1,0:T(8,128)(2,1)} custom-call(bf16[1,128,9216]{2,1,0:T(8,128)(2,1)S(1)} %copy-done.1, bf16[128,3072]{1,0:T(8,128)(2,1)S(1)} %collective-permute-done.1.ahead_ref, f32[128,128]{1,0:T(8,128)S(1)} %get-tuple-element.40.row_scale, ...), custom_call_target="tpu_custom_call", output_to_operand_aliasing={{}: (5, {})} | custom-call | flops 1572864 | bytes 1572864 | tf_op jit(solution)/shard_map/pallas_call | solution.py:301
  82.6 1.7 %shard_map.107._ = bf16[128,9216]{1,0:T(8,128)(2,1)} custom-call(bf16[1,128,9216]{2,1,0:T(8,128)(2,1)S(1)} %copy-done.1, bf16[128,2176]{1,0:T(8,128)(2,1)S(1)} %collective-permute-done.4.scale_ref.ahead_ref, f32[128,128]{1,0:T(8,128)S(1)} %get-tuple-element.40.row_scale, ...), custom_call_target="tpu_custom_call", output_to_operand_aliasing={{}: (5, {})} | custom-call | flops 1048576 | bytes 1048576 | tf_op jit(solution)/shard_map/pallas_call | solution.py:301
  84.3 0.0 collective-permute-done.3.got_ref
  84.3 0.8 shard_map.108._
  85.1 2.2 %collective-permute-done.2.got_ref = bf16[128,1024]{1,0:T(8,128)(2,1)S(1)} collective-permute-done((bf16[128,1024]{1,0:T(8,128)(2,1)S(1)}, bf16[128,1024]{1,0:T(8,128)(2,1)S(1)}, u32[]{:S(2)}, u32[]{:S(2)}) %collective-permute-start.2) | collective-permute-done | bytes 262176 | tf_op jit(solution)/shard_map/ppermute | solution.py:375
  87.3 0.7 shard_map.109
Async XLA Ops:
  0.6 1.7 %copy-start = (bf16[1,128,9216]{2,1,0:T(8,128)(2,1)S(1)}, bf16[1,128,9216]{2,1,0:T(8,128)(2,1)}, u32[]{:S(2)}) copy-start(bf16[1,128,9216]{2,1,0:T(8,128)(2,1)} %grad_ref.7) | copy-start | bytes 7077892
  2.3 4.1 %copy-start.2 = (f32[128,4608]{1,0:T(8,128)S(1)}, f32[128,4608]{1,0:T(8,128)}, u32[]{:S(2)}) copy-start(f32[128,4608]{1,0:T(8,128)} %params_ref.7) | copy-start | bytes 7077892
  2.6 29.2 %collective-permute-start = (bf16[128,4608]{1,0:T(8,128)(2,1)S(1)}, bf16[128,4608]{1,0:T(8,128)(2,1)S(1)}, u32[]{:S(2)}, u32[]{:S(2)}) collective-permute-start(bf16[128,4608]{1,0:T(8,128)(2,1)S(1)} %shard_map.99._), channel_id=1, source_target_pairs={{0,64},{64,0},{1,65},{65,1},{2,66},{66,2},{3,67},{67,3},{4,68},{68... | collective-permute-start | bytes 3538952 | tf_op jit(solution)/shard_map/ppermute | solution.py:324
  7.6 40.3 %copy-start.3 = (f32[9216]{0:T(1024)S(1)}, f32[9216]{0:T(1024)}, u32[]{:S(2)}) copy-start(f32[9216]{0:T(1024)} %param.7) | copy-start | bytes 110596
  7.6 40.3 %copy-start.4 = (f32[128]{0:T(128)S(1)}, f32[128]{0:T(128)}, u32[]{:S(2)}) copy-start(f32[128]{0:T(128)} %param.6) | copy-start | bytes 1540
  7.6 42.2 %collective-permute-start.1 = (bf16[128,3072]{1,0:T(8,128)(2,1)S(1)}, bf16[128,3072]{1,0:T(8,128)(2,1)S(1)}, u32[]{:S(2)}, u32[]{:S(2)}) collective-permute-start(bf16[128,3072]{1,0:T(8,128)(2,1)S(1)} %get-tuple-element.36), channel_id=1, source_target_pairs={{0,64},{64,0},{1,65},{65,1},{2,66},{66,2},{3,67},{67,3},{4,68},{68... | collective-permute-start | bytes 2359304 | tf_op jit(solution)/shard_map/ppermute | solution.py:332
  49.9 31.0 %collective-permute-start.4 = (bf16[128,2176]{1,0:T(8,128)(2,1)S(1)}, bf16[128,2176]{1,0:T(8,128)(2,1)S(1)}, u32[]{:S(2)}, u32[]{:S(2)}) collective-permute-start(bf16[128,2176]{1,0:T(8,128)(2,1)S(1)} %get-tuple-element.45), channel_id=1, source_target_pairs={{0,64},{64,0},{1,65},{65,1},{2,66},{66,2},{3,67},{67,3},{4,68},{68... | collective-permute-start | bytes 1671176 | tf_op jit(solution)/shard_map/ppermute | solution.py:355
  72.9 11.4 %collective-permute-start.3 = (bf16[128,1024]{1,0:T(8,128)(2,1)S(1)}, bf16[128,1024]{1,0:T(8,128)(2,1)S(1)}, u32[]{:S(2)}, u32[]{:S(2)}) collective-permute-start(bf16[128,1024]{1,0:T(8,128)(2,1)S(1)} %get-tuple-element.44), channel_id=1, source_target_pairs={{0,64},{64,0},{1,65},{65,1},{2,66},{66,2},{3,67},{67,3},{4,68},{68... | collective-permute-start | bytes 786440 | tf_op jit(solution)/shard_map/ppermute | solution.py:366
  75.8 5.0 %copy-start.1 = (bf16[1,128,9216]{2,1,0:T(8,128)(2,1)S(1)}, bf16[1,128,9216]{2,1,0:T(8,128)(2,1)}, u32[]{:S(2)}) copy-start(bf16[1,128,9216]{2,1,0:T(8,128)(2,1)} %grad_ref.7) | copy-start | bytes 7077892
  75.8 11.5 %collective-permute-start.2 = (bf16[128,1024]{1,0:T(8,128)(2,1)S(1)}, bf16[128,1024]{1,0:T(8,128)(2,1)S(1)}, u32[]{:S(2)}, u32[]{:S(2)}) collective-permute-start(bf16[128,1024]{1,0:T(8,128)(2,1)S(1)} %shard_map.105), channel_id=1, source_target_pairs={{0,64},{64,0},{1,65},{65,1},{2,66},{66,2},{3,67},{67,3},{4,68},{68... | collective-permute-start | bytes 786440 | tf_op jit(solution)/shard_map/ppermute | solution.py:375

commit v5 on v3

--- a/solution.py
+++ b/solution.py
@@ -14,11 +14,10 @@
 RELATIVE = min(0.01, STEP ** (-0.5))
 LANES = 128
 SWAP = [(0, 1), (1, 0)]
-BLOCK = 512
+BLOCK = 256
 WIDE = 1536
-AHEAD = (3, 2)
-EARLY = sum(AHEAD)
-LATE = (2, 2)
+EARLY = 11
+LATE = (4, 3)
 VMEM_LIMIT = 24 << 20
 f32, bf16 = jnp.float32, jnp.bfloat16
 shape = jax.ShapeDtypeStruct
@@ -30,6 +29,14 @@
 
 def flat(acc):
     return jnp.sum(acc.T, axis=0, keepdims=True)
+
+
+def split(value, count):
+    parts = []
+    for _ in range(count):
+        parts.append(value.astype(bf16).astype(f32))
+        value = value - parts[-1]
+    return parts
 
 
 def tile(at):
@@ -67,38 +74,32 @@
         copy.wait()
 
 
-def prepare_kernel(grad_ref, params_ref, _, *refs):
-    ahead_refs, (weight_ref, params, parts, values, sems, out_sems) = refs[: len(AHEAD)], refs[len(AHEAD) :]
-    width = params.shape[1]
+def prepare_kernel(grad_ref, params_ref, _, ahead_ref, weight_ref, params, parts, values, sems, out_sems):
+    width, early = params.shape[1], parts.shape[1]
     mine = lax.axis_index("dp") * width
     pieces = steps(width)
+    grad = begin((grad_ref.at[0, :, span(mine, early)], parts, sems.at[len(pieces)]))[0]
     ins = [
         begin((params_ref.at[:, s : s + n], params.at[:, s : s + n], sems.at[i]))[0] for i, (s, n) in enumerate(pieces)
     ]
-    grad = begin((grad_ref.at[0, :, span(mine, EARLY * BLOCK)], parts, sems.at[len(pieces)]))[0]
     acc = jnp.zeros((LANES, LANES), f32)
     for i, (s, n) in enumerate(pieces):
         ins[i].wait()
         for t in range(s // LANES, (s + n) // LANES):
             value = params[:, tile(t)]
             acc = acc + value * value
-            if t < EARLY * BLOCK // LANES:
+            if t < early // LANES:
                 values[:, tile(t)] = value.astype(bf16)
     grad.wait()
-    outs, start = [], 0
-    for i, (count, ahead_ref) in enumerate(zip(AHEAD, ahead_refs)):
-        n = count * BLOCK
-        outs += begin(
-            (parts.at[:, start : start + n], ahead_ref.at[:, 0:n], out_sems.at[2 * i]),
-            (values.at[:, start : start + n], ahead_ref.at[:, n : 2 * n], out_sems.at[2 * i + 1]),
-        )
-        start += n
+    outs = begin(
+        (parts, ahead_ref.at[:, 0:early], out_sems.at[0]), (values, ahead_ref.at[:, early : 2 * early], out_sems.at[1])
+    )
     weight_ref[...] = jnp.sum(jnp.sum(acc, axis=0, keepdims=True), axis=1, keepdims=True)
     for copy in outs:
         copy.wait()
 
 
-def sums_kernel(grad_parts_ref, got_ref, _, grad_ref, row_ref, sent_ref, mine, got, grad, cols, sems, out_sems):
+def sums_kernel(grad_parts_ref, got_ref, old_rows_ref, _, grad_ref, row_ref, sent_ref, mine, got, grad, cols, sems, out_sems):
     width = grad.shape[1]
     first = lax.axis_index("dp") * width
     pieces = steps(width)
@@ -123,6 +124,8 @@
             cols[t : t + 1, :] = jnp.sum(squares, axis=0, keepdims=True)
         outs += begin((grad.at[:, s : s + n], grad_ref.at[:, s : s + n], out_sems.at[i]))
     row_ref[...] = flat(acc)
+    for i, part in enumerate(split(old_rows_ref[...], 2)):
+        cols[width // LANES + i : width // LANES + i + 1, :] = part
     sent = cols[...].astype(bf16)
     for peer in range(sent_ref.shape[0]):
         sent_ref[peer] = sent
@@ -131,8 +134,8 @@
 
 
 def moments_kernel(
-    grad_ref, got_ref, row_ref, old_rows_ref, old_cols_ref, weight_ref,
-    new_cols_ref, copy_ref, sent_ref, grad, inv_cols, sent, sems, out_sem,
+    grad_ref, got_ref, row_ref, old_cols_ref, weight_ref,
+    new_cols_ref, copy_ref, old_rows_ref, sent_ref, grad, inv_cols, sems,
 ):
     width = grad.shape[1]
     height = width // LANES
@@ -141,6 +144,9 @@
     totals = got_ref[0].astype(f32)
     for peer in range(1, got_ref.shape[0]):
         totals = totals + got_ref[peer].astype(f32)
+    for peer in range(got_ref.shape[0]):
+        rows = got_ref[peer].astype(f32)
+        old_rows_ref[peer : peer + 1, :] = rows[height : height + 1] + rows[height + 1 : height + 2]
     old_cols = jnp.where(lax.axis_index("dp") == 0, old_cols_ref[:height], old_cols_ref[height:])
     new_cols = DECAY * old_cols + (1.0 - DECAY) * (totals[:height] / R)
     new_cols_ref[...] = new_cols
@@ -152,13 +158,16 @@
         for t in range(s // LANES, (s + n) // LANES):
             g = grad[:, tile(t)]
             acc = acc + g * g * inv_cols[t : t + 1, :]
+    lane = lax.broadcasted_iota(jnp.int32, (1, LANES), 1)
+    weight = jnp.zeros((1, LANES), f32)
+    for i, part in enumerate(split(jnp.broadcast_to(weight_ref[...], (1, LANES)), 3)):
+        weight = jnp.where(lane == i, part, weight)
     at = lax.broadcasted_iota(jnp.int32, (4, LANES), 0)
     value = jnp.zeros((4, LANES), f32)
-    for i, row in enumerate([row_ref[...], flat(acc), old_rows_ref[...], weight_ref[...]]):
+    for i, row in enumerate(split(row_ref[...], 2) + [flat(acc), weight]):
         value = jnp.where(at == i, jnp.broadcast_to(row, (4, LANES)), value)
-    sent[...] = jnp.broadcast_to(value[None], sent.shape)
-    (copy,) = begin((sent, sent_ref, out_sem))
-    copy.wait()
+    value = value.astype(bf16)
+    sent_ref[...] = jnp.broadcast_to(value[None], sent_ref.shape)
 
 
 def weights_piece(grad, params, out_ref, row_scale, col_scale, step_size, first):
@@ -168,8 +177,8 @@
 
 
 def first_weights_kernel(
-    got_ref, cols_ref, grad_ref, params_ref,
-    out_ref, rows_ref, clip_ref, scale_ref, step_ref, row_scale, col_scale, grad, params, all_rows, sems,
+    got_ref, cols_ref, old_rows_ref, grad_ref, params_ref,
+    out_ref, rows_ref, clip_ref, scale_ref, step_ref, row_scale, col_scale, grad, params, all_rows, scale, sems,
 ):
     start, count = EARLY * BLOCK, grad.shape[1]
     ins = begin(
@@ -183,11 +192,11 @@
         got = None
         for d in range(2):
             for c in range(4):
-                term = got_ref[d * 64 + block * 4 + c]
+                term = got_ref[d * 64 + block * 4 + c].astype(f32)
                 got = term if got is None else got + term
-        rows = DECAY * got_ref[block * 4][2:3] + (1.0 - DECAY) * (got[0:1] / C)
+        rows = DECAY * old_rows_ref[block : block + 1, :] + (1.0 - DECAY) * ((got[0:1] + got[1:2]) / C)
         all_rows[block : block + 1, :] = rows
-        update_sum = update_sum + got[1:2] / rows
+        update_sum = update_sum + got[2:3] / rows
         row_sum = row_sum + rows
         weight_sum = weight_sum + got[3:4]
     row_mean = jnp.sum(row_sum, axis=1, keepdims=True) / R
@@ -196,18 +205,16 @@
     row_scale[...] = down(lax.rsqrt(rows / row_mean))
     col_scale[...] = lax.rsqrt(cols_ref[...])
     update_mean = jnp.sum(update_sum, axis=1, keepdims=True) * row_mean / (R * C)
-    weight_mean = weight_sum[:, :1] / (R * C)
+    weight_mean = jnp.sum(weight_sum, axis=1, keepdims=True) / (R * C)
     clip_factor = jnp.maximum(1.0, jnp.sqrt(update_mean))
     param_scale = jnp.maximum(0.001, jnp.sqrt(weight_mean))
     clip_ref[...] = clip_factor
     scale_ref[...] = param_scale
     step_size = RELATIVE * param_scale / clip_factor
     step_ref[...] = step_size
-    scale = jnp.zeros((LANES, LANES), f32)
-    at = lax.broadcasted_iota(jnp.int32, scale.shape, 0)
-    for t in range(EARLY * BLOCK // LANES):
-        scale = jnp.where(at == t, jnp.broadcast_to(col_scale[t : t + 1, :], scale.shape), scale)
-    out_ref[:, count : count + LANES] = scale.astype(bf16)
+    scale[...] = jnp.zeros_like(scale)
+    scale[: start // LANES] = col_scale[: start // LANES]
+    out_ref[:, count : count + LANES] = scale[...].astype(bf16)
     for copy in ins:
         copy.wait()
     weights_piece(grad, params, out_ref, row_scale[...], col_scale, step_size, start // LANES)
@@ -258,26 +265,28 @@
         copy.wait()
 
 
-def early_kernel(start, width, grad_ref, ahead_ref, row_scale, late_ref, step_ref, _, out_ref,
-                 mine, got, scale, out, scales, sems, out_sem):
-    count = mine.shape[1]
-    first = (1 - lax.axis_index("dp")) * width + start
+def early_kernel(width, grad_ref, ahead_ref, row_scale, late_ref, step_ref, _, out_ref,
+                 mine, got, late, out, scale, sems, out_sems):
+    count, extra = mine.shape[1], late.shape[1] - LANES
+    first = (1 - lax.axis_index("dp")) * width
     ins = begin(
-        (late_ref.at[:, LATE[0] * BLOCK : LATE[0] * BLOCK + LANES], scale, sems.at[0]),
-        (grad_ref.at[0, :, span(first, count)], mine, sems.at[1]),
-        (ahead_ref, got, sems.at[2]),
+        (grad_ref.at[0, :, span(first, count)], mine, sems.at[0]),
+        (ahead_ref, got, sems.at[1]),
+        (late_ref, late, sems.at[2]),
     )
     across, step_size = row_scale[...], step_ref[...]
-    for copy in ins:
-        copy.wait()
-    scales[...] = scale[...].astype(f32)
+    ins[2].wait()
+    outs = begin((late.at[:, 0:extra], out_ref.at[:, span(first + count, extra)], out_sems.at[0]))
+    scale[...] = late[:, extra : extra + LANES].astype(f32)
+    for copy in ins[:2]:
+        copy.wait()
     for t in range(count // LANES):
         g = mine[:, tile(t)].astype(f32) + got[:, tile(t)].astype(f32)
-        at = start // LANES + t
-        update = g * across * scales[at : at + 1, :]
+        update = g * across * scale[t : t + 1, :]
         out[:, tile(t)] = (got[:, tile(count // LANES + t)].astype(f32) - step_size * update).astype(bf16)
-    (copy,) = begin((out, out_ref.at[:, span(first, count)], out_sem))
-    copy.wait()
+    outs += begin((out, out_ref.at[:, span(first, count)], out_sems.at[1]))
+    for copy in outs:
+        copy.wait()
 
 
 def place_kernel(start, width, got_ref, _, out_ref, got, sems):
@@ -293,7 +302,7 @@
 dma = pltpu.SemaphoreType.DMA
 
 
-def call(kernel, ins, outs, scratch, args, nbytes, aliases=None):
+def call(kernel, ins, outs, scratch, args, nbytes, aliases=None, limit=VMEM_LIMIT):
     return pl.pallas_call(
         kernel,
         in_specs=[pl.BlockSpec(memory_space=space) for space in ins],
@@ -302,7 +311,7 @@
         scratch_shapes=list(scratch),
         input_output_aliases=aliases or {},
         cost_estimate=pl.CostEstimate(flops=nbytes, bytes_accessed=nbytes, transcendentals=0),
-        compiler_params=pltpu.CompilerParams(vmem_limit_bytes=VMEM_LIMIT),
+        compiler_params=pltpu.CompilerParams(vmem_limit_bytes=limit),
     )(*args)
 
 
@@ -318,44 +327,41 @@
         [VMEM((rows, width), bf16), dma((count,)), dma((count,))], (grad_parts,), 4 * rows * width,
     )
     got = lax.ppermute(outgoing, "dp", SWAP)
-    *ahead, weight_part = call(
+    ahead, weight_part = call(
         prepare_kernel, [HBM, HBM, HBM],
-        [(HBM, shape((rows, 2 * n * BLOCK), bf16)) for n in AHEAD] + [(VMEM, shape((1, 1), f32))],
-        [VMEM((rows, width), f32), VMEM((rows, early), bf16), VMEM((rows, early), bf16), dma((count + 1,)),
-         dma((2 * len(AHEAD),))],
+        [(HBM, shape((rows, 2 * early), bf16)), (VMEM, shape((1, 1), f32))],
+        [VMEM((rows, width), f32), VMEM((rows, early), bf16), VMEM((rows, early), bf16), dma((count + 1,)), dma((2,))],
         (grad_parts, params, outgoing), 4 * rows * (width + early),
     )
-    arrived = [lax.ppermute(ahead[0], "dp", SWAP)]
+    ahead = lax.ppermute(ahead, "dp", SWAP)
 
     gradient, row_part, sent = call(
-        sums_kernel, [HBM, HBM, VMEM],
+        sums_kernel, [HBM, HBM, VMEM, VMEM],
         [(HBM, shape((rows, width), f32)), (VMEM, shape((1, rows), f32)),
          (VMEM, shape((16, padded, LANES), bf16))],
         [VMEM((rows, width), bf16), VMEM((rows, width), bf16), VMEM((rows, width), f32), VMEM((padded, LANES), f32),
          dma((2 * count,)), dma((count,))],
-        (grad_parts, got, weight_part), 8 * rows * width,
+        (grad_parts, got, row_moment.reshape(1, rows), weight_part), 8 * rows * width,
     )
     col_parts = lax.all_to_all(sent, "row", 0, 0)
-    new_cols, cols_copy, sent = call(
-        moments_kernel, [HBM] + [VMEM] * 5,
+    new_cols, cols_copy, old_rows, sent = call(
+        moments_kernel, [HBM] + [VMEM] * 4,
         [(VMEM, shape((height, LANES), f32)), (VMEM, shape((height, LANES), f32)),
-         (HBM, shape((128, 4, LANES), f32))],
-        [VMEM((rows, width), f32), VMEM((height, LANES), f32), VMEM((128, 4, LANES), f32), dma((count,)), dma],
-        (gradient, col_parts, row_part, row_moment.reshape(1, rows), col_moment.reshape(2 * height, LANES), weight_part),
+         (VMEM, shape((16, LANES), f32)), (VMEM, shape((128, 4, LANES), bf16))],
+        [VMEM((rows, width), f32), VMEM((height, LANES), f32), dma((count,))],
+        (gradient, col_parts, row_part, col_moment.reshape(2 * height, LANES), weight_part),
         4 * rows * width,
     )
-    sent, arrived[0], *ahead = lax.optimization_barrier((sent, arrived[0], *ahead))
     parts = lax.all_to_all(sent, ("dp", "row", "col"), 0, 0)
-    arrived += [lax.ppermute(values, "dp", SWAP) for values in ahead[1:]]
 
     n = LATE[0] * BLOCK
     out, new_rows, clip_factor, param_scale, step_size, row_scale, col_scale = call(
-        first_weights_kernel, [VMEM, VMEM, HBM, HBM],
+        first_weights_kernel, [VMEM, VMEM, VMEM, HBM, HBM],
         [(VMEM, shape((rows, n + LANES), bf16)), (VMEM, shape((1, rows), f32)),
          (VMEM, shape((1, 1), f32)), (VMEM, shape((1, 1), f32)), (VMEM, shape((1, 1), f32)),
          (VMEM, shape((rows, LANES), f32)), (VMEM, shape((height, LANES), f32))],
-        [VMEM((rows, n), f32), VMEM((rows, n), f32), VMEM((16, LANES), f32), dma((2,))],
-        (parts, cols_copy, gradient, params), 8 * rows * n,
+        [VMEM((rows, n), f32), VMEM((rows, n), f32), VMEM((16, LANES), f32), VMEM((rows, LANES), f32), dma((2,))],
+        (parts, cols_copy, old_rows, gradient, params), 8 * rows * n,
     )
     late = [lax.ppermute(out, "dp", SWAP)]
     start = early + n
@@ -376,17 +382,15 @@
         [VMEM((rows, width), f32)] * 4 + [VMEM((rows, width), bf16), dma((2 * count,)), dma((3 * count,))],
         (gradient, params, row_scale, col_scale, step_size), 18 * rows * width,
     )
-    start = 0
-    for blocks, values in zip(AHEAD, arrived):
-        n = blocks * BLOCK
-        (new_weights,) = call(
-            functools.partial(early_kernel, start, width), [HBM, HBM, VMEM, HBM, VMEM, HBM], [(HBM, out_shape)],
-            [VMEM((rows, n), bf16), VMEM((rows, 2 * n), bf16), VMEM((rows, LANES), bf16), VMEM((rows, n), bf16),
-             VMEM((rows, LANES), f32), dma((3,)), dma],
-            (grad_parts, values, row_scale, late[0], step_size, new_weights), 8 * rows * n, {5: 0},
-        )
-        start += n
-    for blocks, values in zip(LATE, late):
+    n = LATE[0] * BLOCK
+    (new_weights,) = call(
+        functools.partial(early_kernel, width), [HBM, HBM, VMEM, HBM, VMEM, HBM], [(HBM, out_shape)],
+        [VMEM((rows, early), bf16), VMEM((rows, 2 * early), bf16), VMEM((rows, n + LANES), bf16),
+         VMEM((rows, early), bf16), VMEM((rows, LANES), f32), dma((3,)), dma((2,))],
+        (grad_parts, ahead, row_scale, late[0], step_size, new_weights), 8 * rows * early, {5: 0},
+    )
+    start = early + n
+    for blocks, values in zip(LATE[1:], late[1:]):
         n = blocks * BLOCK
         (new_weights,) = call(
             functools.partial(place_kernel, start, width), [HBM, HBM], [(HBM, out_shape)],

time: 91.1 us -> 85.4 us (0.937)
  blocking collectives: 14.3 us -> 34.2 us
  starting transfers between devices: 21.2 us -> 7.22 us
  waiting for transfers between devices: 32.4 us -> 27.7 us
  Pallas kernels: 16.7 us -> 13.6 us
  local copies, waits for them, and re-layouts: 4.83 us -> 1.83 us
    all_to_all x0 -> x1, blocking collectives: none -> 19.9 us  [shards(): parts = lax.all_to_all(sent, ('dp', 'row', 'col'), 0, 0)]
    all_to_all x1 -> x0, starting transfers between devices: 9.95 us -> none  [shards(): parts = lax.all_to_all(sent, ('dp', 'row', 'col'), 0, 0)]
    all_to_all x1 -> x0, waiting for transfers between devices: 8.03 us -> none  [shards(): parts = lax.all_to_all(sent, ('dp', 'row', 'col'), 0, 0)]
    ppermute x2 -> x1, starting transfers between devices: 4.29 us -> 0.26 us  [shards(): ahead = lax.ppermute(ahead, 'dp', SWAP)]
    pallas_call x11 -> x9, Pallas kernels: 16.7 us -> 13.6 us  [call(): pl.pallas_call(kernel, in_specs=[pl.BlockSpec(memory_space=space) for spa...]
    unnamed x16 -> x10, local copies, waits for them, and re-layouts: 4.83 us -> 1.83 us
    ppermute x1, waiting for transfers between devices: 22.1 us -> 23.9 us  [shards(): got = lax.ppermute(outgoing, 'dp', SWAP)]
    ppermute x1, waiting for transfers between devices: 0.36 us -> 1.9 us  [shards(): late.append(lax.ppermute(out, 'dp', SWAP))]
  transfers between devices with their start and end apart: 6 -> 4, of which waited for: 4 -> 3; matrix products, arithmetic and copies ran while one was open for 0% -> 0% of each run, Pallas kernels for 17% -> 15%
where the time goes in v5:
time: 85.4 us; the launch traced here: 85.2 us
  blocking collectives  34.2 us (40%)
  waiting for transfers between devices  27.7 us (32%)
  Pallas kernels  13.6 us (16%)
  starting transfers between devices  7.22 us (8%)
  local copies, waits for them, and re-layouts  1.83 us (2%)
    ppermute x1, waiting for transfers between devices, shards(): got = lax.ppermute(outgoing, 'dp', SWAP)  23.9 us
    all_to_all x1, blocking collectives, shards(): parts = lax.all_to_all(sent, ('dp', 'row', 'col'), 0, 0)  19.9 us
    all_to_all x1, blocking collectives, shards(): col_parts = lax.all_to_all(sent, 'row', 0, 0)  14.3 us
    pallas_call x9, Pallas kernels, call(): pl.pallas_call(kernel, in_specs=[pl.BlockSpec(memory_space=space) for spa...  13.6 us
    ppermute x1, starting transfers between devices, shards(): got = lax.ppermute(outgoing, 'dp', SWAP)  3.82 us
    ppermute x1, starting transfers between devices, shards(): late = [lax.ppermute(out, 'dp', SWAP)]  2.2 us
    ppermute x1, waiting for transfers between devices, shards(): late.append(lax.ppermute(out, 'dp', SWAP))  1.9 us
    ppermute x1, waiting for transfers between devices, shards(): late = [lax.ppermute(out, 'dp', SWAP)]  1.84 us
  transfers between devices with their start and end apart: 4, of which 3 were waited for; matrix products, arithmetic and copies ran while one was open for 0% of the time, Pallas kernels for 15%

profile of v5, /device:TPU:1, one launch (start us, length us, event | category | flops | bytes accessed | tf_op | source)
XLA Modules:
  0.0 85.2 jit_solution(18203166547331204611)
XLA Ops:
  0.6 0.0 copy-start
  0.6 0.0 copy-start.1
  0.7 1.8 %copy-done.1 = bf16[1,128,9216]{2,1,0:T(8,128)(2,1)S(1)} copy-done((bf16[1,128,9216]{2,1,0:T(8,128)(2,1)S(1)}, bf16[1,128,9216]{2,1,0:T(8,128)(2,1)}, u32[]{:S(2)}) %copy-start.1) | copy-done | bytes 2359320
  2.5 0.3 shard_map.99._
  2.7 0.0 copy-start.4
  2.7 3.8 %collective-permute-start = (bf16[128,4608]{1,0:T(8,128)(2,1)S(1)}, bf16[128,4608]{1,0:T(8,128)(2,1)S(1)}, u32[]{:S(2)}, u32[]{:S(2)}) collective-permute-start(bf16[128,4608]{1,0:T(8,128)(2,1)S(1)} %shard_map.99._), channel_id=1, source_target_pairs={{0,64},{64,0},{1,65},{65,1},{2,66},{66,2},{3,67},{67,3},{4,68},{68... | collective-permute-start | bytes 3538952 | tf_op jit(solution)/shard_map/ppermute | solution.py:329
  6.6 0.0 copy-done
  6.6 1.2 %shard_map.100 = (bf16[128,5632]{1,0:T(8,128)(2,1)S(1)}, f32[1,1]{1,0:T(1,128)}) custom-call(bf16[1,128,9216]{2,1,0:T(8,128)(2,1)S(1)} %copy-done.1, f32[128,4608]{1,0:T(8,128)S(1)} %copy-done, bf16[128,4608]{1,0:T(8,128)(2,1)S(1)} %shard_map.99._), custom_call_target="tpu_custom_call" | custom-call | flops 3801088 | bytes 3801088 | tf_op jit(solution)/shard_map/pallas_call | solution.py:306
  7.8 0.0 copy-start.3
  7.8 0.3 collective-permute-start.2
  8.1 23.9 %collective-permute-done.got_ref = bf16[128,4608]{1,0:T(8,128)(2,1)S(1)} collective-permute-done((bf16[128,4608]{1,0:T(8,128)(2,1)S(1)}, bf16[128,4608]{1,0:T(8,128)(2,1)S(1)}, u32[]{:S(2)}, u32[]{:S(2)}) %collective-permute-start) | collective-permute-done | bytes 1179680 | tf_op jit(solution)/shard_map/ppermute | solution.py:329
  32.0 0.0 copy-done.4
  32.0 1.8 %shard_map.101 = (f32[128,4608]{1,0:T(8,128)S(1)}, f32[1,128]{1,0:T(1,128)S(1)}, bf16[16,48,128]{2,1,0:T(8,128)(2,1)S(1)}) custom-call(bf16[1,128,9216]{2,1,0:T(8,128)(2,1)S(1)} %copy-done.1, bf16[128,4608]{1,0:T(8,128)(2,1)S(1)} %collective-permute-done.got_ref, f32[1,128]{1,0:T(1,128)S(1)} %bitcast.7, f32[1,1]{1,0:T(1,128)} %get-tuple-element.26._.weight_ref), custom_call_target="tpu_custom_call" | custom-call | flops 4718592 | bytes 4718592 | tf_op jit(solution)/shard_map/pallas_call | solution.py:306
  33.8 14.3 %all_to_all.10.got_ref = bf16[16,48,128]{2,1,0:T(8,128)(2,1)S(1)} all-to-all(bf16[16,48,128]{2,1,0:T(8,128)(2,1)S(1)} %get-tuple-element.28), channel_id=1, replica_groups=mesh['dp'=2,'row'=16,'col'=4] {'row'}, dimensions={0} | all-to-all | bytes 393216 | tf_op jit(solution)/shard_map/all_to_all | solution.py:346
  48.1 0.0 copy-done.3
  48.1 1.6 %shard_map.102 = (f32[36,128]{1,0:T(8,128)}, f32[36,128]{1,0:T(8,128)S(1)}, f32[16,128]{1,0:T(8,128)S(1)}, bf16[128,4,128]{2,1,0:T(4,128)(2,1)S(1)}) custom-call(f32[128,4608]{1,0:T(8,128)S(1)} %get-tuple-element.27.grad_ref, bf16[16,48,128]{2,1,0:T(8,128)(2,1)S(1)} %all_to_all.10.got_ref, f32[1,128]{1,0:T(1,128)S(1)} %get-tuple-element.29.row_ref, ...), custom_call_target="tpu_custom_call" | custom-call | flops 2359296 | bytes 2359296 | tf_op jit(solution)/shard_map/pallas_call | solution.py:306
  49.8 19.9 %all_to_all.11.got_ref = bf16[128,4,128]{2,1,0:T(4,128)(2,1)S(1)} all-to-all(bf16[128,4,128]{2,1,0:T(4,128)(2,1)S(1)} %get-tuple-element.30), channel_id=1, replica_groups=mesh['dp'=2,'row'=16,'col'=4] {'dp','row','col'}, dimensions={0} | all-to-all | bytes 262144 | tf_op jit(solution)/shard_map/all_to_all | solution.py:355
  69.6 0.9 %shard_map.103 = (bf16[128,1152]{1,0:T(8,128)(2,1)S(1)}, f32[1,128]{1,0:T(1,128)}, f32[1,1]{1,0:T(1,128)}, f32[1,1]{1,0:T(1,128)}, f32[1,1]{1,0:T(1,128)}, /*ind...) custom-call(bf16[128,4,128]{2,1,0:T(4,128)(2,1)S(1)} %all_to_all.11.got_ref, f32[36,128]{1,0:T(8,128)S(1)} %get-tuple-element.31.cols_ref, ...), custom_call_target="tpu_custom_call" | custom-call | flops 1048576 | bytes 1048576 | tf_op jit(solution)/shard_map/pallas_call | solution.py:306
  70.5 2.2 %collective-permute-start.3 = (bf16[128,1152]{1,0:T(8,128)(2,1)S(1)}, bf16[128,1152]{1,0:T(8,128)(2,1)S(1)}, u32[]{:S(2)}, u32[]{:S(2)}) collective-permute-start(bf16[128,1152]{1,0:T(8,128)(2,1)S(1)} %get-tuple-element.38), channel_id=1, source_target_pairs={{0,64},{64,0},{1,65},{65,1},{2,66},{66,2},{3,67},{67,3},{4,68},{68... | collective-permute-start | bytes 884744 | tf_op jit(solution)/shard_map/ppermute | solution.py:366
  72.7 0.8 shard_map.105
  73.5 0.0 copy-start.2
  73.5 0.9 %collective-permute-start.1 = (bf16[128,768]{1,0:T(8,128)(2,1)S(1)}, bf16[128,768]{1,0:T(8,128)(2,1)S(1)}, u32[]{:S(2)}, u32[]{:S(2)}) collective-permute-start(bf16[128,768]{1,0:T(8,128)(2,1)S(1)} %shard_map.105), channel_id=1, source_target_pairs={{0,64},{64,0},{1,65},{65,1},{2,66},{66,2},{3,67},{67,3},{4,68},{68... | collective-permute-start | bytes 589832 | tf_op jit(solution)/shard_map/ppermute | solution.py:375
  74.4 3.8 %shard_map.104 = (f32[128,4608]{1,0:T(8,128)}, f32[128,4608]{1,0:T(8,128)}, bf16[128,9216]{1,0:T(8,128)(2,1)}) custom-call(f32[128,4608]{1,0:T(8,128)S(1)} %get-tuple-element.27.grad_ref, f32[128,4608]{1,0:T(8,128)S(1)} %copy-done, f32[128,128]{1,0:T(8,128)S(1)} %get-tuple-element.33.row_scale, f32[36,128]{1,0:T(8,128)S(1)} %get-tuple-element.34.col_scale, ...), custom_call_target="tpu_custom_call" | custom-call | flops 10616832 | bytes 10616832 | tf_op jit(solution)/shard_map/pallas_call | solution.py:306
  78.2 0.0 collective-permute-done.2.ahead_ref
  78.2 1.8 %collective-permute-done.3.late_ref = bf16[128,1152]{1,0:T(8,128)(2,1)S(1)} collective-permute-done((bf16[128,1152]{1,0:T(8,128)(2,1)S(1)}, bf16[128,1152]{1,0:T(8,128)(2,1)S(1)}, u32[]{:S(2)}, u32[]{:S(2)}) %collective-permute-start.3) | collective-permute-done | bytes 294944 | tf_op jit(solution)/shard_map/ppermute | solution.py:366
  80.1 0.0 copy-done.2
  80.1 2.3 %shard_map.106._ = bf16[128,9216]{1,0:T(8,128)(2,1)} custom-call(bf16[1,128,9216]{2,1,0:T(8,128)(2,1)S(1)} %copy-done.2, bf16[128,5632]{1,0:T(8,128)(2,1)S(1)} %collective-permute-done.2.ahead_ref, f32[128,128]{1,0:T(8,128)S(1)} %get-tuple-element.33.row_scale, ...), custom_call_target="tpu_custom_call", output_to_operand_aliasing={{}: (5, {})} | custom-call | flops 2883584 | bytes 2883584 | tf_op jit(solution)/shard_map/pallas_call | solution.py:306
  82.4 1.9 %collective-permute-done.1.got_ref = bf16[128,768]{1,0:T(8,128)(2,1)S(1)} collective-permute-done((bf16[128,768]{1,0:T(8,128)(2,1)S(1)}, bf16[128,768]{1,0:T(8,128)(2,1)S(1)}, u32[]{:S(2)}, u32[]{:S(2)}) %collective-permute-start.1) | collective-permute-done | bytes 196640 | tf_op jit(solution)/shard_map/ppermute | solution.py:375
  84.3 0.9 %shard_map.107 = bf16[128,9216]{1,0:T(8,128)(2,1)} custom-call(bf16[128,768]{1,0:T(8,128)(2,1)S(1)} %collective-permute-done.1.got_ref, bf16[128,9216]{1,0:T(8,128)(2,1)} %shard_map.106._), custom_call_target="tpu_custom_call", output_to_operand_aliasing={{}: (1, {})} | custom-call | flops 393216 | bytes 393216 | tf_op jit(solution)/shard_map/pallas_call | solution.py:306
Async XLA Ops:
  0.6 5.9 %copy-start = (f32[128,4608]{1,0:T(8,128)S(1)}, f32[128,4608]{1,0:T(8,128)}, u32[]{:S(2)}) copy-start(f32[128,4608]{1,0:T(8,128)} %params_ref.7) | copy-start | bytes 7077892
  0.6 1.8 %copy-start.1 = (bf16[1,128,9216]{2,1,0:T(8,128)(2,1)S(1)}, bf16[1,128,9216]{2,1,0:T(8,128)(2,1)}, u32[]{:S(2)}) copy-start(bf16[1,128,9216]{2,1,0:T(8,128)(2,1)} %grad_ref.5) | copy-start | bytes 7077892
  2.7 29.3 %copy-start.4 = (f32[128]{0:T(128)S(1)}, f32[128]{0:T(128)}, u32[]{:S(2)}) copy-start(f32[128]{0:T(128)} %param.6) | copy-start | bytes 1540
  2.7 29.2 %collective-permute-start = (bf16[128,4608]{1,0:T(8,128)(2,1)S(1)}, bf16[128,4608]{1,0:T(8,128)(2,1)S(1)}, u32[]{:S(2)}, u32[]{:S(2)}) collective-permute-start(bf16[128,4608]{1,0:T(8,128)(2,1)S(1)} %shard_map.99._), channel_id=1, source_target_pairs={{0,64},{64,0},{1,65},{65,1},{2,66},{66,2},{3,67},{67,3},{4,68},{68... | collective-permute-start | bytes 3538952 | tf_op jit(solution)/shard_map/ppermute | solution.py:329
  7.8 40.4 %copy-start.3 = (f32[9216]{0:T(1024)S(1)}, f32[9216]{0:T(1024)}, u32[]{:S(2)}) copy-start(f32[9216]{0:T(1024)} %param.7) | copy-start | bytes 110596
  7.8 70.4 %collective-permute-start.2 = (bf16[128,5632]{1,0:T(8,128)(2,1)S(1)}, bf16[128,5632]{1,0:T(8,128)(2,1)S(1)}, u32[]{:S(2)}, u32[]{:S(2)}) collective-permute-start(bf16[128,5632]{1,0:T(8,128)(2,1)S(1)} %get-tuple-element.37), channel_id=1, source_target_pairs={{0,64},{64,0},{1,65},{65,1},{2,66},{66,2},{3,67},{67,3},{4,68},{68... | collective-permute-start | bytes 4325384 | tf_op jit(solution)/shard_map/ppermute | solution.py:336
  70.5 9.6 %collective-permute-start.3 = (bf16[128,1152]{1,0:T(8,128)(2,1)S(1)}, bf16[128,1152]{1,0:T(8,128)(2,1)S(1)}, u32[]{:S(2)}, u32[]{:S(2)}) collective-permute-start(bf16[128,1152]{1,0:T(8,128)(2,1)S(1)} %get-tuple-element.38), channel_id=1, source_target_pairs={{0,64},{64,0},{1,65},{65,1},{2,66},{66,2},{3,67},{67,3},{4,68},{68... | collective-permute-start | bytes 884744 | tf_op jit(solution)/shard_map/ppermute | solution.py:366
  73.5 6.6 %copy-start.2 = (bf16[1,128,9216]{2,1,0:T(8,128)(2,1)S(1)}, bf16[1,128,9216]{2,1,0:T(8,128)(2,1)}, u32[]{:S(2)}) copy-start(bf16[1,128,9216]{2,1,0:T(8,128)(2,1)} %grad_ref.5) | copy-start | bytes 7077892
  73.5 10.8 %collective-permute-start.1 = (bf16[128,768]{1,0:T(8,128)(2,1)S(1)}, bf16[128,768]{1,0:T(8,128)(2,1)S(1)}, u32[]{:S(2)}, u32[]{:S(2)}) collective-permute-start(bf16[128,768]{1,0:T(8,128)(2,1)S(1)} %shard_map.105), channel_id=1, source_target_pairs={{0,64},{64,0},{1,65},{65,1},{2,66},{66,2},{3,67},{67,3},{4,68},{68... | collective-permute-start | bytes 589832 | tf_op jit(solution)/shard_map/ppermute | solution.py:375

commit v6 on v5

v6 whole, which is shorter than its diff:
```python
import functools

import jax
import jax.numpy as jnp
from jax import lax
from jax.experimental import pallas as pl
from jax.experimental.pallas import tpu as pltpu
from jax.sharding import PartitionSpec as P

R = 2048
C = 36864
STEP = 10
DECAY = 1.0 - STEP ** (-0.8)
RELATIVE = min(0.01, STEP ** (-0.5))
LANES = 128
SWAP = [(0, 1), (1, 0)]
BLOCK = 256
WIDE = 1536
EARLY = 11
LATE = (7,)
VMEM_LIMIT = 24 << 20
f32, bf16 = jnp.float32, jnp.bfloat16
shape = jax.ShapeDtypeStruct


def down(row):
    return jnp.broadcast_to(row, (LANES, LANES)).T


def flat(acc):
    return jnp.sum(acc.T, axis=0, keepdims=True)


def split(value, count):
    parts = []
    for _ in range(count):
        parts.append(value.astype(bf16).astype(f32))
        value = value - parts[-1]
    return parts


def lanes(value):
    at = lax.broadcasted_iota(jnp.int32, (1, LANES), 1)
    row = jnp.zeros((1, LANES), f32)
    for i, part in enumerate(split(jnp.broadcast_to(value, (1, LANES)), 3)):
        row = jnp.where(at == i, part, row)
    return row


def tile(at):
    return slice(at * LANES, (at + 1) * LANES)


def span(start, count):
    return pl.ds(pl.multiple_of(start, LANES), count)


def begin(*copies):
    copies = [pltpu.make_async_copy(*copy) for copy in copies]
    for copy in copies:
        copy.start()
    return copies


def steps(width):
    return [(start, WIDE) for start in range(0, width, WIDE)]


def half_kernel(grad_ref, out_ref, buf, in_sems, out_sems):
    width = buf.shape[1]
    other = (1 - lax.axis_index("dp")) * width
    pieces = steps(width)
    ins = [
        begin((grad_ref.at[0, :, span(other + s, n)], buf.at[:, s : s + n], in_sems.at[i]))[0]
        for i, (s, n) in enumerate(pieces)
    ]
    outs = []
    for i, (s, n) in enumerate(pieces):
        ins[i].wait()
        outs += begin((buf.at[:, s : s + n], out_ref.at[:, s : s + n], out_sems.at[i]))
    for copy in outs:
        copy.wait()


def prepare_kernel(grad_ref, params_ref, _, ahead_ref, weight_ref, params, parts, values, sems, out_sems):
    width, early = params.shape[1], parts.shape[1]
    mine = lax.axis_index("dp") * width
    pieces = steps(width)
    grad = begin((grad_ref.at[0, :, span(mine, early)], parts, sems.at[len(pieces)]))[0]
    ins = [
        begin((params_ref.at[:, s : s + n], params.at[:, s : s + n], sems.at[i]))[0] for i, (s, n) in enumerate(pieces)
    ]
    acc = jnp.zeros((LANES, LANES), f32)
    for i, (s, n) in enumerate(pieces):
        ins[i].wait()
        for t in range(s // LANES, (s + n) // LANES):
            value = params[:, tile(t)]
            acc = acc + value * value
            if t < early // LANES:
                values[:, tile(t)] = value.astype(bf16)
    grad.wait()
    outs = begin(
        (parts, ahead_ref.at[:, 0:early], out_sems.at[0]), (values, ahead_ref.at[:, early : 2 * early], out_sems.at[1])
    )
    weight_ref[...] = jnp.sum(jnp.sum(acc, axis=0, keepdims=True), axis=1, keepdims=True)
    for copy in outs:
        copy.wait()


def sums_kernel(grad_parts_ref, got, old_rows_ref, weight_ref, grad, row_ref, sent_ref, mine, cols, sems):
    width = grad.shape[1]
    first = lax.axis_index("dp") * width
    pieces = steps(width)
    ins = [
        begin((grad_parts_ref.at[0, :, span(first + s, n)], mine.at[:, s : s + n], sems.at[i]))[0]
        for i, (s, n) in enumerate(pieces)
    ]
    cols[...] = jnp.zeros_like(cols)
    acc = jnp.zeros((LANES, LANES), f32)
    for i, (s, n) in enumerate(pieces):
        ins[i].wait()
        for t in range(s // LANES, (s + n) // LANES):
            g = mine[:, tile(t)].astype(f32) + got[:, tile(t)].astype(f32)
            grad[:, tile(t)] = g
            squares = g * g + 1e-30
            acc = acc + squares
            cols[t : t + 1, :] = jnp.sum(squares, axis=0, keepdims=True)
    row_ref[...] = flat(acc)
    free = width // LANES
    for i, part in enumerate(split(old_rows_ref[...], 2) + [lanes(weight_ref[...])]):
        cols[free + i : free + i + 1, :] = part
    sent = cols[...].astype(bf16)
    for peer in range(sent_ref.shape[0]):
        sent_ref[peer] = sent


def moments_kernel(
    grad, got_ref, row_ref, old_cols_ref, new_cols_ref, copy_ref, old_rows_ref, sent_ref, inv_cols, scale,
):
    height = grad.shape[1] // LANES
    totals = got_ref[0].astype(f32)
    for peer in range(1, got_ref.shape[0]):
        totals = totals + got_ref[peer].astype(f32)
    for peer in range(got_ref.shape[0]):
        rows = got_ref[peer].astype(f32)
        old_rows_ref[peer : peer + 1, :] = rows[height : height + 1] + rows[height + 1 : height + 2]
    weight = jnp.sum(totals[height + 2 : height + 3], axis=1, keepdims=True)
    old_cols = jnp.where(lax.axis_index("dp") == 0, old_cols_ref[:height], old_cols_ref[height:])
    new_cols = DECAY * old_cols + (1.0 - DECAY) * (totals[:height] / R)
    new_cols_ref[...] = new_cols
    copy_ref[...] = new_cols
    inv_cols[...] = 1.0 / new_cols
    acc = jnp.zeros((LANES, LANES), f32)
    for t in range(height):
        g = grad[:, tile(t)]
        acc = acc + g * g * inv_cols[t : t + 1, :]
    scale[...] = lax.rsqrt(new_cols)
    index = lax.axis_index("row")
    second = jnp.where(index == 15, lanes(weight), scale[pl.ds(16 + index, 1), :])
    at = lax.broadcasted_iota(jnp.int32, (4, LANES), 0)
    value = jnp.zeros((4, LANES), f32)
    for i, row in enumerate([row_ref[...], flat(acc), scale[pl.ds(index, 1), :], second]):
        value = jnp.where(at == i, jnp.broadcast_to(row, (4, LANES)), value)
    value = value.astype(bf16)
    sent_ref[...] = jnp.broadcast_to(value[None], sent_ref.shape)


def weights_piece(grad, params, out_ref, row_scale, col_scale, step_size, first):
    for t in range(params.shape[1] // LANES):
        update = grad[:, tile(first + t)] * row_scale * col_scale[first + t : first + t + 1, :]
        out_ref[:, tile(t)] = (params[:, tile(t)] - step_size * update).astype(bf16)


def first_weights_kernel(
    got_ref, cols_ref, old_rows_ref, grad, params_ref,
    out_ref, rows_ref, clip_ref, scale_ref, step_ref, row_scale, col_scale, early_ref, params, all_rows, sem,
):
    start, count = EARLY * BLOCK, params.shape[1]
    (params_copy,) = begin((params_ref.at[:, start : start + count], params, sem))
    update_sum = jnp.zeros((1, LANES), f32)
    row_sum = jnp.zeros((1, LANES), f32)
    for block in range(16):
        got = None
        for d in range(2):
            for c in range(4):
                term = got_ref[d * 64 + block * 4 + c].astype(f32)
                got = term if got is None else got + term
        rows = DECAY * old_rows_ref[block : block + 1, :] + (1.0 - DECAY) * (got[0:1] / C)
        all_rows[block : block + 1, :] = rows
        update_sum = update_sum + got[1:2] / rows
        row_sum = row_sum + rows
        weight_sum = got[3:4]
        theirs = got_ref[(1 - lax.axis_index("dp")) * 64 + block * 4 + lax.axis_index("col")].astype(f32)
        early_ref[block : block + 1, :] = theirs[2:3]
        early_ref[16 + block : 17 + block, :] = theirs[3:4]
    row_mean = jnp.sum(row_sum, axis=1, keepdims=True) / R
    rows = all_rows[pl.ds(lax.axis_index("row"), 1), :]
    rows_ref[...] = rows
    row_scale[...] = down(lax.rsqrt(rows / row_mean))
    col_scale[...] = lax.rsqrt(cols_ref[...])
    update_mean = jnp.sum(update_sum, axis=1, keepdims=True) * row_mean / (R * C)
    weight_mean = jnp.sum(weight_sum, axis=1, keepdims=True) / (R * C)
    clip_factor = jnp.maximum(1.0, jnp.sqrt(update_mean))
    param_scale = jnp.maximum(0.001, jnp.sqrt(weight_mean))
    clip_ref[...] = clip_factor
    scale_ref[...] = param_scale
    step_size = RELATIVE * param_scale / clip_factor
    step_ref[...] = step_size
    params_copy.wait()
    weights_piece(grad, params, out_ref, row_scale[...], col_scale, step_size, start // LANES)


def weights_kernel(start, grad, params_ref, row_scale, col_scale, step_ref, out_ref, params, sem):
    (copy,) = begin((params_ref.at[:, start : start + params.shape[1]], params, sem))
    copy.wait()
    weights_piece(grad, params, out_ref, row_scale[...], col_scale, step_ref[...], start // LANES)


def params_kernel(
    grad, params_ref, row_scale, col_scale, step_ref,
    new_ref, update_ref, weights_ref, params, update, new, weights, sems, out_sems,
):
    width = grad.shape[1]
    mine = lax.axis_index("dp") * width
    pieces = steps(width)
    ins = [
        begin((params_ref.at[:, s : s + n], params.at[:, s : s + n], sems.at[i]))[0] for i, (s, n) in enumerate(pieces)
    ]
    across, step_size = row_scale[...], step_ref[...]
    outs = []
    for i, (s, n) in enumerate(pieces):
        ins[i].wait()
        for t in range(s // LANES, (s + n) // LANES):
            value = grad[:, tile(t)] * across * col_scale[t : t + 1, :]
            moved = params[:, tile(t)] - step_size * value
            update[:, tile(t)] = value
            new[:, tile(t)] = moved
            weights[:, tile(t)] = moved.astype(bf16)
        outs += begin(
            (update.at[:, s : s + n], update_ref.at[:, s : s + n], out_sems.at[3 * i]),
            (new.at[:, s : s + n], new_ref.at[:, s : s + n], out_sems.at[3 * i + 1]),
            (weights.at[:, s : s + n], weights_ref.at[:, span(mine + s, n)], out_sems.at[3 * i + 2]),
        )
    for copy in outs:
        copy.wait()


def early_kernel(width, grad_ref, ahead_ref, row_scale, scale, step_ref, _, out_ref, mine, got, out, sems, out_sem):
    count = mine.shape[1]
    first = (1 - lax.axis_index("dp")) * width
    ins = begin((grad_ref.at[0, :, span(first, count)], mine, sems.at[0]), (ahead_ref, got, sems.at[1]))
    across, step_size = row_scale[...], step_ref[...]
    for copy in ins:
        copy.wait()
    for t in range(count // LANES):
        g = mine[:, tile(t)].astype(f32) + got[:, tile(t)].astype(f32)
        update = g * across * scale[t : t + 1, :]
        out[:, tile(t)] = (got[:, tile(count // LANES + t)].astype(f32) - step_size * update).astype(bf16)
    (copy,) = begin((out, out_ref.at[:, span(first, count)], out_sem))
    copy.wait()


def place_kernel(start, width, got, _, out_ref, sem):
    first = (1 - lax.axis_index("dp")) * width + start
    (copy,) = begin((got, out_ref.at[:, span(first, got.shape[1])], sem))
    copy.wait()


HBM, VMEM = pltpu.HBM, pltpu.VMEM
dma = pltpu.SemaphoreType.DMA


def call(kernel, ins, outs, scratch, args, nbytes, aliases=None, limit=VMEM_LIMIT):
    return pl.pallas_call(
        kernel,
        in_specs=[pl.BlockSpec(memory_space=space) for space in ins],
        out_specs=[pl.BlockSpec(memory_space=space) for space, _ in outs],
        out_shape=[out for _, out in outs],
        scratch_shapes=list(scratch),
        input_output_aliases=aliases or {},
        cost_estimate=pl.CostEstimate(flops=nbytes, bytes_accessed=nbytes, transcendentals=0),
        compiler_params=pltpu.CompilerParams(vmem_limit_bytes=limit),
    )(*args)


def shards(params, grad_parts, row_moment, col_moment):
    rows, width = params.shape
    height = width // LANES
    padded = -(-height // 16) * 16
    early = EARLY * BLOCK
    count = len(steps(width))

    (outgoing,) = call(
        half_kernel, [HBM], [(HBM, shape((rows, width), bf16))],
        [VMEM((rows, width), bf16), dma((count,)), dma((count,))], (grad_parts,), 4 * rows * width,
    )
    got = lax.ppermute(outgoing, "dp", SWAP)
    ahead, weight_part = call(
        prepare_kernel, [HBM, HBM, HBM],
        [(HBM, shape((rows, 2 * early), bf16)), (VMEM, shape((1, 1), f32))],
        [VMEM((rows, width), f32), VMEM((rows, early), bf16), VMEM((rows, early), bf16), dma((count + 1,)), dma((2,))],
        (grad_parts, params, outgoing), 4 * rows * (width + early),
    )
    ahead = lax.ppermute(ahead, "dp", SWAP)

    gradient, row_part, sent = call(
        sums_kernel, [HBM, VMEM, VMEM, VMEM],
        [(VMEM, shape((rows, width), f32)), (VMEM, shape((1, rows), f32)),
         (VMEM, shape((16, padded, LANES), bf16))],
        [VMEM((rows, width), bf16), VMEM((padded, LANES), f32), dma((count,))],
        (grad_parts, got, row_moment.reshape(1, rows), weight_part), 8 * rows * width,
    )
    col_parts = lax.all_to_all(sent, "row", 0, 0)
    new_cols, cols_copy, old_rows, sent = call(
        moments_kernel, [VMEM] * 4,
        [(VMEM, shape((height, LANES), f32)), (VMEM, shape((height, LANES), f32)),
         (VMEM, shape((16, LANES), f32)), (VMEM, shape((128, 4, LANES), bf16))],
        [VMEM((height, LANES), f32)] * 2, (gradient, col_parts, row_part, col_moment.reshape(2 * height, LANES)),
        4 * rows * width,
    )
    parts = lax.all_to_all(sent, ("dp", "row", "col"), 0, 0)

    n = LATE[0] * BLOCK
    out, new_rows, clip_factor, param_scale, step_size, row_scale, col_scale, early_scale = call(
        first_weights_kernel, [VMEM, VMEM, VMEM, VMEM, HBM],
        [(VMEM, shape((rows, n), bf16)), (VMEM, shape((1, rows), f32)),
         (VMEM, shape((1, 1), f32)), (VMEM, shape((1, 1), f32)), (VMEM, shape((1, 1), f32)),
         (VMEM, shape((rows, LANES), f32)), (VMEM, shape((height, LANES), f32)), (VMEM, shape((32, LANES), f32))],
        [VMEM((rows, n), f32), VMEM((16, LANES), f32), dma],
        (parts, cols_copy, old_rows, gradient, params), 8 * rows * n,
    )
    late = [lax.ppermute(out, "dp", SWAP)]
    start = early + n
    for blocks in LATE[1:]:
        n = blocks * BLOCK
        (out,) = call(
            functools.partial(weights_kernel, start), [VMEM, HBM, VMEM, VMEM, VMEM],
            [(VMEM, shape((rows, n), bf16))], [VMEM((rows, n), f32), dma],
            (gradient, params, row_scale, col_scale, step_size), 8 * rows * n,
        )
        late.append(lax.ppermute(out, "dp", SWAP))
        start += n

    out_shape = shape((rows, 2 * width), bf16)
    new_params, update, new_weights = call(
        params_kernel, [VMEM, HBM, VMEM, VMEM, VMEM],
        [(HBM, shape((rows, width), f32)), (HBM, shape((rows, width), f32)), (HBM, out_shape)],
        [VMEM((rows, width), f32)] * 3 + [VMEM((rows, width), bf16), dma((count,)), dma((3 * count,))],
        (gradient, params, row_scale, col_scale, step_size), 18 * rows * width,
    )
    (new_weights,) = call(
        functools.partial(early_kernel, width), [HBM, HBM, VMEM, VMEM, VMEM, HBM], [(HBM, out_shape)],
        [VMEM((rows, early), bf16), VMEM((rows, 2 * early), bf16), VMEM((rows, early), bf16), dma((2,)), dma],
        (grad_parts, ahead, row_scale, early_scale, step_size, new_weights), 8 * rows * early, {5: 0},
    )
    start = early
    for blocks, values in zip(LATE, late):
        n = blocks * BLOCK
        (new_weights,) = call(
            functools.partial(place_kernel, start, width), [VMEM, HBM], [(HBM, out_shape)],
            [dma], (values, new_weights), 4 * rows * n, {1: 0},
        )
        start += n
    return (
        new_params, new_weights, new_rows.reshape(rows), new_cols.reshape(width), update,
        clip_factor.reshape(()), param_scale.reshape(()),
    )


def solution(mesh):
    in_specs = (P("row", ("col", "dp")), P("dp", "row", "col"), P("row"), P("col"))
    out_specs = (
        P("row", ("col", "dp")),
        P("row", "col"),
        P("row"),
        P(("col", "dp")),
        P("row", ("col", "dp")),
        P(),
        P(),
    )
    return jax.shard_map(shards, mesh=mesh, in_specs=in_specs, out_specs=out_specs, check_vma=False)
```

time: 85.4 us -> 84.2 us (0.986)
  Pallas kernels: 13.6 us -> 11.6 us
    ppermute x1, waiting for transfers between devices: 1.84 us -> 4.46 us  [shards(): late = [lax.ppermute(out, 'dp', SWAP)]]
    pallas_call x9 -> x8, Pallas kernels: 13.6 us -> 11.6 us  [call(): pl.pallas_call(kernel, in_specs=[pl.BlockSpec(memory_space=space) for spa...]
    ppermute x1 -> x0, waiting for transfers between devices: 1.9 us -> none  [shards(): late.append(lax.ppermute(out, 'dp', SWAP))]
    ppermute x1, waiting for transfers between devices: 23.9 us -> 22.8 us  [shards(): got = lax.ppermute(outgoing, 'dp', SWAP)]
    ppermute x1, starting transfers between devices: 0.26 us -> 1.38 us  [shards(): ahead = lax.ppermute(ahead, 'dp', SWAP)]
    ppermute x1 -> x0, starting transfers between devices: 0.92 us -> none  [shards(): late.append(lax.ppermute(out, 'dp', SWAP))]
  transfers between devices with their start and end apart: 4 -> 3, of which waited for: 3 -> 2; matrix products, arithmetic and copies ran while one was open for 0% -> 0% of each run, Pallas kernels for 15% -> 13%
where the time goes in v6:
time: 84.2 us; the launch traced here: 84 us
  blocking collectives  34.9 us (41%)
  waiting for transfers between devices  27.3 us (32%)
  Pallas kernels  11.6 us (14%)
  starting transfers between devices  7.88 us (9%)
  local copies, waits for them, and re-layouts  1.68 us (2%)
    ppermute x1, waiting for transfers between devices, shards(): got = lax.ppermute(outgoing, 'dp', SWAP)  22.8 us
    all_to_all x1, blocking collectives, shards(): parts = lax.all_to_all(sent, ('dp', 'row', 'col'), 0, 0)  20.5 us
    all_to_all x1, blocking collectives, shards(): col_parts = lax.all_to_all(sent, 'row', 0, 0)  14.3 us
    pallas_call x8, Pallas kernels, call(): pl.pallas_call(kernel, in_specs=[pl.BlockSpec(memory_space=space) for spa...  11.6 us
    ppermute x1, waiting for transfers between devices, shards(): late = [lax.ppermute(out, 'dp', SWAP)]  4.46 us
    ppermute x1, starting transfers between devices, shards(): got = lax.ppermute(outgoing, 'dp', SWAP)  3.82 us
    ppermute x1, starting transfers between devices, shards(): late = [lax.ppermute(out, 'dp', SWAP)]  2.67 us
  transfers between devices with their start and end apart: 3, of which 2 were waited for; matrix products, arithmetic and copies ran while one was open for 0% of the time, Pallas kernels for 13%

profile of v6, /device:TPU:1, one launch (start us, length us, event | category | flops | bytes accessed | tf_op | source)
XLA Modules:
  0.0 84.0 jit_solution(6836364265311783933)
XLA Ops:
  0.6 0.0 copy-start
  0.6 1.7 %copy-done = bf16[1,128,9216]{2,1,0:T(8,128)(2,1)S(1)} copy-done((bf16[1,128,9216]{2,1,0:T(8,128)(2,1)S(1)}, bf16[1,128,9216]{2,1,0:T(8,128)(2,1)}, u32[]{:S(2)}) %copy-start) | copy-done | bytes 2359320
  2.3 0.0 copy-start.2
  2.3 0.3 shard_map.99._
  2.6 0.0 copy-start.4
  2.6 3.8 %collective-permute-start = (bf16[128,4608]{1,0:T(8,128)(2,1)S(1)}, bf16[128,4608]{1,0:T(8,128)(2,1)S(1)}, u32[]{:S(2)}, u32[]{:S(2)}) collective-permute-start(bf16[128,4608]{1,0:T(8,128)(2,1)S(1)} %shard_map.99._), channel_id=1, source_target_pairs={{0,64},{64,0},{1,65},{65,1},{2,66},{66,2},{3,67},{67,3},{4,68},{68... | collective-permute-start | bytes 3538952 | tf_op jit(solution)/shard_map/ppermute | solution.py:297
  6.4 0.0 copy-done.2
  6.4 1.2 %shard_map.100 = (bf16[128,5632]{1,0:T(8,128)(2,1)S(1)}, f32[1,1]{1,0:T(1,128)}) custom-call(bf16[1,128,9216]{2,1,0:T(8,128)(2,1)S(1)} %copy-done, f32[128,4608]{1,0:T(8,128)S(1)} %copy-done.2, bf16[128,4608]{1,0:T(8,128)(2,1)S(1)} %shard_map.99._), custom_call_target="tpu_custom_call" | custom-call | flops 3801088 | bytes 3801088 | tf_op jit(solution)/shard_map/pallas_call | solution.py:274
  7.6 0.0 copy-start.3
  7.6 1.4 %collective-permute-start.2 = (bf16[128,5632]{1,0:T(8,128)(2,1)S(1)}, bf16[128,5632]{1,0:T(8,128)(2,1)S(1)}, u32[]{:S(2)}, u32[]{:S(2)}) collective-permute-start(bf16[128,5632]{1,0:T(8,128)(2,1)S(1)} %get-tuple-element.39), channel_id=1, source_target_pairs={{0,64},{64,0},{1,65},{65,1},{2,66},{66,2},{3,67},{67,3},{4,68},{68... | collective-permute-start | bytes 4325384 | tf_op jit(solution)/shard_map/ppermute | solution.py:304
  9.0 22.8 %collective-permute-done.got = bf16[128,4608]{1,0:T(8,128)(2,1)S(1)} collective-permute-done((bf16[128,4608]{1,0:T(8,128)(2,1)S(1)}, bf16[128,4608]{1,0:T(8,128)(2,1)S(1)}, u32[]{:S(2)}, u32[]{:S(2)}) %collective-permute-start) | collective-permute-done | bytes 1179680 | tf_op jit(solution)/shard_map/ppermute | solution.py:297
  31.8 0.0 copy-done.4
  31.8 1.5 %shard_map.101 = (f32[128,4608]{1,0:T(8,128)S(1)}, f32[1,128]{1,0:T(1,128)S(1)}, bf16[16,48,128]{2,1,0:T(8,128)(2,1)S(1)}) custom-call(bf16[1,128,9216]{2,1,0:T(8,128)(2,1)S(1)} %copy-done, bf16[128,4608]{1,0:T(8,128)(2,1)S(1)} %collective-permute-done.got, f32[1,128]{1,0:T(1,128)S(1)} %bitcast.7, f32[1,1]{1,0:T(1,128)} %get-tuple-element.27.weight_ref), custom_call_target="tpu_custom_call" | custom-call | flops 4718592 | bytes 4718592 | tf_op jit(solution)/shard_map/pallas_call | solution.py:274
  33.3 14.3 %all_to_all.10.got_ref = bf16[16,48,128]{2,1,0:T(8,128)(2,1)S(1)} all-to-all(bf16[16,48,128]{2,1,0:T(8,128)(2,1)S(1)} %get-tuple-element.29), channel_id=1, replica_groups=mesh['dp'=2,'row'=16,'col'=4] {'row'}, dimensions={0} | all-to-all | bytes 393216 | tf_op jit(solution)/shard_map/all_to_all | solution.py:313
  47.6 0.0 copy-done.3
  47.6 0.9 %shard_map.102 = (f32[36,128]{1,0:T(8,128)}, f32[36,128]{1,0:T(8,128)S(1)}, f32[16,128]{1,0:T(8,128)S(1)}, bf16[128,4,128]{2,1,0:T(4,128)(2,1)S(1)}) custom-call(f32[128,4608]{1,0:T(8,128)S(1)} %get-tuple-element.28.grad, bf16[16,48,128]{2,1,0:T(8,128)(2,1)S(1)} %all_to_all.10.got_ref, f32[1,128]{1,0:T(1,128)S(1)} %get-tuple-element.30.row_ref, ...), custom_call_target="tpu_custom_call" | custom-call | flops 2359296 | bytes 2359296 | tf_op jit(solution)/shard_map/pallas_call | solution.py:274
  48.5 20.5 %all_to_all.11.got_ref = bf16[128,4,128]{2,1,0:T(4,128)(2,1)S(1)} all-to-all(bf16[128,4,128]{2,1,0:T(4,128)(2,1)S(1)} %get-tuple-element.31), channel_id=1, replica_groups=mesh['dp'=2,'row'=16,'col'=4] {'dp','row','col'}, dimensions={0} | all-to-all | bytes 262144 | tf_op jit(solution)/shard_map/all_to_all | solution.py:321
  69.1 0.9 %shard_map.103 = (bf16[128,1792]{1,0:T(8,128)(2,1)S(1)}, f32[1,128]{1,0:T(1,128)}, f32[1,1]{1,0:T(1,128)}, f32[1,1]{1,0:T(1,128)}, f32[1,1]{1,0:T(1,128)}, /*ind...) custom-call(bf16[128,4,128]{2,1,0:T(4,128)(2,1)S(1)} %all_to_all.11.got_ref, ...), custom_call_target="tpu_custom_call" | custom-call | flops 1835008 | bytes 1835008 | tf_op jit(solution)/shard_map/pallas_call | solution.py:274
  69.9 2.7 %collective-permute-start.1 = (bf16[128,1792]{1,0:T(8,128)(2,1)S(1)}, bf16[128,1792]{1,0:T(8,128)(2,1)S(1)}, u32[]{:S(2)}, u32[]{:S(2)}) collective-permute-start(bf16[128,1792]{1,0:T(8,128)(2,1)S(1)} %get-tuple-element.38), channel_id=1, source_target_pairs={{0,64},{64,0},{1,65},{65,1},{2,66},{66,2},{3,67},{67,3},{4,68},{68... | collective-permute-start | bytes 1376264 | tf_op jit(solution)/shard_map/ppermute | solution.py:332
  72.6 0.0 copy-start.1
  72.6 3.8 %shard_map.104 = (f32[128,4608]{1,0:T(8,128)}, f32[128,4608]{1,0:T(8,128)}, bf16[128,9216]{1,0:T(8,128)(2,1)}) custom-call(f32[128,4608]{1,0:T(8,128)S(1)} %get-tuple-element.28.grad, f32[128,4608]{1,0:T(8,128)S(1)} %copy-done.2, f32[128,128]{1,0:T(8,128)S(1)} %get-tuple-element.34.row_scale, f32[36,128]{1,0:T(8,128)S(1)} %get-tuple-element.35.col_scale, ...), custom_call_target="tpu_custom_call" | custom-call | flops 10616832 | bytes 10616832 | tf_op jit(solution)/shard_map/pallas_call | solution.py:274
  76.4 0.0 collective-permute-done.2.ahead_ref
  76.5 0.0 copy-done.1
  76.5 2.3 %shard_map.105._ = bf16[128,9216]{1,0:T(8,128)(2,1)} custom-call(bf16[1,128,9216]{2,1,0:T(8,128)(2,1)S(1)} %copy-done.1, bf16[128,5632]{1,0:T(8,128)(2,1)S(1)} %collective-permute-done.2.ahead_ref, f32[128,128]{1,0:T(8,128)S(1)} %get-tuple-element.34.row_scale, f32[32,128]{1,0:T(8,128)S(1)} %get-tuple-element.40.scale, ...), custom_call_target="tpu_custom_call", output_to_operand_aliasing={{}: (5, {})} | custom-call | flops 2883584 | bytes 2883584 | tf_op jit(solution)/shard_map/pallas_call | solution.py:274
  78.8 4.5 %collective-permute-done.1.got = bf16[128,1792]{1,0:T(8,128)(2,1)S(1)} collective-permute-done((bf16[128,1792]{1,0:T(8,128)(2,1)S(1)}, bf16[128,1792]{1,0:T(8,128)(2,1)S(1)}, u32[]{:S(2)}, u32[]{:S(2)}) %collective-permute-start.1) | collective-permute-done | bytes 458784 | tf_op jit(solution)/shard_map/ppermute | solution.py:332
  83.2 0.8 shard_map.106
Async XLA Ops:
  0.6 1.7 %copy-start = (bf16[1,128,9216]{2,1,0:T(8,128)(2,1)S(1)}, bf16[1,128,9216]{2,1,0:T(8,128)(2,1)}, u32[]{:S(2)}) copy-start(bf16[1,128,9216]{2,1,0:T(8,128)(2,1)} %grad_ref.5) | copy-start | bytes 7077892
  2.3 4.1 %copy-start.2 = (f32[128,4608]{1,0:T(8,128)S(1)}, f32[128,4608]{1,0:T(8,128)}, u32[]{:S(2)}) copy-start(f32[128,4608]{1,0:T(8,128)} %params_ref.5) | copy-start | bytes 7077892
  2.6 29.3 %copy-start.4 = (f32[128]{0:T(128)S(1)}, f32[128]{0:T(128)}, u32[]{:S(2)}) copy-start(f32[128]{0:T(128)} %param.6) | copy-start | bytes 1540
  2.6 29.2 %collective-permute-start = (bf16[128,4608]{1,0:T(8,128)(2,1)S(1)}, bf16[128,4608]{1,0:T(8,128)(2,1)S(1)}, u32[]{:S(2)}, u32[]{:S(2)}) collective-permute-start(bf16[128,4608]{1,0:T(8,128)(2,1)S(1)} %shard_map.99._), channel_id=1, source_target_pairs={{0,64},{64,0},{1,65},{65,1},{2,66},{66,2},{3,67},{67,3},{4,68},{68... | collective-permute-start | bytes 3538952 | tf_op jit(solution)/shard_map/ppermute | solution.py:297
  7.6 40.0 %copy-start.3 = (f32[9216]{0:T(1024)S(1)}, f32[9216]{0:T(1024)}, u32[]{:S(2)}) copy-start(f32[9216]{0:T(1024)} %param.7) | copy-start | bytes 110596
  7.6 68.8 %collective-permute-start.2 = (bf16[128,5632]{1,0:T(8,128)(2,1)S(1)}, bf16[128,5632]{1,0:T(8,128)(2,1)S(1)}, u32[]{:S(2)}, u32[]{:S(2)}) collective-permute-start(bf16[128,5632]{1,0:T(8,128)(2,1)S(1)} %get-tuple-element.39), channel_id=1, source_target_pairs={{0,64},{64,0},{1,65},{65,1},{2,66},{66,2},{3,67},{67,3},{4,68},{68... | collective-permute-start | bytes 4325384 | tf_op jit(solution)/shard_map/ppermute | solution.py:304
  69.9 13.3 %collective-permute-start.1 = (bf16[128,1792]{1,0:T(8,128)(2,1)S(1)}, bf16[128,1792]{1,0:T(8,128)(2,1)S(1)}, u32[]{:S(2)}, u32[]{:S(2)}) collective-permute-start(bf16[128,1792]{1,0:T(8,128)(2,1)S(1)} %get-tuple-element.38), channel_id=1, source_target_pairs={{0,64},{64,0},{1,65},{65,1},{2,66},{66,2},{3,67},{67,3},{4,68},{68... | collective-permute-start | bytes 1376264 | tf_op jit(solution)/shard_map/ppermute | solution.py:332
  72.6 3.8 %copy-start.1 = (bf16[1,128,9216]{2,1,0:T(8,128)(2,1)S(1)}, bf16[1,128,9216]{2,1,0:T(8,128)(2,1)}, u32[]{:S(2)}) copy-start(bf16[1,128,9216]{2,1,0:T(8,128)(2,1)} %grad_ref.5) | copy-start | bytes 7077892

commit v7 on v6

--- a/solution.py
+++ b/solution.py
@@ -66,19 +66,14 @@
     return [(start, WIDE) for start in range(0, width, WIDE)]
 
 
-def half_kernel(grad_ref, out_ref, buf, in_sems, out_sems):
-    width = buf.shape[1]
+def half_kernel(grad_ref, out_ref, sems):
+    width = out_ref.shape[1]
     other = (1 - lax.axis_index("dp")) * width
-    pieces = steps(width)
-    ins = [
-        begin((grad_ref.at[0, :, span(other + s, n)], buf.at[:, s : s + n], in_sems.at[i]))[0]
-        for i, (s, n) in enumerate(pieces)
+    copies = [
+        begin((grad_ref.at[0, :, span(other + s, n)], out_ref.at[:, s : s + n], sems.at[i]))[0]
+        for i, (s, n) in enumerate(steps(width))
     ]
-    outs = []
-    for i, (s, n) in enumerate(pieces):
-        ins[i].wait()
-        outs += begin((buf.at[:, s : s + n], out_ref.at[:, s : s + n], out_sems.at[i]))
-    for copy in outs:
+    for copy in copies:
         copy.wait()
 
 
@@ -291,8 +286,8 @@
     count = len(steps(width))
 
     (outgoing,) = call(
-        half_kernel, [HBM], [(HBM, shape((rows, width), bf16))],
-        [VMEM((rows, width), bf16), dma((count,)), dma((count,))], (grad_parts,), 4 * rows * width,
+        half_kernel, [HBM], [(VMEM, shape((rows, width), bf16))], [dma((count,))],
+        (pltpu.with_memory_space_constraint(grad_parts, HBM),), 4 * rows * width,
     )
     got = lax.ppermute(outgoing, "dp", SWAP)
     ahead, weight_part = call(

time: 84.2 us -> 83.7 us (level)
  Pallas kernels: 11.6 us -> 12.6 us
    pallas_call x8, Pallas kernels: 11.6 us -> 12.6 us  [call(): pl.pallas_call(kernel, in_specs=[pl.BlockSpec(memory_space=space) for spa...]
    ppermute x1, waiting for transfers between devices: 22.8 us -> 21.9 us  [shards(): got = lax.ppermute(outgoing, 'dp', SWAP)]
  transfers between devices with their start and end apart: 3 -> 3, of which waited for: 2 -> 2; matrix products, arithmetic and copies ran while one was open for 0% -> 0% of each run, Pallas kernels for 13% -> 12%
where the time goes in v7:
time: 83.7 us; the launch traced here: 83.5 us
  blocking collectives  34.9 us (42%)
  waiting for transfers between devices  26.6 us (32%)
  Pallas kernels  12.6 us (15%)
  starting transfers between devices  7.08 us (8%)
  local copies, waits for them, and re-layouts  1.69 us (2%)
    ppermute x1, waiting for transfers between devices, shards(): got = lax.ppermute(outgoing, 'dp', SWAP)  21.9 us
    all_to_all x1, blocking collectives, shards(): parts = lax.all_to_all(sent, ('dp', 'row', 'col'), 0, 0)  20.4 us
    all_to_all x1, blocking collectives, shards(): col_parts = lax.all_to_all(sent, 'row', 0, 0)  14.5 us
    pallas_call x8, Pallas kernels, call(): pl.pallas_call(kernel, in_specs=[pl.BlockSpec(memory_space=space) for spa...  12.6 us
    ppermute x1, waiting for transfers between devices, shards(): late = [lax.ppermute(out, 'dp', SWAP)]  4.63 us
    ppermute x1, starting transfers between devices, shards(): got = lax.ppermute(outgoing, 'dp', SWAP)  3.82 us
    ppermute x1, starting transfers between devices, shards(): late = [lax.ppermute(out, 'dp', SWAP)]  2.67 us
    unnamed x10, local copies, waits for them, and re-layouts  1.69 us
  transfers between devices with their start and end apart: 3, of which 2 were waited for; matrix products, arithmetic and copies ran while one was open for 0% of the time, Pallas kernels for 12%

profile of v7, /device:TPU:1, one launch (start us, length us, event | category | flops | bytes accessed | tf_op | source)
XLA Modules:
  0.0 83.5 jit_solution(1065755389259299429)
XLA Ops:
  0.6 0.0 copy-start
  0.6 1.4 %shard_map.99._ = bf16[128,4608]{1,0:T(8,128)(2,1)S(1)} custom-call(bf16[1,128,9216]{2,1,0:T(8,128)(2,1)} %grad_ref.5), custom_call_target="tpu_custom_call" | custom-call | flops 2359296 | bytes 2359296 | tf_op jit(solution)/shard_map/pallas_call | solution.py:269
  2.1 3.8 %collective-permute-start = (bf16[128,4608]{1,0:T(8,128)(2,1)S(1)}, bf16[128,4608]{1,0:T(8,128)(2,1)S(1)}, u32[]{:S(2)}, u32[]{:S(2)}) collective-permute-start(bf16[128,4608]{1,0:T(8,128)(2,1)S(1)} %shard_map.99._), channel_id=1, source_target_pairs={{0,64},{64,0},{1,65},{65,1},{2,66},{66,2},{3,67},{67,3},{4,68},{68... | collective-permute-start | bytes 3538952 | tf_op jit(solution)/shard_map/ppermute | solution.py:292
  5.9 0.0 copy-done
  5.9 0.0 copy-start.1
  5.9 1.7 %copy-done.1 = f32[128,4608]{1,0:T(8,128)S(1)} copy-done((f32[128,4608]{1,0:T(8,128)S(1)}, f32[128,4608]{1,0:T(8,128)}, u32[]{:S(2)}) %copy-start.1) | copy-done | bytes 2359320
  7.6 0.0 copy-start.4
  7.6 1.2 %shard_map.100 = (bf16[128,5632]{1,0:T(8,128)(2,1)S(1)}, f32[1,1]{1,0:T(1,128)}) custom-call(bf16[1,128,9216]{2,1,0:T(8,128)(2,1)S(1)} %copy-done, f32[128,4608]{1,0:T(8,128)S(1)} %copy-done.1, bf16[128,4608]{1,0:T(8,128)(2,1)S(1)} %shard_map.99._), custom_call_target="tpu_custom_call" | custom-call | flops 3801088 | bytes 3801088 | tf_op jit(solution)/shard_map/pallas_call | solution.py:269
  8.8 0.0 copy-start.3
  8.8 0.6 collective-permute-start.2
  9.4 21.9 %collective-permute-done.got = bf16[128,4608]{1,0:T(8,128)(2,1)S(1)} collective-permute-done((bf16[128,4608]{1,0:T(8,128)(2,1)S(1)}, bf16[128,4608]{1,0:T(8,128)(2,1)S(1)}, u32[]{:S(2)}, u32[]{:S(2)}) %collective-permute-start) | collective-permute-done | bytes 1179680 | tf_op jit(solution)/shard_map/ppermute | solution.py:292
  31.3 0.0 copy-done.4
  31.3 1.5 %shard_map.101 = (f32[128,4608]{1,0:T(8,128)S(1)}, f32[1,128]{1,0:T(1,128)S(1)}, bf16[16,48,128]{2,1,0:T(8,128)(2,1)S(1)}) custom-call(bf16[1,128,9216]{2,1,0:T(8,128)(2,1)S(1)} %copy-done, bf16[128,4608]{1,0:T(8,128)(2,1)S(1)} %collective-permute-done.got, f32[1,128]{1,0:T(1,128)S(1)} %bitcast.7, f32[1,1]{1,0:T(1,128)} %get-tuple-element.27.weight_ref), custom_call_target="tpu_custom_call" | custom-call | flops 4718592 | bytes 4718592 | tf_op jit(solution)/shard_map/pallas_call | solution.py:269
  32.8 0.0 copy-start.2
  32.8 14.5 %all_to_all.10.got_ref = bf16[16,48,128]{2,1,0:T(8,128)(2,1)S(1)} all-to-all(bf16[16,48,128]{2,1,0:T(8,128)(2,1)S(1)} %get-tuple-element.29), channel_id=1, replica_groups=mesh['dp'=2,'row'=16,'col'=4] {'row'}, dimensions={0} | all-to-all | bytes 393216 | tf_op jit(solution)/shard_map/all_to_all | solution.py:308
  47.3 0.0 copy-done.3
  47.3 0.9 %shard_map.102 = (f32[36,128]{1,0:T(8,128)}, f32[36,128]{1,0:T(8,128)S(1)}, f32[16,128]{1,0:T(8,128)S(1)}, bf16[128,4,128]{2,1,0:T(4,128)(2,1)S(1)}) custom-call(f32[128,4608]{1,0:T(8,128)S(1)} %get-tuple-element.28.grad, bf16[16,48,128]{2,1,0:T(8,128)(2,1)S(1)} %all_to_all.10.got_ref, f32[1,128]{1,0:T(1,128)S(1)} %get-tuple-element.30.row_ref, ...), custom_call_target="tpu_custom_call" | custom-call | flops 2359296 | bytes 2359296 | tf_op jit(solution)/shard_map/pallas_call | solution.py:269
  48.1 20.4 %all_to_all.11.got_ref = bf16[128,4,128]{2,1,0:T(4,128)(2,1)S(1)} all-to-all(bf16[128,4,128]{2,1,0:T(4,128)(2,1)S(1)} %get-tuple-element.31), channel_id=1, replica_groups=mesh['dp'=2,'row'=16,'col'=4] {'dp','row','col'}, dimensions={0} | all-to-all | bytes 262144 | tf_op jit(solution)/shard_map/all_to_all | solution.py:316
  68.6 0.0 copy-done.2
  68.6 0.9 %shard_map.103 = (bf16[128,1792]{1,0:T(8,128)(2,1)S(1)}, f32[1,128]{1,0:T(1,128)}, f32[1,1]{1,0:T(1,128)}, f32[1,1]{1,0:T(1,128)}, f32[1,1]{1,0:T(1,128)}, /*ind...) custom-call(bf16[128,4,128]{2,1,0:T(4,128)(2,1)S(1)} %all_to_all.11.got_ref, ...), custom_call_target="tpu_custom_call" | custom-call | flops 1835008 | bytes 1835008 | tf_op jit(solution)/shard_map/pallas_call | solution.py:269
  69.4 2.7 %collective-permute-start.1 = (bf16[128,1792]{1,0:T(8,128)(2,1)S(1)}, bf16[128,1792]{1,0:T(8,128)(2,1)S(1)}, u32[]{:S(2)}, u32[]{:S(2)}) collective-permute-start(bf16[128,1792]{1,0:T(8,128)(2,1)S(1)} %get-tuple-element.38), channel_id=1, source_target_pairs={{0,64},{64,0},{1,65},{65,1},{2,66},{66,2},{3,67},{67,3},{4,68},{68... | collective-permute-start | bytes 1376264 | tf_op jit(solution)/shard_map/ppermute | solution.py:327
  72.1 3.7 %shard_map.104 = (f32[128,4608]{1,0:T(8,128)}, f32[128,4608]{1,0:T(8,128)}, bf16[128,9216]{1,0:T(8,128)(2,1)}) custom-call(f32[128,4608]{1,0:T(8,128)S(1)} %get-tuple-element.28.grad, f32[128,4608]{1,0:T(8,128)S(1)} %copy-done.2, f32[128,128]{1,0:T(8,128)S(1)} %get-tuple-element.34.row_scale, f32[36,128]{1,0:T(8,128)S(1)} %get-tuple-element.35.col_scale, ...), custom_call_target="tpu_custom_call" | custom-call | flops 10616832 | bytes 10616832 | tf_op jit(solution)/shard_map/pallas_call | solution.py:269
  75.8 0.0 collective-permute-done.2.ahead_ref
  75.8 2.3 %shard_map.105._ = bf16[128,9216]{1,0:T(8,128)(2,1)} custom-call(bf16[1,128,9216]{2,1,0:T(8,128)(2,1)S(1)} %copy-done, bf16[128,5632]{1,0:T(8,128)(2,1)S(1)} %collective-permute-done.2.ahead_ref, f32[128,128]{1,0:T(8,128)S(1)} %get-tuple-element.34.row_scale, f32[32,128]{1,0:T(8,128)S(1)} %get-tuple-element.40.scale, ...), custom_call_target="tpu_custom_call", output_to_operand_aliasing={{}: (5, {})} | custom-call | flops 2883584 | bytes 2883584 | tf_op jit(solution)/shard_map/pallas_call | solution.py:269
  78.1 4.6 %collective-permute-done.1.got = bf16[128,1792]{1,0:T(8,128)(2,1)S(1)} collective-permute-done((bf16[128,1792]{1,0:T(8,128)(2,1)S(1)}, bf16[128,1792]{1,0:T(8,128)(2,1)S(1)}, u32[]{:S(2)}, u32[]{:S(2)}) %collective-permute-start.1) | collective-permute-done | bytes 458784 | tf_op jit(solution)/shard_map/ppermute | solution.py:327
  82.7 0.8 shard_map.106
Async XLA Ops:
  0.6 5.3 %copy-start = (bf16[1,128,9216]{2,1,0:T(8,128)(2,1)S(1)}, bf16[1,128,9216]{2,1,0:T(8,128)(2,1)}, u32[]{:S(2)}) copy-start(bf16[1,128,9216]{2,1,0:T(8,128)(2,1)} %grad_ref.5) | copy-start | bytes 7077892
  2.1 29.2 %collective-permute-start = (bf16[128,4608]{1,0:T(8,128)(2,1)S(1)}, bf16[128,4608]{1,0:T(8,128)(2,1)S(1)}, u32[]{:S(2)}, u32[]{:S(2)}) collective-permute-start(bf16[128,4608]{1,0:T(8,128)(2,1)S(1)} %shard_map.99._), channel_id=1, source_target_pairs={{0,64},{64,0},{1,65},{65,1},{2,66},{66,2},{3,67},{67,3},{4,68},{68... | collective-permute-start | bytes 3538952 | tf_op jit(solution)/shard_map/ppermute | solution.py:292
  5.9 1.7 %copy-start.1 = (f32[128,4608]{1,0:T(8,128)S(1)}, f32[128,4608]{1,0:T(8,128)}, u32[]{:S(2)}) copy-start(f32[128,4608]{1,0:T(8,128)} %params_ref.5) | copy-start | bytes 7077892
  7.6 23.7 %copy-start.4 = (f32[128]{0:T(128)S(1)}, f32[128]{0:T(128)}, u32[]{:S(2)}) copy-start(f32[128]{0:T(128)} %param.6) | copy-start | bytes 1540
  8.8 38.5 %copy-start.3 = (f32[9216]{0:T(1024)S(1)}, f32[9216]{0:T(1024)}, u32[]{:S(2)}) copy-start(f32[9216]{0:T(1024)} %param.7) | copy-start | bytes 110596
  8.8 67.0 %collective-permute-start.2 = (bf16[128,5632]{1,0:T(8,128)(2,1)S(1)}, bf16[128,5632]{1,0:T(8,128)(2,1)S(1)}, u32[]{:S(2)}, u32[]{:S(2)}) collective-permute-start(bf16[128,5632]{1,0:T(8,128)(2,1)S(1)} %get-tuple-element.39), channel_id=1, source_target_pairs={{0,64},{64,0},{1,65},{65,1},{2,66},{66,2},{3,67},{67,3},{4,68},{68... | collective-permute-start | bytes 4325384 | tf_op jit(solution)/shard_map/ppermute | solution.py:299
  32.8 35.8 %copy-start.2 = (f32[128,4608]{1,0:T(8,128)S(1)}, f32[128,4608]{1,0:T(8,128)}, u32[]{:S(2)}) copy-start(f32[128,4608]{1,0:T(8,128)} %params_ref.5) | copy-start | bytes 7077892
  69.4 13.3 %collective-permute-start.1 = (bf16[128,1792]{1,0:T(8,128)(2,1)S(1)}, bf16[128,1792]{1,0:T(8,128)(2,1)S(1)}, u32[]{:S(2)}, u32[]{:S(2)}) collective-permute-start(bf16[128,1792]{1,0:T(8,128)(2,1)S(1)} %get-tuple-element.38), channel_id=1, source_target_pairs={{0,64},{64,0},{1,65},{65,1},{2,66},{66,2},{3,67},{67,3},{4,68},{68... | collective-permute-start | bytes 1376264 | tf_op jit(solution)/shard_map/ppermute | solution.py:327

commit v8 on v7

--- a/solution.py
+++ b/solution.py
@@ -17,7 +17,7 @@
 BLOCK = 256
 WIDE = 1536
 EARLY = 11
-LATE = (7,)
+LATE = (5, 2)
 VMEM_LIMIT = 24 << 20
 f32, bf16 = jnp.float32, jnp.bfloat16
 shape = jax.ShapeDtypeStruct

time: 83.7 us -> 83.6 us (level)
  waiting for transfers between devices: 26.6 us -> 24.6 us
  Pallas kernels: 12.6 us -> 14 us
    ppermute x1, waiting for transfers between devices: 4.63 us -> 0.58 us  [shards(): late = [lax.ppermute(out, 'dp', SWAP)]]
    ppermute x0 -> x1, waiting for transfers between devices: none -> 2.07 us  [shards(): late.append(lax.ppermute(out, 'dp', SWAP))]
    pallas_call x8 -> x10, Pallas kernels: 12.6 us -> 14 us  [call(): pl.pallas_call(kernel, in_specs=[pl.BlockSpec(memory_space=space) for spa...]
    unnamed x10 -> x8, local copies, waits for them, and re-layouts: 1.69 us -> 1.68 us
  transfers between devices with their start and end apart: 3 -> 4, of which waited for: 2 -> 3; matrix products, arithmetic and copies ran while one was open for 0% -> 0% of each run, Pallas kernels for 12% -> 14%
where the time goes in v8:
time: 83.6 us; the launch traced here: 83.4 us
  blocking collectives  34.9 us (42%)
  waiting for transfers between devices  24.6 us (29%)
  Pallas kernels  14 us (17%)
  starting transfers between devices  7.53 us (9%)
  local copies, waits for them, and re-layouts  1.68 us (2%)
    ppermute x1, waiting for transfers between devices, shards(): got = lax.ppermute(outgoing, 'dp', SWAP)  21.9 us
    all_to_all x1, blocking collectives, shards(): parts = lax.all_to_all(sent, ('dp', 'row', 'col'), 0, 0)  20.5 us
    all_to_all x1, blocking collectives, shards(): col_parts = lax.all_to_all(sent, 'row', 0, 0)  14.3 us
    pallas_call x10, Pallas kernels, call(): pl.pallas_call(kernel, in_specs=[pl.BlockSpec(memory_space=space) for spa...  14 us
    ppermute x1, starting transfers between devices, shards(): got = lax.ppermute(outgoing, 'dp', SWAP)  3.82 us
    ppermute x1, starting transfers between devices, shards(): late = [lax.ppermute(out, 'dp', SWAP)]  2.67 us
    ppermute x1, waiting for transfers between devices, shards(): late.append(lax.ppermute(out, 'dp', SWAP))  2.07 us
    unnamed x8, local copies, waits for them, and re-layouts  1.68 us
  transfers between devices with their start and end apart: 4, of which 3 were waited for; matrix products, arithmetic and copies ran while one was open for 0% of the time, Pallas kernels for 14%

profile of v8, /device:TPU:1, one launch (start us, length us, event | category | flops | bytes accessed | tf_op | source)
XLA Modules:
  0.0 83.4 jit_solution(6065315308091859379)
XLA Ops:
  0.6 0.0 copy-start
  0.6 1.4 %shard_map.99._ = bf16[128,4608]{1,0:T(8,128)(2,1)S(1)} custom-call(bf16[1,128,9216]{2,1,0:T(8,128)(2,1)} %grad_ref.5), custom_call_target="tpu_custom_call" | custom-call | flops 2359296 | bytes 2359296 | tf_op jit(solution)/shard_map/pallas_call | solution.py:269
  2.1 3.8 %collective-permute-start = (bf16[128,4608]{1,0:T(8,128)(2,1)S(1)}, bf16[128,4608]{1,0:T(8,128)(2,1)S(1)}, u32[]{:S(2)}, u32[]{:S(2)}) collective-permute-start(bf16[128,4608]{1,0:T(8,128)(2,1)S(1)} %shard_map.99._), channel_id=1, source_target_pairs={{0,64},{64,0},{1,65},{65,1},{2,66},{66,2},{3,67},{67,3},{4,68},{68... | collective-permute-start | bytes 3538952 | tf_op jit(solution)/shard_map/ppermute | solution.py:292
  5.9 0.0 copy-done
  5.9 0.0 copy-start.1
  5.9 1.7 %copy-done.1 = bf16[1,128,9216]{2,1,0:T(8,128)(2,1)S(1)} copy-done((bf16[1,128,9216]{2,1,0:T(8,128)(2,1)S(1)}, bf16[1,128,9216]{2,1,0:T(8,128)(2,1)}, u32[]{:S(2)}) %copy-start.1) | copy-done | bytes 2359320
  7.6 0.0 copy-start.3
  7.6 1.2 %shard_map.100 = (bf16[128,5632]{1,0:T(8,128)(2,1)S(1)}, f32[1,1]{1,0:T(1,128)}) custom-call(bf16[1,128,9216]{2,1,0:T(8,128)(2,1)S(1)} %copy-done.1, f32[128,4608]{1,0:T(8,128)S(1)} %copy-done, bf16[128,4608]{1,0:T(8,128)(2,1)S(1)} %shard_map.99._), custom_call_target="tpu_custom_call" | custom-call | flops 3801088 | bytes 3801088 | tf_op jit(solution)/shard_map/pallas_call | solution.py:269
  8.8 0.0 copy-start.2
  8.8 0.6 collective-permute-start.3
  9.4 21.9 %collective-permute-done.got = bf16[128,4608]{1,0:T(8,128)(2,1)S(1)} collective-permute-done((bf16[128,4608]{1,0:T(8,128)(2,1)S(1)}, bf16[128,4608]{1,0:T(8,128)(2,1)S(1)}, u32[]{:S(2)}, u32[]{:S(2)}) %collective-permute-start) | collective-permute-done | bytes 1179680 | tf_op jit(solution)/shard_map/ppermute | solution.py:292
  31.3 0.0 copy-done.3
  31.3 1.5 %shard_map.101 = (f32[128,4608]{1,0:T(8,128)S(1)}, f32[1,128]{1,0:T(1,128)S(1)}, bf16[16,48,128]{2,1,0:T(8,128)(2,1)S(1)}) custom-call(bf16[1,128,9216]{2,1,0:T(8,128)(2,1)S(1)} %copy-done.1, bf16[128,4608]{1,0:T(8,128)(2,1)S(1)} %collective-permute-done.got, f32[1,128]{1,0:T(1,128)S(1)} %bitcast.7, f32[1,1]{1,0:T(1,128)} %get-tuple-element.27.weight_ref), custom_call_target="tpu_custom_call" | custom-call | flops 4718592 | bytes 4718592 | tf_op jit(solution)/shard_map/pallas_call | solution.py:269
  32.8 14.3 %all_to_all.10.got_ref = bf16[16,48,128]{2,1,0:T(8,128)(2,1)S(1)} all-to-all(bf16[16,48,128]{2,1,0:T(8,128)(2,1)S(1)} %get-tuple-element.29), channel_id=1, replica_groups=mesh['dp'=2,'row'=16,'col'=4] {'row'}, dimensions={0} | all-to-all | bytes 393216 | tf_op jit(solution)/shard_map/all_to_all | solution.py:308
  47.1 0.0 copy-done.2
  47.1 0.9 %shard_map.102 = (f32[36,128]{1,0:T(8,128)}, f32[36,128]{1,0:T(8,128)S(1)}, f32[16,128]{1,0:T(8,128)S(1)}, bf16[128,4,128]{2,1,0:T(4,128)(2,1)S(1)}) custom-call(f32[128,4608]{1,0:T(8,128)S(1)} %get-tuple-element.28.grad, bf16[16,48,128]{2,1,0:T(8,128)(2,1)S(1)} %all_to_all.10.got_ref, f32[1,128]{1,0:T(1,128)S(1)} %get-tuple-element.30.row_ref, ...), custom_call_target="tpu_custom_call" | custom-call | flops 2359296 | bytes 2359296 | tf_op jit(solution)/shard_map/pallas_call | solution.py:269
  48.0 20.5 %all_to_all.11.got_ref = bf16[128,4,128]{2,1,0:T(4,128)(2,1)S(1)} all-to-all(bf16[128,4,128]{2,1,0:T(4,128)(2,1)S(1)} %get-tuple-element.31), channel_id=1, replica_groups=mesh['dp'=2,'row'=16,'col'=4] {'dp','row','col'}, dimensions={0} | all-to-all | bytes 262144 | tf_op jit(solution)/shard_map/all_to_all | solution.py:316
  68.6 0.9 %shard_map.103 = (bf16[128,1280]{1,0:T(8,128)(2,1)S(1)}, f32[1,128]{1,0:T(1,128)}, f32[1,1]{1,0:T(1,128)}, f32[1,1]{1,0:T(1,128)}, f32[1,1]{1,0:T(1,128)}, /*ind...) custom-call(bf16[128,4,128]{2,1,0:T(4,128)(2,1)S(1)} %all_to_all.11.got_ref, ...), custom_call_target="tpu_custom_call" | custom-call | flops 1310720 | bytes 1310720 | tf_op jit(solution)/shard_map/pallas_call | solution.py:269
  69.4 2.7 %collective-permute-start.2 = (bf16[128,1280]{1,0:T(8,128)(2,1)S(1)}, bf16[128,1280]{1,0:T(8,128)(2,1)S(1)}, u32[]{:S(2)}, u32[]{:S(2)}) collective-permute-start(bf16[128,1280]{1,0:T(8,128)(2,1)S(1)} %get-tuple-element.38), channel_id=1, source_target_pairs={{0,64},{64,0},{1,65},{65,1},{2,66},{66,2},{3,67},{67,3},{4,68},{68... | collective-permute-start | bytes 983048 | tf_op jit(solution)/shard_map/ppermute | solution.py:327
  72.1 0.8 shard_map.105
  72.9 0.5 collective-permute-start.1
  73.3 3.7 %shard_map.104 = (f32[128,4608]{1,0:T(8,128)}, f32[128,4608]{1,0:T(8,128)}, bf16[128,9216]{1,0:T(8,128)(2,1)}) custom-call(f32[128,4608]{1,0:T(8,128)S(1)} %get-tuple-element.28.grad, f32[128,4608]{1,0:T(8,128)S(1)} %copy-done, f32[128,128]{1,0:T(8,128)S(1)} %get-tuple-element.34.row_scale, f32[36,128]{1,0:T(8,128)S(1)} %get-tuple-element.35.col_scale, ...), custom_call_target="tpu_custom_call" | custom-call | flops 10616832 | bytes 10616832 | tf_op jit(solution)/shard_map/pallas_call | solution.py:269
  77.0 0.0 collective-permute-done.3.ahead_ref
  77.0 2.3 %shard_map.106._ = bf16[128,9216]{1,0:T(8,128)(2,1)} custom-call(bf16[1,128,9216]{2,1,0:T(8,128)(2,1)S(1)} %copy-done.1, bf16[128,5632]{1,0:T(8,128)(2,1)S(1)} %collective-permute-done.3.ahead_ref, f32[128,128]{1,0:T(8,128)S(1)} %get-tuple-element.34.row_scale, f32[32,128]{1,0:T(8,128)S(1)} %get-tuple-element.40.scale, ...), custom_call_target="tpu_custom_call", output_to_operand_aliasing={{}: (5, {})} | custom-call | flops 2883584 | bytes 2883584 | tf_op jit(solution)/shard_map/pallas_call | solution.py:269
  79.3 0.6 collective-permute-done.2.got
  79.9 0.7 shard_map.107._
  80.6 2.1 %collective-permute-done.1.got = bf16[128,512]{1,0:T(8,128)(2,1)S(1)} collective-permute-done((bf16[128,512]{1,0:T(8,128)(2,1)S(1)}, bf16[128,512]{1,0:T(8,128)(2,1)S(1)}, u32[]{:S(2)}, u32[]{:S(2)}) %collective-permute-start.1) | collective-permute-done | bytes 131104 | tf_op jit(solution)/shard_map/ppermute | solution.py:336
  82.7 0.7 shard_map.108
Async XLA Ops:
  0.6 5.3 %copy-start = (f32[128,4608]{1,0:T(8,128)S(1)}, f32[128,4608]{1,0:T(8,128)}, u32[]{:S(2)}) copy-start(f32[128,4608]{1,0:T(8,128)} %params_ref.7) | copy-start | bytes 7077892
  2.1 29.2 %collective-permute-start = (bf16[128,4608]{1,0:T(8,128)(2,1)S(1)}, bf16[128,4608]{1,0:T(8,128)(2,1)S(1)}, u32[]{:S(2)}, u32[]{:S(2)}) collective-permute-start(bf16[128,4608]{1,0:T(8,128)(2,1)S(1)} %shard_map.99._), channel_id=1, source_target_pairs={{0,64},{64,0},{1,65},{65,1},{2,66},{66,2},{3,67},{67,3},{4,68},{68... | collective-permute-start | bytes 3538952 | tf_op jit(solution)/shard_map/ppermute | solution.py:292
  5.9 1.7 %copy-start.1 = (bf16[1,128,9216]{2,1,0:T(8,128)(2,1)S(1)}, bf16[1,128,9216]{2,1,0:T(8,128)(2,1)}, u32[]{:S(2)}) copy-start(bf16[1,128,9216]{2,1,0:T(8,128)(2,1)} %grad_ref.5) | copy-start | bytes 7077892
  7.6 23.7 %copy-start.3 = (f32[128]{0:T(128)S(1)}, f32[128]{0:T(128)}, u32[]{:S(2)}) copy-start(f32[128]{0:T(128)} %param.6) | copy-start | bytes 1540
  8.8 38.3 %copy-start.2 = (f32[9216]{0:T(1024)S(1)}, f32[9216]{0:T(1024)}, u32[]{:S(2)}) copy-start(f32[9216]{0:T(1024)} %param.7) | copy-start | bytes 110596
  8.8 68.2 %collective-permute-start.3 = (bf16[128,5632]{1,0:T(8,128)(2,1)S(1)}, bf16[128,5632]{1,0:T(8,128)(2,1)S(1)}, u32[]{:S(2)}, u32[]{:S(2)}) collective-permute-start(bf16[128,5632]{1,0:T(8,128)(2,1)S(1)} %get-tuple-element.39), channel_id=1, source_target_pairs={{0,64},{64,0},{1,65},{65,1},{2,66},{66,2},{3,67},{67,3},{4,68},{68... | collective-permute-start | bytes 4325384 | tf_op jit(solution)/shard_map/ppermute | solution.py:299
  69.4 10.5 %collective-permute-start.2 = (bf16[128,1280]{1,0:T(8,128)(2,1)S(1)}, bf16[128,1280]{1,0:T(8,128)(2,1)S(1)}, u32[]{:S(2)}, u32[]{:S(2)}) collective-permute-start(bf16[128,1280]{1,0:T(8,128)(2,1)S(1)} %get-tuple-element.38), channel_id=1, source_target_pairs={{0,64},{64,0},{1,65},{65,1},{2,66},{66,2},{3,67},{67,3},{4,68},{68... | collective-permute-start | bytes 983048 | tf_op jit(solution)/shard_map/ppermute | solution.py:327
  72.9 9.8 %collective-permute-start.1 = (bf16[128,512]{1,0:T(8,128)(2,1)S(1)}, bf16[128,512]{1,0:T(8,128)(2,1)S(1)}, u32[]{:S(2)}, u32[]{:S(2)}) collective-permute-start(bf16[128,512]{1,0:T(8,128)(2,1)S(1)} %shard_map.105), channel_id=1, source_target_pairs={{0,64},{64,0},{1,65},{65,1},{2,66},{66,2},{3,67},{67,3},{4,68},{68... | collective-permute-start | bytes 393224 | tf_op jit(solution)/shard_map/ppermute | solution.py:336

commit v9 on v7

--- a/solution.py
+++ b/solution.py
@@ -285,16 +285,17 @@
     early = EARLY * BLOCK
     count = len(steps(width))
 
+    held = pltpu.with_memory_space_constraint(grad_parts, HBM)
     (outgoing,) = call(
         half_kernel, [HBM], [(VMEM, shape((rows, width), bf16))], [dma((count,))],
-        (pltpu.with_memory_space_constraint(grad_parts, HBM),), 4 * rows * width,
+        (held,), 4 * rows * width,
     )
     got = lax.ppermute(outgoing, "dp", SWAP)
     ahead, weight_part = call(
         prepare_kernel, [HBM, HBM, HBM],
         [(HBM, shape((rows, 2 * early), bf16)), (VMEM, shape((1, 1), f32))],
         [VMEM((rows, width), f32), VMEM((rows, early), bf16), VMEM((rows, early), bf16), dma((count + 1,)), dma((2,))],
-        (grad_parts, params, outgoing), 4 * rows * (width + early),
+        (held, params, outgoing), 4 * rows * (width + early),
     )
     ahead = lax.ppermute(ahead, "dp", SWAP)
 

time: 83.7 us -> 83.8 us (level)
  local copies, waits for them, and re-layouts: 1.69 us -> 0.02 us
  waiting for transfers between devices: 26.6 us -> 27.5 us
    unnamed x10 -> x8, local copies, waits for them, and re-layouts: 1.69 us -> 0.02 us
    ppermute x1, waiting for transfers between devices: 21.9 us -> 22.8 us  [shards(): got = lax.ppermute(outgoing, 'dp', SWAP)]
  transfers between devices with their start and end apart: 3 -> 3, of which waited for: 2 -> 2; matrix products, arithmetic and copies ran while one was open for 0% -> 0% of each run, Pallas kernels for 12% -> 13%
where the time goes in v9:
time: 83.8 us; the launch traced here: 83.6 us
  blocking collectives  34.9 us (42%)
  waiting for transfers between devices  27.5 us (33%)
  Pallas kernels  13.2 us (16%)
  starting transfers between devices  7.2 us (9%)
    ppermute x1, waiting for transfers between devices, shards(): got = lax.ppermute(outgoing, 'dp', SWAP)  22.8 us
    all_to_all x1, blocking collectives, shards(): parts = lax.all_to_all(sent, ('dp', 'row', 'col'), 0, 0)  20.6 us
    all_to_all x1, blocking collectives, shards(): col_parts = lax.all_to_all(sent, 'row', 0, 0)  14.3 us
    pallas_call x8, Pallas kernels, call(): pl.pallas_call(kernel, in_specs=[pl.BlockSpec(memory_space=space) for spa...  13.2 us
    ppermute x1, waiting for transfers between devices, shards(): late = [lax.ppermute(out, 'dp', SWAP)]  4.65 us
    ppermute x1, starting transfers between devices, shards(): got = lax.ppermute(outgoing, 'dp', SWAP)  3.82 us
    ppermute x1, starting transfers between devices, shards(): late = [lax.ppermute(out, 'dp', SWAP)]  2.67 us
  transfers between devices with their start and end apart: 3, of which 2 were waited for; matrix products, arithmetic and copies ran while one was open for 0% of the time, Pallas kernels for 13%

profile of v9, /device:TPU:1, one launch (start us, length us, event | category | flops | bytes accessed | tf_op | source)
XLA Modules:
  0.0 83.6 jit_solution(17939311568683145064)
XLA Ops:
  0.6 0.0 copy-start.1
  0.6 1.4 %shard_map.99._ = bf16[128,4608]{1,0:T(8,128)(2,1)S(1)} custom-call(bf16[1,128,9216]{2,1,0:T(8,128)(2,1)} %grad_ref.5), custom_call_target="tpu_custom_call" | custom-call | flops 2359296 | bytes 2359296 | tf_op jit(solution)/shard_map/pallas_call | solution.py:269
  2.1 0.0 copy-start
  2.1 0.0 copy-start.3
  2.1 3.8 %collective-permute-start = (bf16[128,4608]{1,0:T(8,128)(2,1)S(1)}, bf16[128,4608]{1,0:T(8,128)(2,1)S(1)}, u32[]{:S(2)}, u32[]{:S(2)}) collective-permute-start(bf16[128,4608]{1,0:T(8,128)(2,1)S(1)} %shard_map.99._), channel_id=1, source_target_pairs={{0,64},{64,0},{1,65},{65,1},{2,66},{66,2},{3,67},{67,3},{4,68},{68... | collective-permute-start | bytes 3538952 | tf_op jit(solution)/shard_map/ppermute | solution.py:293
  5.9 0.0 copy-done.1
  5.9 1.9 %shard_map.100 = (bf16[128,5632]{1,0:T(8,128)(2,1)S(1)}, f32[1,1]{1,0:T(1,128)}) custom-call(bf16[1,128,9216]{2,1,0:T(8,128)(2,1)} %grad_ref.5, f32[128,4608]{1,0:T(8,128)S(1)} %copy-done.1, bf16[128,4608]{1,0:T(8,128)(2,1)S(1)} %shard_map.99._), custom_call_target="tpu_custom_call" | custom-call | flops 3801088 | bytes 3801088 | tf_op jit(solution)/shard_map/pallas_call | solution.py:269
  7.8 0.0 copy-start.2
  7.8 0.7 collective-permute-start.2
  8.5 22.8 %collective-permute-done.got = bf16[128,4608]{1,0:T(8,128)(2,1)S(1)} collective-permute-done((bf16[128,4608]{1,0:T(8,128)(2,1)S(1)}, bf16[128,4608]{1,0:T(8,128)(2,1)S(1)}, u32[]{:S(2)}, u32[]{:S(2)}) %collective-permute-start) | collective-permute-done | bytes 1179680 | tf_op jit(solution)/shard_map/ppermute | solution.py:293
  31.3 0.0 copy-done
  31.3 0.0 copy-done.3
  31.3 1.5 %shard_map.101 = (f32[128,4608]{1,0:T(8,128)S(1)}, f32[1,128]{1,0:T(1,128)S(1)}, bf16[16,48,128]{2,1,0:T(8,128)(2,1)S(1)}) custom-call(bf16[1,128,9216]{2,1,0:T(8,128)(2,1)S(1)} %copy-done, bf16[128,4608]{1,0:T(8,128)(2,1)S(1)} %collective-permute-done.got, f32[1,128]{1,0:T(1,128)S(1)} %bitcast.7, f32[1,1]{1,0:T(1,128)} %get-tuple-element.27.weight_ref), custom_call_target="tpu_custom_call" | custom-call | flops 4718592 | bytes 4718592 | tf_op jit(solution)/shard_map/pallas_call | solution.py:269
  32.8 14.3 %all_to_all.10.got_ref = bf16[16,48,128]{2,1,0:T(8,128)(2,1)S(1)} all-to-all(bf16[16,48,128]{2,1,0:T(8,128)(2,1)S(1)} %get-tuple-element.29), channel_id=1, replica_groups=mesh['dp'=2,'row'=16,'col'=4] {'row'}, dimensions={0} | all-to-all | bytes 393216 | tf_op jit(solution)/shard_map/all_to_all | solution.py:309
  47.1 0.0 copy-done.2
  47.1 0.9 %shard_map.102 = (f32[36,128]{1,0:T(8,128)}, f32[36,128]{1,0:T(8,128)S(1)}, f32[16,128]{1,0:T(8,128)S(1)}, bf16[128,4,128]{2,1,0:T(4,128)(2,1)S(1)}) custom-call(f32[128,4608]{1,0:T(8,128)S(1)} %get-tuple-element.28.grad, bf16[16,48,128]{2,1,0:T(8,128)(2,1)S(1)} %all_to_all.10.got_ref, f32[1,128]{1,0:T(1,128)S(1)} %get-tuple-element.30.row_ref, ...), custom_call_target="tpu_custom_call" | custom-call | flops 2359296 | bytes 2359296 | tf_op jit(solution)/shard_map/pallas_call | solution.py:269
  48.0 20.6 %all_to_all.11.got_ref = bf16[128,4,128]{2,1,0:T(4,128)(2,1)S(1)} all-to-all(bf16[128,4,128]{2,1,0:T(4,128)(2,1)S(1)} %get-tuple-element.31), channel_id=1, replica_groups=mesh['dp'=2,'row'=16,'col'=4] {'dp','row','col'}, dimensions={0} | all-to-all | bytes 262144 | tf_op jit(solution)/shard_map/all_to_all | solution.py:317
  68.6 0.9 %shard_map.103 = (bf16[128,1792]{1,0:T(8,128)(2,1)S(1)}, f32[1,128]{1,0:T(1,128)}, f32[1,1]{1,0:T(1,128)}, f32[1,1]{1,0:T(1,128)}, f32[1,1]{1,0:T(1,128)}, /*ind...) custom-call(bf16[128,4,128]{2,1,0:T(4,128)(2,1)S(1)} %all_to_all.11.got_ref, ...), custom_call_target="tpu_custom_call" | custom-call | flops 1835008 | bytes 1835008 | tf_op jit(solution)/shard_map/pallas_call | solution.py:269
  69.5 2.7 %collective-permute-start.1 = (bf16[128,1792]{1,0:T(8,128)(2,1)S(1)}, bf16[128,1792]{1,0:T(8,128)(2,1)S(1)}, u32[]{:S(2)}, u32[]{:S(2)}) collective-permute-start(bf16[128,1792]{1,0:T(8,128)(2,1)S(1)} %get-tuple-element.38), channel_id=1, source_target_pairs={{0,64},{64,0},{1,65},{65,1},{2,66},{66,2},{3,67},{67,3},{4,68},{68... | collective-permute-start | bytes 1376264 | tf_op jit(solution)/shard_map/ppermute | solution.py:328
  72.2 3.7 %shard_map.104 = (f32[128,4608]{1,0:T(8,128)}, f32[128,4608]{1,0:T(8,128)}, bf16[128,9216]{1,0:T(8,128)(2,1)}) custom-call(f32[128,4608]{1,0:T(8,128)S(1)} %get-tuple-element.28.grad, f32[128,4608]{1,0:T(8,128)S(1)} %copy-done.1, f32[128,128]{1,0:T(8,128)S(1)} %get-tuple-element.34.row_scale, f32[36,128]{1,0:T(8,128)S(1)} %get-tuple-element.35.col_scale, ...), custom_call_target="tpu_custom_call" | custom-call | flops 10616832 | bytes 10616832 | tf_op jit(solution)/shard_map/pallas_call | solution.py:269
  75.8 0.0 collective-permute-done.2.ahead_ref
  75.8 2.3 %shard_map.105._ = bf16[128,9216]{1,0:T(8,128)(2,1)} custom-call(bf16[1,128,9216]{2,1,0:T(8,128)(2,1)S(1)} %copy-done, bf16[128,5632]{1,0:T(8,128)(2,1)S(1)} %collective-permute-done.2.ahead_ref, f32[128,128]{1,0:T(8,128)S(1)} %get-tuple-element.34.row_scale, f32[32,128]{1,0:T(8,128)S(1)} %get-tuple-element.40.scale, ...), custom_call_target="tpu_custom_call", output_to_operand_aliasing={{}: (5, {})} | custom-call | flops 2883584 | bytes 2883584 | tf_op jit(solution)/shard_map/pallas_call | solution.py:269
  78.1 4.7 %collective-permute-done.1.got = bf16[128,1792]{1,0:T(8,128)(2,1)S(1)} collective-permute-done((bf16[128,1792]{1,0:T(8,128)(2,1)S(1)}, bf16[128,1792]{1,0:T(8,128)(2,1)S(1)}, u32[]{:S(2)}, u32[]{:S(2)}) %collective-permute-start.1) | collective-permute-done | bytes 458784 | tf_op jit(solution)/shard_map/ppermute | solution.py:328
  82.8 0.8 shard_map.106
Async XLA Ops:
  0.6 5.3 %copy-start.1 = (f32[128,4608]{1,0:T(8,128)S(1)}, f32[128,4608]{1,0:T(8,128)}, u32[]{:S(2)}) copy-start(f32[128,4608]{1,0:T(8,128)} %params_ref.5) | copy-start | bytes 7077892
  2.1 29.3 %copy-start = (bf16[1,128,9216]{2,1,0:T(8,128)(2,1)S(1)}, bf16[1,128,9216]{2,1,0:T(8,128)(2,1)}, u32[]{:S(2)}) copy-start(bf16[1,128,9216]{2,1,0:T(8,128)(2,1)} %grad_ref.5) | copy-start | bytes 7077892
  2.1 29.3 %copy-start.3 = (f32[128]{0:T(128)S(1)}, f32[128]{0:T(128)}, u32[]{:S(2)}) copy-start(f32[128]{0:T(128)} %param.6) | copy-start | bytes 1540
  2.1 29.2 %collective-permute-start = (bf16[128,4608]{1,0:T(8,128)(2,1)S(1)}, bf16[128,4608]{1,0:T(8,128)(2,1)S(1)}, u32[]{:S(2)}, u32[]{:S(2)}) collective-permute-start(bf16[128,4608]{1,0:T(8,128)(2,1)S(1)} %shard_map.99._), channel_id=1, source_target_pairs={{0,64},{64,0},{1,65},{65,1},{2,66},{66,2},{3,67},{67,3},{4,68},{68... | collective-permute-start | bytes 3538952 | tf_op jit(solution)/shard_map/ppermute | solution.py:293
  7.8 39.3 %copy-start.2 = (f32[9216]{0:T(1024)S(1)}, f32[9216]{0:T(1024)}, u32[]{:S(2)}) copy-start(f32[9216]{0:T(1024)} %param.7) | copy-start | bytes 110596
  7.8 68.0 %collective-permute-start.2 = (bf16[128,5632]{1,0:T(8,128)(2,1)S(1)}, bf16[128,5632]{1,0:T(8,128)(2,1)S(1)}, u32[]{:S(2)}, u32[]{:S(2)}) collective-permute-start(bf16[128,5632]{1,0:T(8,128)(2,1)S(1)} %get-tuple-element.39), channel_id=1, source_target_pairs={{0,64},{64,0},{1,65},{65,1},{2,66},{66,2},{3,67},{67,3},{4,68},{68... | collective-permute-start | bytes 4325384 | tf_op jit(solution)/shard_map/ppermute | solution.py:300
  69.5 13.3 %collective-permute-start.1 = (bf16[128,1792]{1,0:T(8,128)(2,1)S(1)}, bf16[128,1792]{1,0:T(8,128)(2,1)S(1)}, u32[]{:S(2)}, u32[]{:S(2)}) collective-permute-start(bf16[128,1792]{1,0:T(8,128)(2,1)S(1)} %get-tuple-element.38), channel_id=1, source_target_pairs={{0,64},{64,0},{1,65},{65,1},{2,66},{66,2},{3,67},{67,3},{4,68},{68... | collective-permute-start | bytes 1376264 | tf_op jit(solution)/shard_map/ppermute | solution.py:328
